TPU v7x, 32 devices: a whole 2x2x4 slice. The times are simulated.
32 devices in a mesh: parts: 2 (over y), seq: 4 (over z), head: 4 (over x, core).
Axes of the slice: x: 2, y: 2, z: 4, core: 2. Of those that a mesh axis runs over, the one named last changes fastest.
Arguments:
- xs: bfloat16 [8192, 5120], P(('parts', 'seq'), 'head'), parts along dimension 0, may hold values from -70 to 70
- gate_in: bfloat16 [8192, 5120], P(('parts', 'seq'), 'head'), parts along dimension 0, may hold values from -6 to 6
- bc_in: bfloat16 [8192, 256], P(('parts', 'seq')), parts along dimension 0, may hold values from -6 to 6
- dt_in: bfloat16 [8192, 64], P(('parts', 'seq'), 'head'), parts along dimension 0, may hold values from -3 to 3
- placement: int32 [8192], P(('parts', 'seq')), parts along dimension 0, may hold values from 0 to 4095, as said below
- lengths: int32 [6], P('parts'), parts along dimension 0, may hold values from 1 to 3072, 4096 in all
- conv_x: float32 [4, 5120], P(None, 'head'), may hold values from -3 to 3
- conv_bc: float32 [4, 256], replicated, may hold values from -3 to 3
- a_log: float32 [64], P('head'), may hold values from -9.5 to -0.5
- dt_bias: float32 [64], P('head'), may hold values from -3 to -1
- d_skip: float32 [64], P('head'), may hold values from 0.3 to 3
- norm_gain: float32 [5120], P('head'), may hold values from 0.1 to 1.9
Outputs:
- mixed: bfloat16 [8192, 5120], P(('parts', 'seq'), 'head'), parts along dimension 0
There are 2 independent parts, one for each index of `parts`. A program takes and returns all parts, laid end to end along the dimension named above; an argument that names none is the same for every part. Nothing has to cross between parts.
Inputs may be any that keep to these rules, and one draw needn't show every extreme that they name: `placement`: A permutation of the packed positions; each ingest device holds exactly 1024 // 4 rows bound for every sequence shard. The lengths sum to 4096; the longest is 3072.
All inputs are finite; a program needn't handle non-finite values.
Results may differ from a plain program's by a relative error of at most 0.0025.
The roundings to bfloat16 on the way count: a program that leaves them out, or rounds other values in their place, can miss the bound.
Values may be sent and summed in bfloat16 or wider, within the bound.
No kernel may reach another device: no remote copies, remote signals or barrier semaphores. Data moves between devices by JAX's collectives and lax.ppermute only.
A program may use at most 128 MiB of HBM per device.

v0:
```python
import jax
import jax.numpy as jnp
from jax import lax
from jax.sharding import PartitionSpec as P

BLOCK = 256
INNER = 5120


highest = lax.Precision.HIGHEST


def passed_along(value, axis, steps):
    count = lax.axis_size(axis)
    first, last = (max(0, -steps), min(count, count - steps))
    return lax.ppermute(value, axis, [(source, source + steps) for source in range(first, last)])


def carried_in(array, axis, combine, identity):
    length, mine = (lax.axis_size(axis), lax.axis_index(axis))
    everything = jax.tree.map(lambda part: lax.all_gather(part, axis), array)
    start = jax.tree.map(
        lambda part, zero: jnp.broadcast_to(jnp.asarray(zero, part.dtype), part.shape),
        array,
        identity,
    )

    def step(k, before):
        reached = k < mine
        new = combine(before, jax.tree.map(lambda part: part[k], everything))
        return jax.tree.map(lambda a, b: jnp.where(reached, a, b), new, before)

    return lax.fori_loop(0, length, step, start)


def convolve(rows, docs_rows, kernel):
    width = kernel.shape[0]
    count = rows.shape[0] - (width - 1)
    total = jnp.zeros((count, rows.shape[1]), jnp.float32)
    for lag in range(width):
        lower = width - 1 - lag
        match = (docs_rows[lower : lower + count] == docs_rows[width - 1 :]).astype(jnp.float32)
        total = (
            total
            + kernel[lag][None, :]
            * rows[lower : lower + count].astype(jnp.float32)
            * match[:, None]
        )
    return jax.nn.silu(total).astype(jnp.bfloat16)


def block_pass(carry_state, pieces):
    conv_rows, key_rows, query_rows, step_sizes, log_decay, begins = pieces
    length = step_sizes.shape[0]
    head_count = step_sizes.shape[1]
    log_sums = jnp.cumsum(log_decay, axis=0)
    resets = jnp.cumsum(begins)
    places = jnp.arange(length)
    linked = (places[:, None] >= places[None, :]) & (resets[:, None] == resets[None, :])
    log_gaps = log_sums[:, None, :] - log_sums[None, :, :]
    weights = jnp.exp(jnp.where(linked[:, :, None], log_gaps, -jnp.inf))
    scores = jnp.dot(query_rows, key_rows.T, preferred_element_type=jnp.float32)
    mixing = scores[:, :, None] * weights * step_sizes[None, :, :]
    inputs = conv_rows.astype(jnp.float32).reshape(length, head_count, -1)
    outputs = jnp.einsum("tsh,shp->thp", mixing, inputs, precision=highest)
    carried = jnp.where((resets == 0)[:, None], jnp.exp(log_sums), 0.0)
    queries = query_rows.astype(jnp.float32)
    outputs = outputs + carried[:, :, None] * jnp.einsum(
        "tn,hpn->thp", queries, carry_state, precision=highest
    )
    closing = (
        jnp.where((resets == resets[-1])[:, None], jnp.exp(log_sums[-1][None, :] - log_sums), 0.0)
        * step_sizes
    )
    key_values = key_rows.astype(jnp.float32)
    carry_state = carried[-1][:, None, None] * carry_state + jnp.einsum(
        "sh,shp,sn->hpn", closing, inputs, key_values, precision=highest
    )
    return (carry_state, outputs.reshape(length, -1))


def link_states(earlier, later):
    early_log, early_reset, early_state = earlier
    late_log, late_reset, late_state = later
    keeping = jnp.where(late_reset > 0, 0.0, jnp.exp(late_log))
    return (
        early_log + late_log,
        jnp.maximum(early_reset, late_reset),
        keeping[:, None, None] * early_state + late_state,
    )


def body(
    xs,
    gate_in,
    bc_in,
    dt_in,
    placement,
    lengths,
    conv_x,
    conv_bc,
    a_log,
    dt_bias,
    d_skip,
    norm_gain,
):
    shards = lax.axis_size("seq")
    rows_dev = xs.shape[0]
    per_dest = rows_dev // shards
    targets = placement // rows_dev
    order = jnp.argsort(targets, stable=True)

    def grouped(array):
        return array[order].reshape((shards, per_dest) + array.shape[1:])

    arrived = (
        lax.all_to_all(grouped(xs), "seq", split_axis=0, concat_axis=0, tiled=True),
        lax.all_to_all(grouped(gate_in), "seq", split_axis=0, concat_axis=0, tiled=True),
        lax.all_to_all(grouped(bc_in), "seq", split_axis=0, concat_axis=0, tiled=True),
        lax.all_to_all(grouped(dt_in), "seq", split_axis=0, concat_axis=0, tiled=True),
    )
    slots = lax.all_to_all(grouped(placement), "seq", split_axis=0, concat_axis=0, tiled=True)
    local_slots = slots.reshape(-1) % rows_dev

    def settle(array):
        flat = array.reshape((rows_dev,) + array.shape[2:])
        return jnp.zeros_like(flat).at[local_slots].set(flat)

    packed_x = settle(arrived[0])
    packed_gate = settle(arrived[1])
    packed_bc = settle(arrived[2])
    packed_dt = settle(arrived[3])
    width = conv_x.shape[0]
    my_shard = lax.axis_index("seq")
    base = my_shard * rows_dev
    starts = jnp.cumsum(lengths) - lengths
    positions = base - (width - 1) + jnp.arange(rows_dev + width - 1, dtype=jnp.int32)
    docs = jnp.sum((starts[None, :] <= positions[:, None]).astype(jnp.int32), axis=1) - 1
    begins = jnp.sum((starts[None, :] == positions[width - 1 :, None]).astype(jnp.int32), axis=1)
    channels = jnp.concatenate([packed_x, packed_bc], 1)
    rim = passed_along(channels[rows_dev - width + 1 :], "seq", 1)
    convolved = convolve(
        jnp.concatenate([rim, channels], 0), docs, jnp.concatenate([conv_x, conv_bc], 1)
    )
    inner_dev = packed_x.shape[1]
    state_size = packed_bc.shape[1] // 2
    conv_rows = convolved[:, :inner_dev]
    key_rows = convolved[:, inner_dev : inner_dev + state_size]
    query_rows = convolved[:, inner_dev + state_size :]
    step_sizes = jax.nn.softplus(packed_dt.astype(jnp.float32) + dt_bias[None, :])
    log_decay = -jnp.exp(a_log)[None, :] * step_sizes
    head_count = step_sizes.shape[1]
    head_dim = inner_dev // head_count
    blocks = rows_dev // BLOCK

    def split(array):
        return array.reshape((blocks, BLOCK) + array.shape[1:])

    empty = jnp.zeros((head_count, head_dim, state_size), jnp.float32)
    local_state, outputs = lax.scan(
        block_pass,
        empty,
        (
            split(conv_rows),
            split(key_rows),
            split(query_rows),
            split(step_sizes),
            split(log_decay),
            split(begins),
        ),
    )
    outputs = outputs.reshape(rows_dev, head_count, head_dim)
    log_total = jnp.sum(log_decay, axis=0)
    reset_flag = jnp.broadcast_to((jnp.sum(begins) > 0).astype(jnp.float32), (head_count,))
    zero_heads = jnp.zeros((head_count,), jnp.float32)
    prefix = carried_in(
        (log_total, reset_flag, local_state), "seq", link_states, (zero_heads, zero_heads, empty)
    )
    incoming = prefix[2]
    shard_sums = jnp.cumsum(log_decay, axis=0)
    shard_resets = jnp.cumsum(begins)
    carried = jnp.where((shard_resets == 0)[:, None], jnp.exp(shard_sums), 0.0)
    queries = query_rows.astype(jnp.float32)
    outputs = outputs + carried[:, :, None] * jnp.einsum(
        "tn,hpn->thp", queries, incoming, precision=highest
    )
    inputs = conv_rows.astype(jnp.float32).reshape(rows_dev, head_count, head_dim)
    outputs = outputs + d_skip[None, :, None] * inputs
    gated = outputs.reshape(rows_dev, inner_dev) * jax.nn.silu(packed_gate.astype(jnp.float32))
    squares = lax.psum(jnp.sum(gated * gated, axis=1), "head")
    result = gated * lax.rsqrt(squares / INNER + 1e-05)[:, None] * norm_gain[None, :]
    return result.astype(jnp.bfloat16)


def solution(mesh):
    in_specs = (
        P(("parts", "seq"), "head"),
        P(("parts", "seq"), "head"),
        P(("parts", "seq"), None),
        P(("parts", "seq"), "head"),
        P(("parts", "seq")),
        P("parts"),
        P(None, "head"),
        P(),
        P("head"),
        P("head"),
        P("head"),
        P("head"),
    )
    out_specs = P(("parts", "seq"), "head")
    return jax.shard_map(body, mesh=mesh, in_specs=in_specs, out_specs=out_specs, check_vma=False)
```

profile of v0, /device:TPU:26, one launch (start us, length us, event | category | flops | bytes accessed | tf_op | source)
XLA Modules:
  0.0 477.9 jit_solution(12829732319555716730)
XLA Ops:
  7.4 4.4 sort.17
  11.8 10.4 %gather_fusion = s32[1024]{0:T(1024)} fusion(s32[1024]{0:T(1024)} %param.20, s32[1024]{0:T(1024)S(1)} %fusion.62), kind=kCustom, calls=%fused_computation | custom fusion | bytes 12288 | tf_op jit(solution)/shard_map/gather | solution.py:114
  22.2 5.1 %all-to-all-start = ((s32[4,1,256]{2,1,0:T(1,128)}), s32[4,1,256]{2,1,0:T(1,128)S(1)}, u32[]{:S(2)}, u32[]{:S(2)}) async-start(s32[4,1,256]{2,1,0:T(1,128)} %bitcast.2), calls=%async_computation | async-start | bytes 8192 | tf_op jit(solution)/shard_map/all_to_all | solution.py:122
  27.4 4.3 gather_fusion.1
  31.7 1.7 copy.103
  33.4 5.1 %all-to-all-start.1 = ((bf16[4,256,16]{1,2,0:T(8,128)(2,1)}), bf16[4,256,16]{1,2,0:T(8,128)(2,1)S(1)}, u32[]{:S(2)}, u32[]{:S(2)}) async-start(bf16[4,256,16]{1,2,0:T(8,128)(2,1)} %copy.103), calls=%async_computation.1 | async-start | bytes 65536 | tf_op jit(solution)/shard_map/all_to_all | solution.py:120
  38.5 4.9 %gather_fusion.3 = bf16[1024,256]{1,0:T(8,128)(2,1)} fusion(bf16[1024,256]{1,0:T(8,128)(2,1)S(1)} %copy-done.4, s32[1024]{0:T(1024)S(1)} %fusion.62), kind=kCustom, calls=%fused_computation.3 | custom fusion | bytes 1052672 | tf_op jit(solution)/shard_map/gather | solution.py:114
  43.4 5.1 %all-to-all-start.3 = ((bf16[4,256,256]{2,1,0:T(8,128)(2,1)}), bf16[4,256,256]{2,1,0:T(8,128)(2,1)S(1)}, u32[]{:S(2)}, u32[]{:S(2)}) async-start(bf16[4,256,256]{2,1,0:T(8,128)(2,1)} %bitcast.157), calls=%async_computation.3 | async-start | bytes 1048576 | tf_op jit(solution)/shard_map/all_to_all | solution.py:119
  48.5 5.5 %gather_fusion.2 = bf16[1024,1280]{1,0:T(8,128)(2,1)} fusion(bf16[1024,1280]{1,0:T(8,128)(2,1)S(1)} %copy-done, s32[1024]{0:T(1024)S(1)} %fusion.62), kind=kCustom, calls=%fused_computation.2 | custom fusion | bytes 5246976 | tf_op jit(solution)/shard_map/gather | solution.py:114
  54.0 5.5 %all-to-all-done.3 = bf16[4,256,256]{2,1,0:T(8,128)(2,1)S(1)} async-done(((bf16[4,256,256]{2,1,0:T(8,128)(2,1)}), bf16[4,256,256]{2,1,0:T(8,128)(2,1)S(1)}, u32[]{:S(2)}, u32[]{:S(2)}) %all-to-all-start.3) | async-done | bytes 524320 | tf_op jit(solution)/shard_map/all_to_all | solution.py:119
  59.5 6.9 %all-to-all-start.2 = ((bf16[4,256,1280]{2,1,0:T(8,128)(2,1)}), bf16[4,256,1280]{2,1,0:T(8,128)(2,1)}, u32[]{:S(2)}, u32[]{:S(2)}) async-start(bf16[4,256,1280]{2,1,0:T(8,128)(2,1)} %bitcast.153), calls=%async_computation.2 | async-start | bytes 5242880 | tf_op jit(solution)/shard_map/all_to_all | solution.py:117
  68.1 5.5 %gather_fusion.4 = bf16[1024,1280]{1,0:T(8,128)(2,1)} fusion(bf16[1024,1280]{1,0:T(8,128)(2,1)S(1)} %copy-done.2, s32[1024]{0:T(1024)S(1)} %fusion.62), kind=kCustom, calls=%fused_computation.4 | custom fusion | bytes 5246976 | tf_op jit(solution)/shard_map/gather | solution.py:114
  74.1 3.2 scatter_custom_fusion
  77.4 6.1 %scatter_custom_fusion.2 = bf16[1024,256]{1,0:T(8,128)(2,1)} fusion(s32[1024]{0:T(1024)S(1)} %bitcast.170, bf16[1024,256]{1,0:T(8,128)(2,1)} %bitcast.160, bf16[]{:T(256)} %constant.117.clone.1), kind=kCustom, calls=%fused_computation.94 | custom fusion | bytes 524800 | tf_op jit(solution)/shard_map/scatter | solution.py:127
  83.5 39.4 %all-to-all-done.2 = bf16[4,256,1280]{2,1,0:T(8,128)(2,1)} async-done(((bf16[4,256,1280]{2,1,0:T(8,128)(2,1)}), bf16[4,256,1280]{2,1,0:T(8,128)(2,1)}, u32[]{:S(2)}, u32[]{:S(2)}) %all-to-all-start.2) | async-done | bytes 2621472 | tf_op jit(solution)/shard_map/all_to_all | solution.py:117
  122.9 6.9 %all-to-all-start.4 = ((bf16[4,256,1280]{2,1,0:T(8,128)(2,1)}), bf16[4,256,1280]{2,1,0:T(8,128)(2,1)}, u32[]{:S(2)}, u32[]{:S(2)}) async-start(bf16[4,256,1280]{2,1,0:T(8,128)(2,1)} %bitcast.152), calls=%async_computation.4 | async-start | bytes 5242880 | tf_op jit(solution)/shard_map/all_to_all | solution.py:118
  129.9 6.9 %scatter_custom_fusion.1 = bf16[1024,1280]{1,0:T(8,128)(2,1)S(1)} fusion(s32[1024]{0:T(1024)S(1)} %bitcast.171, bf16[1024,1280]{1,0:T(8,128)(2,1)} %bitcast.8, bf16[]{:T(256)} %constant.117.clone.1), kind=kCustom, calls=%fused_computation.90 | custom fusion | bytes 2621952 | tf_op jit(solution)/shard_map/scatter | solution.py:127
  137.9 1.7 copy-done.8
  139.6 1.5 collective-permute-start
  142.0 17.2 %collective-permute-done = bf16[3,1536]{1,0:T(4,128)(2,1)S(1)} collective-permute-done((bf16[3,1536]{1,0:T(4,128)(2,1)S(1)}, bf16[3,1536]{1,0:T(4,128)(2,1)S(1)}, u32[]{:S(2)}, u32[]{:S(2)}) %collective-permute-start) | collective-permute-done | bytes 9248 | tf_op jit(solution)/shard_map/ppermute | solution.py:16
  159.1 10.6 %multiply_convert_fusion = bf16[1024,1536]{1,0:T(8,128)(2,1)S(1)} fusion(bf16[1024,1536]{1,0:T(8,128)(2,1)} %copy-done.8, bf16[3,1536]{1,0:T(4,128)(2,1)S(1)} %collective-permute-done, f32[1024]{0:T(1024)S(1)} %get-tuple-element.334, f32[1536]{0:T(1024)S(1)} %get-tuple-element.282, f32[1024]{0:T(1024)S(1)} %get-tuple-element.333, ...), kind=kLoop, calls=%fused_computation.75 | loop fusion | flops 44040192 | bytes 6337536 | tf_op jit(solution)/shard_map/convert_element_type | solution.py:49
  169.7 3.9 fusion.72
  173.8 179.0 %while.27 = (s32[]{:T(128)}, f32[16,80,128]{2,1,0:T(8,128)S(1)}, f32[4,256,1280]{1,0,2:T(4,128)}, s32[4,256]{1,0:T(4,128)}, f32[4,256,16]{1,0,2:T(4,128)S(1)}, /...) while((s32[]{:T(128)}, f32[16,80,128]{2,1,0:T(8,128)S(1)}, ...), condition=%wide.region_12.13_spmd.clone, body=%wide.region_7.12_spmd.clone.sunk | while | flops 2036978176 | bytes 17380640 | solution.py:160
  173.8 1.2 constant_dynamic-slice_fusion.9
  177.8 3.2 fusion.101
  183.4 1.0 fusion.98
  184.5 5.4 %copy.156 = f32[1,256,1280]{1,0,2:T(1,128)S(1)} copy(f32[1,256,1280]{1,2,0:T(8,128)S(1)} %bitcast.146) | data formatting | bytes 2621440 | tf_op jit(solution)/shard_map/while/body/jit(dynamic_update_index_in_dim)/dynamic_update_slice | solution.py:160
  189.9 28.6 %dynamic_update_slice.6 = f32[4,256,1280]{1,0,2:T(4,128)} dynamic-update-slice(f32[4,256,1280]{1,0,2:T(4,128)} %get-tuple-element.453, f32[1,256,1280]{1,0,2:T(1,128)S(1)} %copy.156, s32[]{:T(128)S(6)} %copy.163, s32[]{:T(128)} %constant.115.clone.1..sunk, s32[]{:T(128)} %constant.115.clone.1..sunk) | dynamic-update-slice | bytes 2621444 | tf_op jit(solution)/shard_map/while/body/jit(dynamic_update_index_in_dim)/dynamic_update_slice | solution.py:160
  218.6 1.2 constant_dynamic-slice_fusion.9
  222.6 3.2 fusion.101
  228.2 1.0 fusion.98
  229.2 5.4 %copy.156 = f32[1,256,1280]{1,0,2:T(1,128)S(1)} copy(f32[1,256,1280]{1,2,0:T(8,128)S(1)} %bitcast.146) | data formatting | bytes 2621440 | tf_op jit(solution)/shard_map/while/body/jit(dynamic_update_index_in_dim)/dynamic_update_slice | solution.py:160
  234.7 28.6 %dynamic_update_slice.6 = f32[4,256,1280]{1,0,2:T(4,128)} dynamic-update-slice(f32[4,256,1280]{1,0,2:T(4,128)} %get-tuple-element.453, f32[1,256,1280]{1,0,2:T(1,128)S(1)} %copy.156, s32[]{:T(128)S(6)} %copy.163, s32[]{:T(128)} %constant.115.clone.1..sunk, s32[]{:T(128)} %constant.115.clone.1..sunk) | dynamic-update-slice | bytes 2621444 | tf_op jit(solution)/shard_map/while/body/jit(dynamic_update_index_in_dim)/dynamic_update_slice | solution.py:160
  263.3 1.2 constant_dynamic-slice_fusion.9
  267.3 3.2 fusion.101
  272.9 1.0 fusion.98
  274.0 5.4 %copy.156 = f32[1,256,1280]{1,0,2:T(1,128)S(1)} copy(f32[1,256,1280]{1,2,0:T(8,128)S(1)} %bitcast.146) | data formatting | bytes 2621440 | tf_op jit(solution)/shard_map/while/body/jit(dynamic_update_index_in_dim)/dynamic_update_slice | solution.py:160
  279.4 28.6 %dynamic_update_slice.6 = f32[4,256,1280]{1,0,2:T(4,128)} dynamic-update-slice(f32[4,256,1280]{1,0,2:T(4,128)} %get-tuple-element.453, f32[1,256,1280]{1,0,2:T(1,128)S(1)} %copy.156, s32[]{:T(128)S(6)} %copy.163, s32[]{:T(128)} %constant.115.clone.1..sunk, s32[]{:T(128)} %constant.115.clone.1..sunk) | dynamic-update-slice | bytes 2621444 | tf_op jit(solution)/shard_map/while/body/jit(dynamic_update_index_in_dim)/dynamic_update_slice | solution.py:160
  308.1 1.2 constant_dynamic-slice_fusion.9
  312.1 3.2 fusion.101
  317.7 1.0 fusion.98
  318.7 5.4 %copy.156 = f32[1,256,1280]{1,0,2:T(1,128)S(1)} copy(f32[1,256,1280]{1,2,0:T(8,128)S(1)} %bitcast.146) | data formatting | bytes 2621440 | tf_op jit(solution)/shard_map/while/body/jit(dynamic_update_index_in_dim)/dynamic_update_slice | solution.py:160
  324.2 28.6 %dynamic_update_slice.6 = f32[4,256,1280]{1,0,2:T(4,128)} dynamic-update-slice(f32[4,256,1280]{1,0,2:T(4,128)} %get-tuple-element.453, f32[1,256,1280]{1,0,2:T(1,128)S(1)} %copy.156, s32[]{:T(128)S(6)} %copy.163, s32[]{:T(128)} %constant.115.clone.1..sunk, s32[]{:T(128)} %constant.115.clone.1..sunk) | dynamic-update-slice | bytes 2621444 | tf_op jit(solution)/shard_map/while/body/jit(dynamic_update_index_in_dim)/dynamic_update_slice | solution.py:160
  354.3 1.0 reduce-window.45
  355.4 1.3 dynamic-slice
  358.2 0.8 dynamic-update-slice.1
  359.1 35.9 %all-reduce.2 = (f32[4]{0:T(128)S(1)}, f32[64]{0:T(128)S(1)}) all-reduce(f32[4]{0:T(128)S(1)} %dynamic-update-slice, f32[64]{0:T(128)S(1)} %dynamic-update-slice.1), channel_id=2, replica_groups=mesh['parts'=2,'seq'=4,'head'=4] {'seq'}, use_global_device_ids=true, to_apply=%add | all-reduce | flops 68 | bytes 544
  395.1 0.9 copy.128
  395.9 4.5 reduce-window.54
  400.9 7.0 %scatter_custom_fusion.3 = bf16[1024,1280]{1,0:T(8,128)(2,1)S(1)} fusion(s32[1024]{0:T(1024)} %bitcast.172, bf16[1024,1280]{1,0:T(8,128)(2,1)} %bitcast.27, bf16[]{:T(256)} %constant.117.clone.1), kind=kCustom, calls=%fused_computation.88 | custom fusion | bytes 2621952 | tf_op jit(solution)/shard_map/scatter | solution.py:127
  407.9 7.0 %copy.113 = f32[1024,1280]{0,1:T(8,128)} copy(f32[1024,1280]{1,0:T(8,128)} %get-tuple-element.330) | data formatting | bytes 10485760 | tf_op jit(solution)/shard_map/reshape | solution.py:187
  414.9 7.7 %reshape.351 = f32[1024,16,80]{0,2,1:T(8,128)} reshape(f32[4,256,1280]{1,0,2:T(4,128)} %get-tuple-element.164) | data formatting | bytes 10485760 | tf_op jit(solution)/shard_map/reshape | solution.py:172
  422.6 11.4 %all-gather.4.cloned.1.call-done = f32[64,80,128]{2,1,0:T(8,128)} async-done(((f32[16,80,128]{2,1,0:T(8,128)}), f32[64,80,128]{2,1,0:T(8,128)}) %all-gather.4.cloned.1.call-update) | async-done | bytes 2621456 | tf_op jit(solution)/shard_map/all_gather | solution.py:21
  434.1 5.1 %while.28 = (s32[]{:T(128)}, f32[16,80,128]{2,1,0:T(8,128)S(1)}, s32[]{:T(128)}, f32[4,16]{1,0:T(4,128)S(1)}, f32[4,16]{1,0:T(4,128)S(1)}, /*index=5*/f32[4,16,80,128]{3,2,1,0:T(8,128)}, s32[]{:T(128)}, s32[]{:T(128)}) while((s32[]{:T(128)}, f32[16,80,128]{2,1,0:T(8,128)S(1)}, s32[]{:T(128)}, f32[4,16]{1,0:T(4,128)S(1)}, ...), condition=%wide.region_20.21_spmd.clone, body=%wide.region_19.20_spmd.clone.sunk | while | flops 655396 | bytes 1966457 | solution.py:33
  434.1 1.2 fusion.104
  435.4 1.2 fusion.104
  436.7 1.2 fusion.104
  437.9 1.2 fusion.104
  439.2 3.3 fusion.54
  442.5 6.9 %multiply_add_fusion = f32[1024,16,80]{0,2,1:T(8,128)} fusion(f32[1024,16,80]{0,2,1:T(8,128)} %bitcast.149, f32[1024,16,80]{0,2,1:T(8,128)S(1)} %copy-done.6, f32[1024,16,80]{0,2,1:T(8,128)S(1)} %fusion.54, f32[16]{0:T(128)S(1)} %copy-done.25, f32[1024,16]{0,1:T(8,128)S(1)} %fusion.60), kind=kLoop, calls=%fused_computation.82 | loop fusion | flops 5242880 | bytes 21037120 | tf_op jit(solution)/shard_map/add | solution.py:188
  449.4 6.0 %copy.114 = f32[1024,1280]{1,0:T(8,128)} copy(f32[1024,1280]{0,1:T(8,128)} %bitcast.150) | data formatting | bytes 10485760 | tf_op jit(solution)/shard_map/reshape | solution.py:189
  455.4 4.2 multiply_reduce_fusion
  459.6 5.8 %psum.7 = f32[1024]{0:T(1024)S(1)} all-reduce(f32[1024]{0:T(1024)S(1)} %multiply_reduce_fusion), channel_id=1, replica_groups=mesh['parts'=2,'seq'=4,'head'=4] {'head'}, use_global_device_ids=true, to_apply=%region_23.24 | all-reduce | flops 1024 | bytes 8192 | tf_op jit(solution)/shard_map/psum | solution.py:190
  465.4 5.7 %multiply_convert_fusion.1 = bf16[1024,1280]{1,0:T(8,128)(2,1)} fusion(f32[1280]{0:T(1024)S(1)} %copy-done.21, f32[1024]{0:T(1024)S(1)} %add_rsqrt_fusion, f32[1024,1280]{1,0:T(8,128)} %copy.114, bf16[1024,1280]{1,0:T(8,128)(2,1)} %copy-done.5), kind=kLoop, calls=%fused_computation.80 | loop fusion | flops 11796480 | bytes 10494976 | tf_op jit(solution)/shard_map/convert_element_type | solution.py:192
  (239 shorter events, 28.5 us)
Async XLA Ops:
  6.5 42.0 %copy-start = (bf16[1024,1280]{1,0:T(8,128)(2,1)S(1)}, bf16[1024,1280]{1,0:T(8,128)(2,1)}, u32[]{:S(2)}) copy-start(bf16[1024,1280]{1,0:T(8,128)(2,1)} %param.16) | copy-start | bytes 7864324
  6.5 20.7 %copy-start.19 = (bf16[1024,16]{0,1:T(8,128)(2,1)S(1)}, bf16[1024,16]{0,1:T(8,128)(2,1)}, u32[]{:S(2)}) copy-start(bf16[1024,16]{0,1:T(8,128)(2,1)} %param.19) | copy-start | bytes 98308
  6.5 32.0 %copy-start.4 = (bf16[1024,256]{1,0:T(8,128)(2,1)S(1)}, bf16[1024,256]{1,0:T(8,128)(2,1)}, u32[]{:S(2)}) copy-start(bf16[1024,256]{1,0:T(8,128)(2,1)} %param.18) | copy-start | bytes 1572868
  22.2 11.2 %all-to-all-start = ((s32[4,1,256]{2,1,0:T(1,128)}), s32[4,1,256]{2,1,0:T(1,128)S(1)}, u32[]{:S(2)}, u32[]{:S(2)}) async-start(s32[4,1,256]{2,1,0:T(1,128)} %bitcast.2), calls=%async_computation | async-start | bytes 8192 | tf_op jit(solution)/shard_map/all_to_all | solution.py:122
  33.4 10.0 %all-to-all-start.1 = ((bf16[4,256,16]{1,2,0:T(8,128)(2,1)}), bf16[4,256,16]{1,2,0:T(8,128)(2,1)S(1)}, u32[]{:S(2)}, u32[]{:S(2)}) async-start(bf16[4,256,16]{1,2,0:T(8,128)(2,1)} %copy.103), calls=%async_computation.1 | async-start | bytes 65536 | tf_op jit(solution)/shard_map/all_to_all | solution.py:120
  43.4 16.1 %all-to-all-start.3 = ((bf16[4,256,256]{2,1,0:T(8,128)(2,1)}), bf16[4,256,256]{2,1,0:T(8,128)(2,1)S(1)}, u32[]{:S(2)}, u32[]{:S(2)}) async-start(bf16[4,256,256]{2,1,0:T(8,128)(2,1)} %bitcast.157), calls=%async_computation.3 | async-start | bytes 1048576 | tf_op jit(solution)/shard_map/all_to_all | solution.py:119
  54.0 12.4 %copy-start.26 = (s32[3]{0:T(128)S(1)}, s32[3]{0:T(128)}, u32[]{:S(2)}) copy-start(s32[3]{0:T(128)} %param.21) | copy-start | bytes 40
  54.0 14.1 %copy-start.2 = (bf16[1024,1280]{1,0:T(8,128)(2,1)S(1)}, bf16[1024,1280]{1,0:T(8,128)(2,1)}, u32[]{:S(2)}) copy-start(bf16[1024,1280]{1,0:T(8,128)(2,1)} %param.17) | copy-start | bytes 7864324
  59.5 6.9 %copy-start.11 = (bf16[4,256,256]{2,1,0:T(8,128)(2,1)}, bf16[4,256,256]{2,1,0:T(8,128)(2,1)S(1)}, u32[]{:S(2)}) copy-start(bf16[4,256,256]{2,1,0:T(8,128)(2,1)S(1)} %all-to-all-done.3) | copy-start | bytes 1572868
  59.5 63.4 %all-to-all-start.2 = ((bf16[4,256,1280]{2,1,0:T(8,128)(2,1)}), bf16[4,256,1280]{2,1,0:T(8,128)(2,1)}, u32[]{:S(2)}, u32[]{:S(2)}) async-start(bf16[4,256,1280]{2,1,0:T(8,128)(2,1)} %bitcast.153), calls=%async_computation.2 | async-start | bytes 5242880 | tf_op jit(solution)/shard_map/all_to_all | solution.py:117
  67.5 6.1 %copy-start.18 = (s32[1024]{0:T(1024)}, s32[1024]{0:T(1024)S(1)}, u32[]{:S(2)}) copy-start(s32[1024]{0:T(1024)S(1)} %get-tuple-element.286) | copy-start | bytes 12292
  68.1 5.5 %copy-start.20 = (f32[4,1280]{1,0:T(4,128)S(1)}, f32[4,1280]{1,0:T(4,128)}, u32[]{:S(2)}) copy-start(f32[4,1280]{1,0:T(4,128)} %param.22) | copy-start | bytes 61444
  68.1 5.5 %copy-start.22 = (f32[4,256]{1,0:T(4,128)S(1)}, f32[4,256]{1,0:T(4,128)}, u32[]{:S(2)}) copy-start(f32[4,256]{1,0:T(4,128)} %param.23) | copy-start | bytes 12292
  68.1 5.7 %copy-start.27 = (f32[16]{0:T(128)S(1)}, f32[16]{0:T(128)}, u32[]{:S(2)}) copy-start(f32[16]{0:T(128)} %param.24) | copy-start | bytes 196
  73.9 63.0 %copy-start.23 = (s32[1024,1]{0,1:T(1,128)}, s32[1024,1]{0,1:T(1,128)S(1)}, u32[]{:S(2)}) copy-start(s32[1024,1]{0,1:T(1,128)S(1)} %compare_select_fusion.2) | copy-start | bytes 12292
  122.9 278.0 %all-to-all-start.4 = ((bf16[4,256,1280]{2,1,0:T(8,128)(2,1)}), bf16[4,256,1280]{2,1,0:T(8,128)(2,1)}, u32[]{:S(2)}, u32[]{:S(2)}) async-start(bf16[4,256,1280]{2,1,0:T(8,128)(2,1)} %bitcast.152), calls=%async_computation.4 | async-start | bytes 5242880 | tf_op jit(solution)/shard_map/all_to_all | solution.py:118
  129.9 304.2 %all-gather.4.cloned.1.call-start = ((), (), s32[]{:S(2)}) async-start(), calls=%async_computation.5 | async-start | bytes 3276800 | tf_op jit(solution)/shard_map/all_gather | solution.py:21
  129.9 11.2 %copy-start.24 = (f32[16]{0:T(128)S(1)}, f32[16]{0:T(128)}, u32[]{:S(2)}) copy-start(f32[16]{0:T(128)} %param.25) | copy-start | bytes 196
  136.8 1.0 copy-start.9
  137.9 1.7 copy-start.8
  139.6 19.5 %collective-permute-start = (bf16[3,1536]{1,0:T(4,128)(2,1)S(1)}, bf16[3,1536]{1,0:T(4,128)(2,1)S(1)}, u32[]{:S(2)}, u32[]{:S(2)}) collective-permute-start(bf16[3,1536]{1,0:T(4,128)(2,1)S(1)} %slice.130), channel_id=1, source_target_pairs={{0,4},{4,8},{8,12},{1,5},{5,9},{9,13},{2,6},{6,10},{10,14},{3,7},{... | collective-permute-start | bytes 27656 | tf_op jit(solution)/shard_map/ppermute | solution.py:16
  141.9 31.7 %copy-start.10 = (f32[1024,16]{0,1:T(8,128)}, f32[1024,16]{0,1:T(8,128)S(1)}, u32[]{:S(2)}) copy-start(f32[1024,16]{0,1:T(8,128)S(1)} %get-tuple-element.322) | copy-start | bytes 196612
  169.7 4.0 copy-start.7
  173.8 2.3 copy-start.12
  173.8 3.9 copy-start.14
  176.1 1.6 copy-start.16
  177.7 4.7 copy-start.17
  183.2 35.3 %copy-start.13 = (f32[4,256,16]{1,0,2:T(4,128)S(1)}, f32[4,256,16]{1,0,2:T(4,128)}, u32[]{:S(2)}) copy-start(f32[4,256,16]{1,0,2:T(4,128)} %copy-done.12) | copy-start | bytes 196612 | tf_op jit(solution)/shard_map/while
  183.2 35.3 %copy-start.15 = (f32[4,256,16]{1,0,2:T(4,128)S(1)}, f32[4,256,16]{1,0,2:T(4,128)}, u32[]{:S(2)}) copy-start(f32[4,256,16]{1,0,2:T(4,128)} %copy-done.14) | copy-start | bytes 196612 | tf_op jit(solution)/shard_map/while
  218.6 2.3 copy-start.12
  218.6 3.9 copy-start.14
  220.9 1.6 copy-start.16
  222.4 4.7 copy-start.17
  228.0 35.3 %copy-start.13 = (f32[4,256,16]{1,0,2:T(4,128)S(1)}, f32[4,256,16]{1,0,2:T(4,128)}, u32[]{:S(2)}) copy-start(f32[4,256,16]{1,0,2:T(4,128)} %copy-done.12) | copy-start | bytes 196612 | tf_op jit(solution)/shard_map/while
  228.0 35.3 %copy-start.15 = (f32[4,256,16]{1,0,2:T(4,128)S(1)}, f32[4,256,16]{1,0,2:T(4,128)}, u32[]{:S(2)}) copy-start(f32[4,256,16]{1,0,2:T(4,128)} %copy-done.14) | copy-start | bytes 196612 | tf_op jit(solution)/shard_map/while
  263.3 2.3 copy-start.12
  263.3 3.9 copy-start.14
  265.6 1.6 copy-start.16
  267.2 4.7 copy-start.17
  272.7 35.3 %copy-start.13 = (f32[4,256,16]{1,0,2:T(4,128)S(1)}, f32[4,256,16]{1,0,2:T(4,128)}, u32[]{:S(2)}) copy-start(f32[4,256,16]{1,0,2:T(4,128)} %copy-done.12) | copy-start | bytes 196612 | tf_op jit(solution)/shard_map/while
  272.7 35.3 %copy-start.15 = (f32[4,256,16]{1,0,2:T(4,128)S(1)}, f32[4,256,16]{1,0,2:T(4,128)}, u32[]{:S(2)}) copy-start(f32[4,256,16]{1,0,2:T(4,128)} %copy-done.14) | copy-start | bytes 196612 | tf_op jit(solution)/shard_map/while
  308.1 2.3 copy-start.12
  308.1 3.9 copy-start.14
  310.4 1.6 copy-start.16
  311.9 4.7 copy-start.17
  317.5 35.3 %copy-start.13 = (f32[4,256,16]{1,0,2:T(4,128)S(1)}, f32[4,256,16]{1,0,2:T(4,128)}, u32[]{:S(2)}) copy-start(f32[4,256,16]{1,0,2:T(4,128)} %copy-done.12) | copy-start | bytes 196612 | tf_op jit(solution)/shard_map/while
  317.5 35.3 %copy-start.15 = (f32[4,256,16]{1,0,2:T(4,128)S(1)}, f32[4,256,16]{1,0,2:T(4,128)}, u32[]{:S(2)}) copy-start(f32[4,256,16]{1,0,2:T(4,128)} %copy-done.14) | copy-start | bytes 196612 | tf_op jit(solution)/shard_map/while
  352.8 0.8 copy-start.3
  407.9 47.5 %copy-start.5 = (bf16[1024,1280]{1,0:T(8,128)(2,1)}, bf16[1024,1280]{1,0:T(8,128)(2,1)S(1)}, u32[]{:S(2)}) copy-start(bf16[1024,1280]{1,0:T(8,128)(2,1)S(1)} %scatter_custom_fusion.3) | copy-start | bytes 7864324
  439.2 3.3 copy-start.6
  439.2 3.3 copy-start.25
  455.4 10.0 %copy-start.21 = (f32[1280]{0:T(1024)S(1)}, f32[1280]{0:T(1024)}, u32[]{:S(2)}) copy-start(f32[1280]{0:T(1024)} %param.27) | copy-start | bytes 15364
  465.4 5.7 %copy-start.1 = (bf16[1024,1280]{1,0:T(8,128)(2,1)S(1)}, bf16[1024,1280]{1,0:T(8,128)(2,1)}, u32[]{:S(2)}) copy-start(bf16[1024,1280]{1,0:T(8,128)(2,1)} %param.16) | copy-start | bytes 7864324
Sparse Core Ops, SparseCore 0:
  353.8 80.1 all-gather.3
where the time goes:
time: 488 us; the launch traced here: 478 us
  local copies, waits for them, and re-layouts  236 us (48%)
  waiting for transfers between devices  73.6 us (15%)
  other arithmetic  56.9 us (12%)
  blocking collectives  41.7 us (9%)
  starting transfers between devices  30.5 us (6%)
  matrix products  23.7 us (5%)
  between operations  15 us (3%)
    dynamic_update_slice x8, local copies, waits for them, and re-layouts, body(): lax.scan(block_pass, empty, (split(conv_rows), split(key_rows), split(que...  136 us
    all_to_all x1, waiting for transfers between devices, body(): lax.all_to_all(grouped(xs), 'seq', split_axis=0, concat_axis=0, tiled=True)  39.4 us
    unnamed x1, blocking collectives  35.9 us
    gather x5, local copies, waits for them, and re-layouts, grouped(): return array[order].reshape((shards, per_dest) + array.shape[1:])  30.6 us
    scatter x5, local copies, waits for them, and re-layouts, settle(): return jnp.zeros_like(flat).at[local_slots].set(flat)  23.4 us
    ppermute x1, waiting for transfers between devices, passed_along(): lax.ppermute(value, axis, [(source, source + steps) for source in range(f...  17.2 us
    dot_general x4, matrix products, block_pass(): outputs = jnp.einsum('tsh,shp->thp', mixing, inputs, precision=highest)  12.7 us
    all_gather x1, waiting for transfers between devices, carried_in(): everything = jax.tree.map(lambda part: lax.all_gather(part, axis), array)  11.4 us
  transfers between devices with their start and end apart: 7, of which 4 were waited for; matrix products, arithmetic and copies ran while one was open for 56% of the time, Pallas kernels for 0%

commit v1 on v0

v1 whole, which is shorter than its diff:
```python
import functools

import jax
import jax.numpy as jnp
from jax import lax
from jax.experimental import pallas as pl
from jax.experimental.pallas import tpu as pltpu
from jax.sharding import PartitionSpec as P

CHUNK = 64
ROWS = 256
TILE = 256
LANES = 128
RIM = 16
HALO = 8
GROUPS = 3
FAR = 1 << 28
bf16 = jnp.bfloat16
f32 = jnp.float32


def dot(a, b):
    return jnp.dot(a, b, preferred_element_type=f32)


def dot_nt(a, b):
    return lax.dot_general(a, b, (((1,), (1,)), ((), ())), preferred_element_type=f32)


def iota(shape, dim):
    return lax.broadcasted_iota(jnp.int32, shape, dim)


def ones_where(mask):
    return jnp.where(mask, 1.0, 0.0).astype(bf16)


def high_low(value):
    high = value.astype(bf16)
    return high, (value - high.astype(f32)).astype(bf16)


def split_lanes(value, heads):
    lane = iota(value.shape, 1)
    high = value.astype(bf16).astype(f32)
    rest = value - high
    middle = rest.astype(bf16).astype(f32)
    lowest = rest - middle
    pieces = jnp.where(lane < heads, high, jnp.where(lane < 2 * heads, middle, lowest))
    return jnp.where(lane < GROUPS * heads, pieces, 0.0).astype(bf16)


def silu(value):
    return value * jax.nn.sigmoid(value)


def call(kernel, outs, args, in_specs, out_specs, grid=(1,), scratch=(), flops=0, nbytes=0, limit=56):
    return pl.pallas_call(
        kernel,
        grid=grid,
        in_specs=in_specs,
        out_specs=out_specs,
        out_shape=outs,
        scratch_shapes=list(scratch),
        compiler_params=pltpu.CompilerParams(vmem_limit_bytes=limit * 1024 * 1024),
        cost_estimate=pl.CostEstimate(flops=flops, bytes_accessed=nbytes, transcendentals=0),
    )(*args)


def whole(array):
    rank = len(array.shape)
    return pl.BlockSpec(array.shape, lambda *_: (0,) * rank)


def columns(rows, width=TILE):
    return pl.BlockSpec((rows, width), lambda j: (0, j))


def smem():
    return pl.BlockSpec(memory_space=pltpu.SMEM)


def shape(*dims, dtype=bf16):
    return jax.ShapeDtypeStruct(dims, dtype)


def send_order(shards, width, info, place_ref, bc_ref, dt_ref, pick_ref, *small_refs):
    rows = place_ref.shape[1]
    per = rows // shards
    heads = dt_ref.shape[1]
    quarter = bc_ref.shape[1] // info[2]
    me, lane_group = info[0], info[1]
    place = place_ref[...]
    padded = max(8, shards)
    owner = iota((padded, rows), 0)
    first = owner * rows
    mine = (place >= first) & (place < first + rows)
    earlier = ones_where(iota((rows, rows), 0) < iota((rows, rows), 1))
    before = dot(ones_where(mine), earlier)
    relative = jnp.where(owner >= me, owner - me, owner - me + shards)
    target = before + (relative * per).astype(f32)
    target = jnp.sum(jnp.where(mine, target, 0.0), axis=0, keepdims=True).astype(jnp.int32)
    local = jnp.sum(jnp.where(mine, (place - first + 1).astype(f32), 0.0), axis=0, keepdims=True)
    high = jnp.floor(local * (1.0 / 64.0))
    low = local - 64.0 * high
    base_lane = quarter + heads
    line = iota((LANES, rows), 0)
    digits = jnp.where(line == base_lane, high, jnp.where(line == base_lane + 1, low, 0.0)).astype(bf16)
    from_bc = ones_where(
        (iota((bc_ref.shape[1], LANES), 0) == iota((bc_ref.shape[1], LANES), 1) + lane_group * quarter)
        & (iota((bc_ref.shape[1], LANES), 1) < quarter)
    )
    from_dt = ones_where(iota((heads, LANES), 0) + quarter == iota((heads, LANES), 1))
    payload = (dot(bc_ref[...], from_bc) + dot(dt_ref[...], from_dt)).astype(bf16)
    for k in range(shards):
        pick = ones_where(iota((per, rows), 0) + k * per == target)
        pick_ref[k * per : (k + 1) * per] = pick
        dest = jnp.where(me + k >= shards, me + k - shards, me + k)
        row = iota((RIM, rows), 0)
        rim = ones_where((row < width - 1) & (place == row + (dest * rows - (width - 1))))
        pick_ref[rows + k * RIM : rows + (k + 1) * RIM] = rim
        small_refs[k][:per] = (dot(pick, payload) + dot_nt(pick, digits)).astype(bf16)
        small_refs[k][per:] = (dot(rim, payload) + dot_nt(rim, digits)).astype(bf16)


def gather_rows(shards, with_rim, pick_ref, x_ref, *out_refs):
    rows = x_ref.shape[0]
    per = rows // shards
    values = x_ref[...]
    for k in range(shards):
        out_refs[k][:per] = dot(pick_ref[k * per : (k + 1) * per], values).astype(bf16)
    if with_rim:
        rims = dot(pick_ref[rows:], values).astype(bf16)
        for k in range(shards):
            out_refs[k][per:] = rims[k * RIM : (k + 1) * RIM]


def distance(position, info, seqs, limit):
    gap = limit
    for j in range(seqs):
        start = info[4 + j]
        gap = jnp.where(position >= start, jnp.minimum(gap, position - start), gap)
    return gap


def convolve(block_of, taps, gap, width):
    total = taps[0:1] * block_of(0)
    for lag in range(1, width):
        total = total + jnp.where(gap >= lag, taps[lag : lag + 1] * block_of(lag), 0.0)
    return silu(total).astype(bf16)


def prepare(
    shards, width, seqs, heads, head_dim,
    info, own_ref, all_ref, taps_ref, lines_ref,
    pick_ref, rims_ref, gap_ref, score_high_ref, score_low_ref, query_ref, kept_query_ref,
    keys_ref, inside_ref, outside_ref, carried_ref, expand_ref, factor_ref, rest_ref,
    packed, log_sums, steps,
):
    rows = pick_ref.shape[0]
    per = rows // shards
    group = per + RIM
    state = query_ref.shape[1]
    groups = all_ref.shape[0]
    quarter = 2 * state // groups
    base = info[3]
    own_main = jnp.concatenate([own_ref[k * group : k * group + per] for k in range(shards)], 0)
    own_rim = jnp.concatenate([own_ref[k * group + per : (k + 1) * group] for k in range(shards)], 0)
    lane = iota((8, LANES), 1)
    weights = jnp.where(lane == quarter + heads, 64.0, jnp.where(lane == quarter + heads + 1, 1.0, 0.0)).astype(bf16)
    slots = dot_nt(weights, own_main)[0:1].astype(jnp.int32) - 1
    rim_slots = dot_nt(weights, own_rim)[0:1].astype(jnp.int32) - 1 - (rows - (width - 1)) + HALO - (width - 1)
    rim_pick = ones_where(iota((RIM, shards * RIM), 0) == rim_slots)
    rims_ref[...] = rim_pick
    bc_main = jnp.zeros((rows, 2 * state), f32)
    bc_rim = jnp.zeros((shards * RIM, 2 * state), f32)
    for g in range(groups):
        spread = ones_where(
            (iota((LANES, 2 * state), 0) + g * quarter == iota((LANES, 2 * state), 1))
            & (iota((LANES, 2 * state), 0) < quarter)
        )
        for k in range(shards):
            pass
        main = jnp.concatenate([all_ref[g, k * group : k * group + per] for k in range(shards)], 0)
        rim = jnp.concatenate([all_ref[g, k * group + per : (k + 1) * group] for k in range(shards)], 0)
        bc_main = bc_main + dot(main, spread)
        bc_rim = bc_rim + dot(rim, spread)
    bc_main = bc_main.astype(bf16)
    packed[0:HALO] = dot(rim_pick, bc_rim.astype(bf16))[0:HALO]
    lane_of = iota((LANES, LANES), 0) - quarter
    wide = iota((LANES, LANES), 1)
    copy_dt = ones_where(
        (lane_of >= 0) & (lane_of < heads)
        & ((lane_of == wide) | (lane_of + heads == wide) | (lane_of + 2 * heads == wide))
    )
    decay_rate = -jnp.exp(lines_ref[1:2])
    row_in = iota((ROWS, ROWS), 0)
    col_in = iota((ROWS, ROWS), 1)
    same_chunk = (row_in // CHUNK) == (col_in // CHUNK)
    lower = same_chunk & (col_in <= row_in)
    sums = ones_where(lower)
    expand = iota((LANES, heads * head_dim), 0)
    head_of = jnp.where(expand >= 2 * heads, expand - 2 * heads, jnp.where(expand >= heads, expand - heads, expand))
    channel = iota((LANES, heads * head_dim), 1)
    expand = ones_where(
        (expand < GROUPS * heads) & (channel >= head_of * head_dim) & (channel < (head_of + 1) * head_dim)
    )
    expand_ref[...] = expand
    for b in range(rows // ROWS):
        here = slice(b * ROWS, (b + 1) * ROWS)
        pick = ones_where(iota((ROWS, rows), 0) + b * ROWS == slots)
        pick_ref[here] = pick
        packed[HALO + b * ROWS : HALO + (b + 1) * ROWS] = dot(pick, bc_main)
        raw = dot(pick, own_main).astype(bf16)
        step = jax.nn.softplus(dot(raw, copy_dt) + lines_ref[0:1])
        log_decay = decay_rate * step
        high = log_decay.astype(bf16)
        rest = log_decay - high.astype(f32)
        middle = rest.astype(bf16)
        lowest = (rest - middle.astype(f32)).astype(bf16)
        log_sums[here] = dot(sums, high) + dot(sums, middle) + dot(sums, lowest)
        steps[here] = step
    total = jnp.zeros((1, LANES), f32)
    chunks = rows // CHUNK
    factors = []
    pending = None
    for c in range(chunks):
        here = slice(c * CHUNK, (c + 1) * CHUNK)
        logs = log_sums[here]
        centre = logs[CHUNK // 2 - 1 : CHUNK // 2]
        last = logs[CHUNK - 1 : CHUNK]
        outside_ref[here] = split_lanes(jnp.exp(logs - centre), heads)
        inside_ref[here] = split_lanes(jnp.exp(centre - logs) * steps[here], heads)
        offset = iota((CHUNK, LANES), 0) + c * CHUNK
        gap = distance(offset + base, info, seqs, FAR)
        gap_ref[here] = gap
        carried_ref[here] = split_lanes(jnp.where(gap > offset, jnp.exp(logs + total), 0.0), heads)
        if pending is not None:
            factors.append(jnp.exp(pending + centre))
        pending = last - centre
        total = total + last
    factors.append(jnp.exp(pending))
    end_gap = distance(base + rows - 1, info, seqs, FAR)
    decay = jnp.where(end_gap >= rows, jnp.exp(total), 0.0)
    for c in range(chunks):
        log_sums[c : c + 1] = factors[c]
    factor_ref[...] = dot(split_lanes(log_sums[0:chunks], heads), expand)
    log_sums[0:1] = decay
    log_sums[1:2] = lines_ref[2:3]
    rest_ref[...] = dot(split_lanes(log_sums[0:8], heads), expand)
    for b in range(rows // ROWS):
        here = slice(b * ROWS, (b + 1) * ROWS)
        gap = gap_ref[here]
        wide_gap = jnp.concatenate([gap] * (2 * state // LANES), 1)

        def shifted(lag):
            return packed[HALO + b * ROWS - lag : HALO + (b + 1) * ROWS - lag]

        both = convolve(shifted, taps_ref[...], wide_gap, width)
        keys, queries = both[:, :state], both[:, state:]
        query_ref[here] = queries
        offset = iota((ROWS, state), 0)
        in_chunk = offset % CHUNK
        zero = jnp.zeros_like(queries)
        kept_query_ref[here] = jnp.where(gap > in_chunk, queries.astype(f32), 0.0).astype(bf16)
        ends = jnp.zeros((ROWS, state), jnp.int32)
        for c in range(ROWS // CHUNK):
            end = base + b * ROWS + (c + 1) * CHUNK - 1
            ends = jnp.where(offset // CHUNK == c, distance(end, info, seqs, FAR), ends)
        last_keys = jnp.where(CHUNK - 1 - in_chunk <= ends, keys.astype(f32), 0.0)
        keys_ref[:, here] = last_keys.T.astype(bf16)
        scores = dot_nt(queries, keys)
        gap_square = jnp.concatenate([gap] * (ROWS // LANES), 1)
        scores = jnp.where(lower & (row_in - col_in <= gap_square), scores, 0.0)
        high, low = high_low(scores)
        score_high_ref[here] = high
        score_low_ref[here] = low


def scan_columns(
    shards, width, seqs,
    info, pick_ref, rims_ref, gap_ref, score_high_ref, score_low_ref, kept_query_ref, keys_ref,
    inside_ref, outside_ref, expand_ref, factor_ref, rest_ref, taps_ref, *refs,
):
    blocks = refs[:shards]
    out_ref, state_ref, arrived, packed = refs[shards:]
    rows = pick_ref.shape[0]
    per = rows // shards
    base = info[3]
    for k in range(shards):
        arrived[k * per : (k + 1) * per] = blocks[k][:per]
    rim = jnp.concatenate([blocks[k][per:] for k in range(shards)], 0)
    packed[0:HALO] = dot(rims_ref[...], rim)[0:HALO]
    expand = expand_ref[...]
    state_ref[...] = jnp.zeros_like(state_ref)
    for b in range(rows // ROWS):
        here = slice(b * ROWS, (b + 1) * ROWS)
        packed[HALO + b * ROWS : HALO + (b + 1) * ROWS] = dot(pick_ref[here], arrived[...])
        gap = gap_ref[here]

        def shifted(lag):
            return packed[HALO + b * ROWS - lag : HALO + (b + 1) * ROWS - lag]

        conv = convolve(shifted, taps_ref[...], jnp.concatenate([gap] * (TILE // LANES), 1), width).astype(f32)
        scaled = conv * dot(inside_ref[here], expand)
        high, low = high_low(scaled)
        score_high, score_low = score_high_ref[here], score_low_ref[here]
        total = dot(score_high, high) + dot(score_low, high) + dot(score_high, low)
        outside = dot(outside_ref[here], expand)
        carry = state_ref[...]
        parts = []
        for c in range(ROWS // CHUNK):
            inner = slice(c * CHUNK, (c + 1) * CHUNK)
            place = slice(b * ROWS + c * CHUNK, b * ROWS + (c + 1) * CHUNK)
            carry_high, carry_low = high_low(carry)
            kept = kept_query_ref[place]
            parts.append(dot(kept, carry_high) + dot(kept, carry_low))
            keys = keys_ref[:, place]
            added = dot(keys, high[inner]) + dot(keys, low[inner])
            end = base + b * ROWS + (c + 1) * CHUNK - 1
            keep = jnp.where(distance(end, info, seqs, FAR) >= CHUNK, 1.0, 0.0)
            number = b * (ROWS // CHUNK) + c
            carry = (carry * keep + added) * factor_ref[number : number + 1]
        state_ref[...] = carry
        out_ref[here] = outside * (total + jnp.concatenate(parts, 0)) + rest_ref[1:2] * conv


def gate_columns(shards, pick_ref, query_ref, carried_ref, expand_ref, scan_ref, state_ref, *refs):
    blocks = refs[:shards]
    out_ref, square_ref, arrived = refs[shards:]
    rows = pick_ref.shape[0]
    per = rows // shards
    for k in range(shards):
        arrived[k * per : (k + 1) * per] = blocks[k][...]

    @pl.when(pl.program_id(0) == 0)
    def _():
        square_ref[...] = jnp.zeros_like(square_ref)

    carry_high, carry_low = high_low(state_ref[...])
    for b in range(rows // ROWS):
        here = slice(b * ROWS, (b + 1) * ROWS)
        gate = dot(pick_ref[here], arrived[...])
        queries = query_ref[here]
        earlier = dot(queries, carry_high) + dot(queries, carry_low)
        outputs = scan_ref[here] + dot(carried_ref[here], expand_ref[...]) * earlier
        gated = outputs * silu(gate)
        out_ref[here] = gated
        squares = gated * gated
        part = squares[:, :LANES]
        for piece in range(1, TILE // LANES):
            part = part + squares[:, piece * LANES : (piece + 1) * LANES]
        square_ref[here] = square_ref[here] + part


def exchanged(blocks, axis):
    count = lax.axis_size(axis)
    moved = [
        lax.ppermute(blocks[k], axis, [(i, (i + k) % count) for i in range(count)]) for k in range(1, count)
    ]
    return [blocks[0]] + moved


def body(xs, gate_in, bc_in, dt_in, placement, lengths, conv_x, conv_bc, a_log, dt_bias, d_skip, norm_gain):
    shards = lax.axis_size("seq")
    groups = lax.axis_size("head")
    rows, inner = xs.shape
    width, seqs = conv_x.shape[0], lengths.shape[0]
    heads = a_log.shape[0]
    head_dim = inner // heads
    state = bc_in.shape[1] // 2
    per = rows // shards
    group = per + RIM
    tiles = inner // TILE
    chunks = rows // CHUNK
    me = lax.axis_index("seq").astype(jnp.int32)
    starts = jnp.cumsum(lengths) - lengths
    info = jnp.concatenate(
        [
            jnp.stack([me, lax.axis_index("head").astype(jnp.int32), jnp.int32(groups), me * rows]),
            starts.astype(jnp.int32),
        ]
    )
    triple = jnp.stack([dt_bias, a_log, d_skip])
    lines = jnp.pad(jnp.concatenate([triple] * GROUPS, 1), ((0, 5), (0, LANES - GROUPS * heads)))

    place = placement.reshape(1, rows)
    full = rows + shards * RIM
    sent = call(
        functools.partial(send_order, shards, width),
        [shape(full, rows)] + [shape(group, LANES)] * shards,
        (info, place, bc_in, dt_in),
        [smem(), whole(place), whole(bc_in), whole(dt_in)],
        [whole(shape(full, rows))] + [whole(shape(group, LANES))] * shards,
        flops=2 * full * rows * LANES * 2,
        nbytes=2 * full * rows,
    )
    picks, small = sent[0], sent[1:]
    small = exchanged(small, "seq")
    own = jnp.concatenate(small, 0)
    every = lax.all_gather(own, "head")

    x_send = call(
        functools.partial(gather_rows, shards, True),
        [shape(group, inner)] * shards,
        (picks, xs),
        [whole(picks), columns(rows)],
        [columns(group)] * shards,
        grid=(tiles,),
        flops=2 * full * rows * inner,
        nbytes=2 * full * rows + 4 * rows * inner,
    )
    x_blocks = exchanged(x_send, "seq")
    gate_send = call(
        functools.partial(gather_rows, shards, False),
        [shape(per, inner)] * shards,
        (picks, gate_in),
        [pl.BlockSpec((rows, rows), lambda j: (0, 0)), columns(rows)],
        [columns(per)] * shards,
        grid=(tiles,),
        flops=2 * rows * rows * inner,
        nbytes=2 * rows * rows + 4 * rows * inner,
    )

    kept = [
        shape(rows, rows),
        shape(RIM, shards * RIM),
        shape(rows, LANES, dtype=jnp.int32),
        shape(rows, ROWS),
        shape(rows, ROWS),
        shape(rows, state),
        shape(rows, state),
        shape(state, rows),
        shape(rows, LANES),
        shape(rows, LANES),
        shape(rows, LANES),
        shape(LANES, inner),
        shape(chunks, inner, dtype=f32),
        shape(8, inner, dtype=f32),
    ]
    (
        pick, rims, gap, score_high, score_low, query, kept_query,
        keys, inside, outside, carried, expand, factor, rest,
    ) = call(
        functools.partial(prepare, shards, width, seqs, heads, head_dim),
        kept,
        (info, own, every, conv_bc, lines),
        [smem(), whole(own), whole(every), whole(conv_bc), whole(lines)],
        [whole(s) for s in kept],
        scratch=[
            pltpu.VMEM((rows + HALO, 2 * state), f32),
            pltpu.VMEM((rows, LANES), f32),
            pltpu.VMEM((rows, LANES), f32),
        ],
        flops=2 * rows * rows * 4 * LANES,
        nbytes=2 * rows * rows,
    )

    gate_send, x_blocks = lax.optimization_barrier((gate_send, x_blocks))
    gate_blocks = exchanged(gate_send, "seq")

    scanned, local_state = call(
        functools.partial(scan_columns, shards, width, seqs),
        [shape(rows, inner, dtype=f32), shape(state, inner, dtype=f32)],
        (
            info, pick, rims, gap, score_high, score_low, kept_query, keys, inside, outside,
            expand, factor, rest, conv_x, *x_blocks,
        ),
        [smem()]
        + [whole(a) for a in (pick, rims, gap, score_high, score_low, kept_query, keys, inside, outside)]
        + [columns(LANES), columns(chunks), columns(8), columns(width)]
        + [columns(group)] * shards,
        [columns(rows), columns(state)],
        grid=(tiles,),
        scratch=[pltpu.VMEM((rows, TILE), bf16), pltpu.VMEM((rows + HALO, TILE), f32)],
        flops=2 * rows * inner * (rows + 8 * ROWS),
        nbytes=10 * rows * inner,
    )

    incoming = jnp.zeros((state, inner), f32)
    for step in range(1, shards):
        leaving = local_state + rest[0:1] * incoming
        incoming = incoming + lax.ppermute(leaving, "seq", [(step - 1, step)])

    gated, squares = call(
        functools.partial(gate_columns, shards),
        [shape(rows, inner, dtype=f32), shape(rows, LANES, dtype=f32)],
        (pick, query, carried, expand, scanned, incoming, *gate_blocks),
        [whole(pick), whole(query), whole(carried), columns(LANES), columns(rows), columns(state)]
        + [columns(per)] * shards,
        [columns(rows), pl.BlockSpec((rows, LANES), lambda j: (0, 0))],
        grid=(tiles,),
        scratch=[pltpu.VMEM((rows, TILE), bf16)],
        flops=2 * rows * inner * (rows + 3 * ROWS),
        nbytes=12 * rows * inner,
    )
    mean = lax.psum(jnp.sum(squares, axis=1), "head") / (inner * groups)
    result = gated * lax.rsqrt(mean + 1e-05)[:, None] * norm_gain[None, :]
    return result.astype(jnp.bfloat16)


def solution(mesh):
    in_specs = (
        P(("parts", "seq"), "head"),
        P(("parts", "seq"), "head"),
        P(("parts", "seq"), None),
        P(("parts", "seq"), "head"),
        P(("parts", "seq")),
        P("parts"),
        P(None, "head"),
        P(),
        P("head"),
        P("head"),
        P("head"),
        P("head"),
    )
    out_specs = P(("parts", "seq"), "head")
    return jax.shard_map(body, mesh=mesh, in_specs=in_specs, out_specs=out_specs, check_vma=False)
```

time: 488 us -> 255 us (0.52); the launches traced: 478 us -> 254 us
  local copies, waits for them, and re-layouts: 236 us -> 5.76 us
  Pallas kernels: 0 us -> 61.2 us
  other arithmetic: 56.9 us -> 12.5 us
  waiting for transfers between devices: 73.6 us -> 111 us
  blocking collectives: 41.7 us -> 5.68 us
  matrix products: 23.7 us -> 0 us
  starting transfers between devices: 30.5 us -> 44.4 us
    dynamic_update_slice x8 -> x0, local copies, waits for them, and re-layouts: 136 us -> none  [body(): lax.scan(block_pass, empty, (split(conv_rows), split(key_rows), split(que...]
    ppermute x1 -> x12, waiting for transfers between devices: 17.2 us -> 111 us  [the longest x9 96.3 us: exchanged(): lax.ppermute(blocks[k], axis, [(i, (i + k) % count) for i in range(count)])]
    pallas_call x0 -> x6, Pallas kernels: none -> 61.2 us  [call(): pl.pallas_call(kernel, grid=grid, in_specs=in_specs, out_specs=out_specs,...]
    all_to_all x5 -> x0, waiting for transfers between devices: 45 us -> none  [the longest x1 39.4 us: body(): lax.all_to_all(grouped(xs), 'seq', split_axis=0, concat_axis=0, tiled=True)]
    ppermute x1 -> x12, starting transfers between devices: 1.47 us -> 44.4 us  [the longest x9 41.7 us: exchanged(): lax.ppermute(blocks[k], axis, [(i, (i + k) % count) for i in range(count)])]
    unnamed x1 -> x0, blocking collectives: 35.9 us -> none
    gather x5 -> x0, local copies, waits for them, and re-layouts: 30.6 us -> none  [grouped(): return array[order].reshape((shards, per_dest) + array.shape[1:])]
    all_to_all x5 -> x0, starting transfers between devices: 29.1 us -> none  [the longest x1 6.92 us: body(): lax.all_to_all(grouped(gate_in), 'seq', split_axis=0, concat_axis=0, tile...]
  transfers between devices with their start and end apart: 7 -> 13, of which waited for: 4 -> 7; matrix products, arithmetic and copies ran while one was open for 56% -> 1% of each run, Pallas kernels for 0% -> 6%
where the time goes in v1:
time: 255 us; the launch traced here: 254 us
  waiting for transfers between devices  111 us (44%)
  Pallas kernels  61.2 us (24%)
  starting transfers between devices  44.4 us (17%)
  between operations  13.6 us (5%)
  other arithmetic  12.5 us (5%)
  local copies, waits for them, and re-layouts  5.76 us (2%)
  blocking collectives  5.68 us (2%)
    ppermute x9, waiting for transfers between devices, exchanged(): lax.ppermute(blocks[k], axis, [(i, (i + k) % count) for i in range(count)])  96.3 us
    pallas_call x6, Pallas kernels, call(): pl.pallas_call(kernel, grid=grid, in_specs=in_specs, out_specs=out_specs,...  61.2 us
    ppermute x9, starting transfers between devices, exchanged(): lax.ppermute(blocks[k], axis, [(i, (i + k) % count) for i in range(count)])  41.7 us
    ppermute x3, waiting for transfers between devices, body(): incoming = incoming + lax.ppermute(leaving, 'seq', [(step - 1, step)])  14.5 us
    psum x1, blocking collectives, body(): mean = lax.psum(jnp.sum(squares, axis=1), 'head') / (inner * groups)  5.68 us
  transfers between devices with their start and end apart: 13, of which 7 were waited for; matrix products, arithmetic and copies ran while one was open for 1% of the time, Pallas kernels for 6%

profile of v1, /device:TPU:26, one launch (start us, length us, event | category | flops | bytes accessed | tf_op | source)
XLA Modules:
  0.0 254.0 jit_solution(9908305764720683972)
XLA Ops:
  6.5 0.0 all-gather.3.cloned.1.call-start
  6.5 0.8 reduce-window.9
  7.4 0.7 bitcast_subtract_fusion
  8.0 1.6 copy.13.dt_ref
  9.6 0.6 concatenate.9.info
  10.2 4.7 %shard_map.118 = (bf16[1088,1024]{1,0:T(8,128)(2,1)}, bf16[272,128]{1,0:T(8,128)(2,1)}, bf16[272,128]{1,0:T(8,128)(2,1)}, bf16[272,128]{1,0:T(8,128)(2,1)}, bf16[272,128]{1,0:T(8,128)(2,1)}) custom-call(s32[7]{0:T(128)} %concatenate.9.info, s32[1,1024]{1,0:T(1,128)} %bitcast.15, bf16[1024,256]{1,0:T(8,128)(2,1)} %bc_ref.1, bf16[1024,16]{1,0:T(8,128)(2,1)} %copy.13.dt_ref), custom_call_target="tpu_custom_call" | custom-call | flops 570425344 | bytes 2228224 | tf_op jit(solution)/shard_map/pallas_call | solution.py:58
  14.9 0.2 collective-permute-start
  15.2 1.7 collective-permute-start.1
  16.8 0.4 collective-permute-start.2
  17.3 0.9 constant_dynamic-update-slice_fusion.3
  18.2 1.8 collective-permute-done
  20.0 3.8 %collective-permute-done.1 = bf16[272,128]{1,0:T(8,128)(2,1)S(1)} collective-permute-done((bf16[272,128]{1,0:T(8,128)(2,1)}, bf16[272,128]{1,0:T(8,128)(2,1)S(1)}, u32[]{:S(2)}, u32[]{:S(2)}) %collective-permute-start.1) | collective-permute-done | bytes 69664 | tf_op jit(solution)/shard_map/ppermute | solution.py:359
  23.8 0.0 collective-permute-done.2
  23.8 0.0 copy-start
  23.8 0.7 copy-done
  24.5 0.0 all-gather.3.cloned.1.call-update
  24.5 0.0 copy-start.2
  24.6 0.0 copy-start.3
  24.6 0.0 copy-start.4
  24.6 7.5 %shard_map.121 = (bf16[272,1280]{1,0:T(8,128)(2,1)}, bf16[272,1280]{1,0:T(8,128)(2,1)}, bf16[272,1280]{1,0:T(8,128)(2,1)}, bf16[272,1280]{1,0:T(8,128)(2,1)}) custom-call(bf16[1088,1024]{1,0:T(8,128)(2,1)} %get-tuple-element.62.pick_ref, bf16[1024,1280]{1,0:T(8,128)(2,1)} %x_ref.3), custom_call_target="tpu_custom_call" | custom-call | flops 2852126720 | bytes 7471104 | tf_op jit(solution)/shard_map/pallas_call | solution.py:58
  32.1 0.7 collective-permute-start.3
  32.8 0.3 collective-permute-start.4
  33.1 2.0 collective-permute-start.5
  35.0 0.0 copy-done.2
  35.0 0.0 copy-done.3
  35.0 0.0 copy-done.4
  35.0 0.7 fusion.lines_ref
  35.7 7.0 %shard_map.120 = (bf16[256,1280]{1,0:T(8,128)(2,1)}, bf16[256,1280]{1,0:T(8,128)(2,1)}, bf16[256,1280]{1,0:T(8,128)(2,1)}, bf16[256,1280]{1,0:T(8,128)(2,1)}) custom-call(bf16[1088,1024]{1,0:T(8,128)(2,1)} %get-tuple-element.62.pick_ref, bf16[1024,1280]{1,0:T(8,128)(2,1)} %x_ref.2), custom_call_target="tpu_custom_call" | custom-call | flops 2684354560 | bytes 7340032 | tf_op jit(solution)/shard_map/pallas_call | solution.py:58
  42.7 6.5 %collective-permute-done.3.refs_1_ = bf16[272,1280]{1,0:T(8,128)(2,1)S(1)} collective-permute-done((bf16[272,1280]{1,0:T(8,128)(2,1)}, bf16[272,1280]{1,0:T(8,128)(2,1)S(1)}, u32[]{:S(2)}, u32[]{:S(2)}) %collective-permute-start.3) | collective-permute-done | bytes 696352 | tf_op jit(solution)/shard_map/ppermute | solution.py:359
  49.2 44.3 %collective-permute-done.4.refs_2_ = bf16[272,1280]{1,0:T(8,128)(2,1)S(1)} collective-permute-done((bf16[272,1280]{1,0:T(8,128)(2,1)}, bf16[272,1280]{1,0:T(8,128)(2,1)S(1)}, u32[]{:S(2)}, u32[]{:S(2)}) %collective-permute-start.4) | collective-permute-done | bytes 696352 | tf_op jit(solution)/shard_map/ppermute | solution.py:359
  93.5 0.0 collective-permute-done.5.refs_3_
  93.5 0.0 all-gather.3.cloned.1.call-done
  93.6 8.8 %shard_map.119 = (bf16[1024,1024]{1,0:T(8,128)(2,1)}, bf16[16,64]{1,0:T(8,128)(2,1)}, s32[1024,128]{1,0:T(8,128)}, bf16[1024,256]{1,0:T(8,128)(2,1)}, bf16[1024,...) custom-call(s32[7]{0:T(128)} %concatenate.9.info, ...), custom_call_target="tpu_custom_call" | custom-call | flops 1073741824 | bytes 2097152 | tf_op jit(solution)/shard_map/pallas_call | solution.py:58
  102.3 0.8 slice_reduce_fusion
  103.1 0.0 copy-done.5
  103.1 0.0 copy-done.6
  103.2 0.0 copy-done.7
  103.2 22.2 %shard_map.122 = (f32[1024,1280]{1,0:T(8,128)}, f32[128,1280]{1,0:T(8,128)}) custom-call(s32[7]{0:T(128)} %concatenate.9.info, bf16[1024,1024]{1,0:T(8,128)(2,1)} %get-tuple-element.48.pick_ref, bf16[16,64]{1,0:T(8,128)(2,1)} %get-tuple-element.52.rims_ref, s32[1024,128]{1,0:T(8,128)} %get-tuple-element.53.gap_ref, ...), custom_call_target="tpu_custom_call" | custom-call | flops 8053063680 | bytes 13107200 | tf_op jit(solution)/shard_map/pallas_call | solution.py:58
  125.4 0.0 copy-start.10
  125.4 1.3 broadcast_add_fusion
  126.7 0.7 collective-permute-start.6
  127.4 0.0 collective-permute-done.6
  127.4 1.2 multiply_add_fusion.1
  128.6 0.7 collective-permute-start.7
  129.3 0.0 collective-permute-done.7
  129.3 1.2 multiply_add_fusion
  130.5 1.3 collective-permute-start.8
  131.8 0.0 copy-done.10
  131.8 18.1 %collective-permute-start.9 = (bf16[256,1280]{1,0:T(8,128)(2,1)S(1)}, bf16[256,1280]{1,0:T(8,128)(2,1)S(1)}, u32[]{:S(2)}, u32[]{:S(2)}) collective-permute-start(bf16[256,1280]{1,0:T(8,128)(2,1)S(1)} %copy-done.10), channel_id=1, source_target_pairs={{0,4},{4,8},{8,12},{12,0},{1,5},{5,9},{9,13},{13,1},{2,6},{6,10},{... | collective-permute-start | bytes 1966088 | tf_op jit(solution)/shard_map/ppermute | solution.py:359
  150.0 0.0 copy-done.9
  150.0 18.3 %collective-permute-start.10 = (bf16[256,1280]{1,0:T(8,128)(2,1)S(1)}, bf16[256,1280]{1,0:T(8,128)(2,1)S(1)}, u32[]{:S(2)}, u32[]{:S(2)}) collective-permute-start(bf16[256,1280]{1,0:T(8,128)(2,1)S(1)} %copy-done.9), channel_id=1, source_target_pairs={{0,8},{4,12},{8,0},{12,4},{1,9},{5,13},{9,1},{13,5},{2,10},{6,14},... | collective-permute-start | bytes 1966088 | tf_op jit(solution)/shard_map/ppermute | solution.py:359
  168.3 0.0 copy-done.8
  168.3 0.0 collective-permute-start.11
  168.3 14.5 %collective-permute-done.8 = f32[128,1280]{1,0:T(8,128)S(1)} collective-permute-done((f32[128,1280]{1,0:T(8,128)S(1)}, f32[128,1280]{1,0:T(8,128)S(1)}, u32[]{:S(2)}, u32[]{:S(2)}) %collective-permute-start.8) | collective-permute-done | bytes 655392 | tf_op jit(solution)/shard_map/ppermute | solution.py:483
  182.8 0.9 add.29.state_ref
  183.7 25.6 %collective-permute-done.9.refs_1_ = bf16[256,1280]{1,0:T(8,128)(2,1)S(1)} collective-permute-done((bf16[256,1280]{1,0:T(8,128)(2,1)S(1)}, bf16[256,1280]{1,0:T(8,128)(2,1)S(1)}, u32[]{:S(2)}, u32[]{:S(2)}) %collective-permute-start.9) | collective-permute-done | bytes 655392 | tf_op jit(solution)/shard_map/ppermute | solution.py:359
  209.3 14.2 %collective-permute-done.10.refs_2_ = bf16[256,1280]{1,0:T(8,128)(2,1)S(1)} collective-permute-done((bf16[256,1280]{1,0:T(8,128)(2,1)S(1)}, bf16[256,1280]{1,0:T(8,128)(2,1)S(1)}, u32[]{:S(2)}, u32[]{:S(2)}) %collective-permute-start.10) | collective-permute-done | bytes 655392 | tf_op jit(solution)/shard_map/ppermute | solution.py:359
  223.6 0.0 collective-permute-done.11.refs_3_
  223.6 0.9 copy-done.12
  224.4 0.2 copy-done.13
  224.6 11.1 %shard_map.123 = (f32[1024,1280]{1,0:T(8,128)}, f32[1024,128]{1,0:T(8,128)}) custom-call(bf16[1024,1024]{1,0:T(8,128)(2,1)} %get-tuple-element.48.pick_ref, bf16[1024,128]{1,0:T(8,128)(2,1)} %get-tuple-element.49.query_ref, bf16[1024,128]{1,0:T(8,128)(2,1)} %get-tuple-element.50.carried_ref, bf16[128,1280]{1,0:T(8,128)(2,1)} %get-tuple-element.51.expand_ref, ...), custom_call_target="tpu_custom_call" | custom-call | flops 4697620480 | bytes 15728640 | tf_op jit(solution)/shard_map/pallas_call | solution.py:58
  235.7 1.2 reduce_sum.9
  237.0 5.7 %psum.7 = f32[1024]{0:T(1024)S(1)} all-reduce(f32[1024]{0:T(1024)S(1)} %reduce_sum.9), channel_id=1, replica_groups=mesh['parts'=2,'seq'=4,'head'=4] {'head'}, use_global_device_ids=true, to_apply=%region_2.3 | all-reduce | flops 1024 | bytes 8192 | tf_op jit(solution)/shard_map/psum | solution.py:497
  242.6 4.5 %multiply_convert_fusion = bf16[1024,1280]{1,0:T(8,128)(2,1)} fusion(f32[1024,1280]{1,0:T(8,128)} %get-tuple-element.81, f32[1280]{0:T(1024)S(1)} %copy-done.1, f32[1024]{0:T(1024)S(1)} %add_rsqrt_fusion), kind=kLoop, calls=%fused_computation | loop fusion | flops 3932160 | bytes 7873536 | tf_op jit(solution)/shard_map/convert_element_type | solution.py:499
  (16 shorter events, 0.1 us)
Async XLA Ops:
  6.5 87.0 %all-gather.3.cloned.1.call-start = ((), (), s32[]{:S(2)}) async-start(), calls=%async_computation | async-start | bytes 1392640 | tf_op jit(solution)/shard_map/all_gather | solution.py:401
  14.9 5.0 %collective-permute-start = (bf16[272,128]{1,0:T(8,128)(2,1)}, bf16[272,128]{1,0:T(8,128)(2,1)S(1)}, u32[]{:S(2)}, u32[]{:S(2)}) collective-permute-start(bf16[272,128]{1,0:T(8,128)(2,1)} %get-tuple-element.45), channel_id=1, source_target_pairs={{0,4},{4,8},{8,12},{12,0},{1,5},{5,9},{9,13},{13,1},{2,6},{6,10},{... | collective-permute-start | bytes 208904 | tf_op jit(solution)/shard_map/ppermute | solution.py:359
  15.2 8.6 %collective-permute-start.1 = (bf16[272,128]{1,0:T(8,128)(2,1)}, bf16[272,128]{1,0:T(8,128)(2,1)S(1)}, u32[]{:S(2)}, u32[]{:S(2)}) collective-permute-start(bf16[272,128]{1,0:T(8,128)(2,1)} %get-tuple-element.46), channel_id=1, source_target_pairs={{0,8},{4,12},{8,0},{12,4},{1,9},{5,13},{9,1},{13,5},{2,10},{6,14},... | collective-permute-start | bytes 208904 | tf_op jit(solution)/shard_map/ppermute | solution.py:359
  16.8 6.9 %collective-permute-start.2 = (bf16[272,128]{1,0:T(8,128)(2,1)}, bf16[272,128]{1,0:T(8,128)(2,1)S(1)}, u32[]{:S(2)}, u32[]{:S(2)}) collective-permute-start(bf16[272,128]{1,0:T(8,128)(2,1)} %get-tuple-element.47), channel_id=1, source_target_pairs={{0,12},{4,0},{8,4},{12,8},{1,13},{5,1},{9,5},{13,9},{2,14},{6,2},{... | collective-permute-start | bytes 208904 | tf_op jit(solution)/shard_map/ppermute | solution.py:359
  23.8 0.7 copy-start
  24.5 10.5 %copy-start.2 = (f32[16]{0:T(128)S(1)}, f32[16]{0:T(128)}, u32[]{:S(2)}) copy-start(f32[16]{0:T(128)} %param.22) | copy-start | bytes 196
  24.6 10.5 %copy-start.3 = (f32[16]{0:T(128)S(1)}, f32[16]{0:T(128)}, u32[]{:S(2)}) copy-start(f32[16]{0:T(128)} %param.20) | copy-start | bytes 196
  24.6 10.5 %copy-start.4 = (f32[16]{0:T(128)S(1)}, f32[16]{0:T(128)}, u32[]{:S(2)}) copy-start(f32[16]{0:T(128)} %param.21) | copy-start | bytes 196
  32.1 17.2 %collective-permute-start.3 = (bf16[272,1280]{1,0:T(8,128)(2,1)}, bf16[272,1280]{1,0:T(8,128)(2,1)S(1)}, u32[]{:S(2)}, u32[]{:S(2)}) collective-permute-start(bf16[272,1280]{1,0:T(8,128)(2,1)} %get-tuple-element.68), channel_id=1, source_target_pairs={{0,4},{4,8},{8,12},{12,0},{1,5},{5,9},{9,13},{13,1},{2,6},{6,10},{... | collective-permute-start | bytes 2088968 | tf_op jit(solution)/shard_map/ppermute | solution.py:359
  32.8 60.8 %collective-permute-start.4 = (bf16[272,1280]{1,0:T(8,128)(2,1)}, bf16[272,1280]{1,0:T(8,128)(2,1)S(1)}, u32[]{:S(2)}, u32[]{:S(2)}) collective-permute-start(bf16[272,1280]{1,0:T(8,128)(2,1)} %get-tuple-element.69), channel_id=1, source_target_pairs={{0,8},{4,12},{8,0},{12,4},{1,9},{5,13},{9,1},{13,5},{2,10},{6,14},... | collective-permute-start | bytes 2088968 | tf_op jit(solution)/shard_map/ppermute | solution.py:359
  33.1 60.5 %collective-permute-start.5 = (bf16[272,1280]{1,0:T(8,128)(2,1)}, bf16[272,1280]{1,0:T(8,128)(2,1)S(1)}, u32[]{:S(2)}, u32[]{:S(2)}) collective-permute-start(bf16[272,1280]{1,0:T(8,128)(2,1)} %get-tuple-element.70), channel_id=1, source_target_pairs={{0,12},{4,0},{8,4},{12,8},{1,13},{5,1},{9,5},{13,9},{2,14},{6,2},{... | collective-permute-start | bytes 2088968 | tf_op jit(solution)/shard_map/ppermute | solution.py:359
  49.2 53.9 %copy-start.5 = (bf16[272,1280]{1,0:T(8,128)(2,1)}, bf16[272,1280]{1,0:T(8,128)(2,1)S(1)}, u32[]{:S(2)}) copy-start(bf16[272,1280]{1,0:T(8,128)(2,1)S(1)} %collective-permute-done.3.refs_1_) | copy-start | bytes 2088964
  93.5 9.6 %copy-start.6 = (bf16[272,1280]{1,0:T(8,128)(2,1)}, bf16[272,1280]{1,0:T(8,128)(2,1)S(1)}, u32[]{:S(2)}) copy-start(bf16[272,1280]{1,0:T(8,128)(2,1)S(1)} %collective-permute-done.4.refs_2_) | copy-start | bytes 2088964
  93.5 9.6 %copy-start.7 = (bf16[272,1280]{1,0:T(8,128)(2,1)}, bf16[272,1280]{1,0:T(8,128)(2,1)S(1)}, u32[]{:S(2)}) copy-start(bf16[272,1280]{1,0:T(8,128)(2,1)S(1)} %collective-permute-done.5.refs_3_) | copy-start | bytes 2088964
  125.4 6.4 %copy-start.10 = (bf16[256,1280]{1,0:T(8,128)(2,1)S(1)}, bf16[256,1280]{1,0:T(8,128)(2,1)}, u32[]{:S(2)}) copy-start(bf16[256,1280]{1,0:T(8,128)(2,1)} %get-tuple-element.78) | copy-start | bytes 1966084
  125.4 24.6 %copy-start.9 = (bf16[256,1280]{1,0:T(8,128)(2,1)S(1)}, bf16[256,1280]{1,0:T(8,128)(2,1)}, u32[]{:S(2)}) copy-start(bf16[256,1280]{1,0:T(8,128)(2,1)} %get-tuple-element.79) | copy-start | bytes 1966084
  125.4 42.9 %copy-start.8 = (bf16[256,1280]{1,0:T(8,128)(2,1)S(1)}, bf16[256,1280]{1,0:T(8,128)(2,1)}, u32[]{:S(2)}) copy-start(bf16[256,1280]{1,0:T(8,128)(2,1)} %get-tuple-element.80) | copy-start | bytes 1966084
  126.7 0.7 collective-permute-start.6
  128.6 0.7 collective-permute-start.7
  130.5 52.3 %collective-permute-start.8 = (f32[128,1280]{1,0:T(8,128)S(1)}, f32[128,1280]{1,0:T(8,128)S(1)}, u32[]{:S(2)}, u32[]{:S(2)}) collective-permute-start(f32[128,1280]{1,0:T(8,128)S(1)} %get-tuple-element.83), channel_id=1, source_target_pairs={{8,12},{9,13},{10,14},{11,15},{24,28},{25,29},{26,30},{27,31}} | collective-permute-start | bytes 1966088 | tf_op jit(solution)/shard_map/ppermute | solution.py:483
  131.8 77.5 %collective-permute-start.9 = (bf16[256,1280]{1,0:T(8,128)(2,1)S(1)}, bf16[256,1280]{1,0:T(8,128)(2,1)S(1)}, u32[]{:S(2)}, u32[]{:S(2)}) collective-permute-start(bf16[256,1280]{1,0:T(8,128)(2,1)S(1)} %copy-done.10), channel_id=1, source_target_pairs={{0,4},{4,8},{8,12},{12,0},{1,5},{5,9},{9,13},{13,1},{2,6},{6,10},{... | collective-permute-start | bytes 1966088 | tf_op jit(solution)/shard_map/ppermute | solution.py:359
  150.0 73.6 %collective-permute-start.10 = (bf16[256,1280]{1,0:T(8,128)(2,1)S(1)}, bf16[256,1280]{1,0:T(8,128)(2,1)S(1)}, u32[]{:S(2)}, u32[]{:S(2)}) collective-permute-start(bf16[256,1280]{1,0:T(8,128)(2,1)S(1)} %copy-done.9), channel_id=1, source_target_pairs={{0,8},{4,12},{8,0},{12,4},{1,9},{5,13},{9,1},{13,5},{2,10},{6,14},... | collective-permute-start | bytes 1966088 | tf_op jit(solution)/shard_map/ppermute | solution.py:359
  168.3 55.3 %collective-permute-start.11 = (bf16[256,1280]{1,0:T(8,128)(2,1)S(1)}, bf16[256,1280]{1,0:T(8,128)(2,1)S(1)}, u32[]{:S(2)}, u32[]{:S(2)}) collective-permute-start(bf16[256,1280]{1,0:T(8,128)(2,1)S(1)} %copy-done.8), channel_id=1, source_target_pairs={{0,12},{4,0},{8,4},{12,8},{1,13},{5,1},{9,5},{13,9},{2,14},{6,2},{... | collective-permute-start | bytes 1966088 | tf_op jit(solution)/shard_map/ppermute | solution.py:359
  209.3 14.2 %copy-start.11 = (bf16[256,1280]{1,0:T(8,128)(2,1)}, bf16[256,1280]{1,0:T(8,128)(2,1)S(1)}, u32[]{:S(2)}) copy-start(bf16[256,1280]{1,0:T(8,128)(2,1)S(1)} %collective-permute-done.9.refs_1_) | copy-start | bytes 1966084
  223.6 0.9 copy-start.12
  223.6 1.1 copy-start.13
  224.6 18.0 %copy-start.1 = (f32[1280]{0:T(1024)S(1)}, f32[1280]{0:T(1024)}, u32[]{:S(2)}) copy-start(f32[1280]{0:T(1024)} %param.23) | copy-start | bytes 15364
Sparse Core Ops, SparseCore 0:
  24.7 17.1 all-gather.2

commit v2 on v1

v2 whole, which is shorter than its diff:
```python
import functools

import jax
import jax.numpy as jnp
from jax import lax
from jax.experimental import pallas as pl
from jax.experimental.pallas import tpu as pltpu
from jax.sharding import PartitionSpec as P

CHUNK = 64
ROWS = 256
TILE = 256
LANES = 128
RIM = 16
SHARES = (0.4, 0.8)
GATE_SHARES = (0.4, 0.8)
HALO = 8
GROUPS = 3
FAR = 1 << 28
FLOPS_US = 1_150_000_000
bf16 = jnp.bfloat16
f32 = jnp.float32


def dot(a, b):
    return jnp.dot(a, b, preferred_element_type=f32)


def dot_nt(a, b):
    return lax.dot_general(a, b, (((1,), (1,)), ((), ())), preferred_element_type=f32)


def iota(shape, dim):
    return lax.broadcasted_iota(jnp.int32, shape, dim)


def ones_where(mask):
    return jnp.where(mask, 1.0, 0.0).astype(bf16)


def high_low(value):
    high = value.astype(bf16)
    return high, (value - high.astype(f32)).astype(bf16)


def split_lanes(value, heads):
    lane = iota(value.shape, 1)
    high = value.astype(bf16).astype(f32)
    rest = value - high
    middle = rest.astype(bf16).astype(f32)
    lowest = rest - middle
    pieces = jnp.where(lane < heads, high, jnp.where(lane < 2 * heads, middle, lowest))
    return jnp.where(lane < GROUPS * heads, pieces, 0.0).astype(bf16)


def silu(value):
    return value * jax.nn.sigmoid(value)


def call(kernel, outs, args, in_specs, out_specs, grid=(1,), scratch=(), micros=1, limit=24):
    return pl.pallas_call(
        kernel,
        grid=grid,
        in_specs=in_specs,
        out_specs=out_specs,
        out_shape=outs,
        scratch_shapes=list(scratch),
        compiler_params=pltpu.CompilerParams(vmem_limit_bytes=limit * 1024 * 1024),
        cost_estimate=pl.CostEstimate(flops=int(micros * FLOPS_US), bytes_accessed=0, transcendentals=0),
    )(*args)


def whole(array):
    rank = len(array.shape)
    return pl.BlockSpec(array.shape, lambda *_: (0,) * rank)


def columns(rows, width=TILE, start=0):
    return pl.BlockSpec((rows, width), lambda j: (0, j + start))


def smem():
    return pl.BlockSpec(memory_space=pltpu.SMEM)


def shape(*dims, dtype=bf16):
    return jax.ShapeDtypeStruct(dims, dtype)


def send_order(shards, width, place_ref, bc_ref, dt_ref, x_ref, pick_ref, *refs):
    small_refs, x_refs = refs[:shards], refs[shards:]
    rows = place_ref.shape[1]
    per = rows // shards
    heads = dt_ref.shape[0]
    wide = bc_ref.shape[1]

    @pl.when(pl.program_id(0) == 0)
    def _():
        me = lax.axis_index("seq")
        place = place_ref[...]
        padded = max(8, shards)
        owner = iota((padded, rows), 0)
        first = owner * rows
        mine = (place >= first) & (place < first + rows)
        chosen = ones_where(mine)
        earlier = ones_where(iota((LANES, LANES), 0) < iota((LANES, LANES), 1))
        before, seen = [], jnp.zeros((padded, 1), f32)
        for piece in range(rows // LANES):
            part = chosen[:, piece * LANES : (piece + 1) * LANES]
            before.append(dot(part, earlier) + seen)
            seen = seen + jnp.sum(part.astype(f32), axis=1, keepdims=True)
        before = jnp.concatenate(before, 1)
        relative = jnp.where(owner >= me, owner - me, owner - me + shards)
        target = before + (relative * per).astype(f32)
        target = jnp.sum(jnp.where(mine, target, 0.0), axis=0, keepdims=True).astype(jnp.int32)
        local = jnp.sum(jnp.where(mine, (place - first + 1).astype(f32), 0.0), axis=0, keepdims=True)
        high = jnp.floor(local * (1.0 / 64.0))
        low = local - 64.0 * high
        line = iota((LANES - heads, rows), 0)
        digits = jnp.where(line == 0, high, jnp.where(line == 1, low, 0.0)).astype(bf16)
        thin = jnp.concatenate([dt_ref[...], digits], 0)
        for k in range(shards):
            pick = ones_where(iota((per, rows), 0) + k * per == target)
            pick_ref[k * per : (k + 1) * per] = pick
            dest = jnp.where(me + k >= shards, me + k - shards, me + k)
            row = iota((RIM, rows), 0)
            rim = ones_where((row < width - 1) & (place == row + (dest * rows - (width - 1))))
            pick_ref[rows + k * RIM : rows + (k + 1) * RIM] = rim
            small_refs[k][:per, :wide] = dot(pick, bc_ref[...]).astype(bf16)
            small_refs[k][per:, :wide] = dot(rim, bc_ref[...]).astype(bf16)
            small_refs[k][:per, wide:] = dot_nt(pick, thin).astype(bf16)
            small_refs[k][per:, wide:] = dot_nt(rim, thin).astype(bf16)

    gather_rows(shards, True, pick_ref, x_ref, *x_refs)


def gather_rows(shards, with_rim, pick_ref, x_ref, *out_refs):
    rows = x_ref.shape[0]
    per = rows // shards
    values = x_ref[...]
    for k in range(shards):
        out_refs[k][:per] = dot(pick_ref[k * per : (k + 1) * per], values).astype(bf16)
    if with_rim:
        rims = dot(pick_ref[rows:], values).astype(bf16)
        for k in range(shards):
            out_refs[k][per:] = rims[k * RIM : (k + 1) * RIM]


def gather_parts(shards, parts, pick_ref, x_ref, *out_refs):
    rows = x_ref.shape[0]
    per = rows // shards
    values = x_ref[...]
    for number, (first, last) in enumerate(parts):

        @pl.when((pl.program_id(0) >= first) & (pl.program_id(0) < last))
        def _():
            for k in range(shards):
                taken = dot(pick_ref[k * per : (k + 1) * per], values)
                out_refs[number * shards + k][...] = taken.astype(bf16)


def distance(position, lengths, limit):
    gap, start = limit, 0
    for j in range(lengths.shape[0]):
        gap = jnp.where(position >= start, jnp.minimum(gap, position - start), gap)
        start = start + lengths[j]
    return gap


def convolve(block_of, taps, gap, width):
    total = taps[0:1] * block_of(0)
    for lag in range(1, width):
        total = total + jnp.where(gap >= lag, taps[lag : lag + 1] * block_of(lag), 0.0)
    return silu(total).astype(bf16)


def prepare(
    shards, width, heads, head_dim, lengths, *refs
):
    own_refs = refs[:shards]
    (
        taps_ref, lines_ref,
        pick_ref, rims_ref, gap_ref, score_high_ref, score_low_ref, query_ref, kept_query_ref,
        keys_ref, inside_ref, outside_ref, carried_ref, expand_ref, factor_ref, rest_ref,
        packed, log_sums, steps,
    ) = refs[shards:]
    rows = pick_ref.shape[0]
    per = rows // shards
    state = query_ref.shape[1]
    base = lax.axis_index("seq") * rows
    own_main = jnp.concatenate([ref[:per] for ref in own_refs], 0)
    own_rim = jnp.concatenate([ref[per:] for ref in own_refs], 0)
    lane = iota((8, LANES), 1)
    weights = jnp.where(lane == heads, 64.0, jnp.where(lane == heads + 1, 1.0, 0.0)).astype(bf16)
    slots = dot_nt(weights, own_main[:, 2 * state :])[0:1].astype(jnp.int32) - 1
    rim_slots = dot_nt(weights, own_rim[:, 2 * state :])[0:1].astype(jnp.int32) - 1 - rows + HALO
    rim_pick = ones_where(iota((RIM, shards * RIM), 0) == rim_slots)
    rims_ref[...] = rim_pick
    bc_main = own_main[:, : 2 * state]
    own_main = own_main[:, 2 * state :]
    packed[0:HALO] = dot(rim_pick, own_rim[:, : 2 * state])[0:HALO]
    lane_of = iota((LANES, LANES), 0)
    wide = iota((LANES, LANES), 1)
    copy_dt = ones_where(
        (lane_of < heads)
        & ((lane_of == wide) | (lane_of + heads == wide) | (lane_of + 2 * heads == wide))
    )
    decay_rate = -jnp.exp(lines_ref[1:2])
    row_in = iota((ROWS, ROWS), 0)
    col_in = iota((ROWS, ROWS), 1)
    same_chunk = (row_in // CHUNK) == (col_in // CHUNK)
    lower = same_chunk & (col_in <= row_in)
    sums = ones_where(lower)
    expand = iota((LANES, heads * head_dim), 0)
    head_of = jnp.where(expand >= 2 * heads, expand - 2 * heads, jnp.where(expand >= heads, expand - heads, expand))
    channel = iota((LANES, heads * head_dim), 1)
    expand = ones_where(
        (expand < GROUPS * heads) & (channel >= head_of * head_dim) & (channel < (head_of + 1) * head_dim)
    )
    expand_ref[...] = expand
    for b in range(rows // ROWS):
        here = slice(b * ROWS, (b + 1) * ROWS)
        pick = ones_where(iota((ROWS, rows), 0) + b * ROWS == slots)
        pick_ref[here] = pick
        packed[HALO + b * ROWS : HALO + (b + 1) * ROWS] = dot(pick, bc_main)
        raw = dot(pick, own_main).astype(bf16)
        step = jax.nn.softplus(dot(raw, copy_dt) + lines_ref[0:1])
        log_decay = decay_rate * step
        high = log_decay.astype(bf16)
        rest = log_decay - high.astype(f32)
        middle = rest.astype(bf16)
        lowest = (rest - middle.astype(f32)).astype(bf16)
        log_sums[here] = dot(sums, high) + dot(sums, middle) + dot(sums, lowest)
        steps[here] = step
    total = jnp.zeros((1, LANES), f32)
    chunks = rows // CHUNK
    factors = []
    pending = None
    for c in range(chunks):
        here = slice(c * CHUNK, (c + 1) * CHUNK)
        logs = log_sums[here]
        centre = logs[CHUNK // 2 - 1 : CHUNK // 2]
        last = logs[CHUNK - 1 : CHUNK]
        outside_ref[here] = split_lanes(jnp.exp(logs - centre), heads)
        inside_ref[here] = split_lanes(jnp.exp(centre - logs) * steps[here], heads)
        offset = iota((CHUNK, LANES), 0) + c * CHUNK
        gap = distance(offset + base, lengths, FAR)
        gap_ref[here] = gap
        carried_ref[here] = split_lanes(jnp.where(gap > offset, jnp.exp(logs + total), 0.0), heads)
        if pending is not None:
            factors.append(jnp.exp(pending + centre))
        pending = last - centre
        total = total + last
    factors.append(jnp.exp(pending))
    end_gap = distance(base + rows - 1, lengths, FAR)
    decay = jnp.where(end_gap >= rows, jnp.exp(total), 0.0)
    for c in range(chunks):
        log_sums[c : c + 1] = factors[c]
    factor_ref[...] = dot(split_lanes(log_sums[0:chunks], heads), expand)
    log_sums[0:1] = decay
    log_sums[1:2] = lines_ref[2:3]
    rest_ref[...] = dot(split_lanes(log_sums[0:8], heads), expand)
    for b in range(rows // ROWS):
        here = slice(b * ROWS, (b + 1) * ROWS)
        gap = gap_ref[here]
        wide_gap = jnp.concatenate([gap] * (2 * state // LANES), 1)

        def shifted(lag):
            return packed[HALO + b * ROWS - lag : HALO + (b + 1) * ROWS - lag]

        both = convolve(shifted, taps_ref[...], wide_gap, width)
        keys, queries = both[:, :state], both[:, state:]
        query_ref[here] = queries
        offset = iota((ROWS, state), 0)
        in_chunk = offset % CHUNK
        zero = jnp.zeros_like(queries)
        kept_query_ref[here] = jnp.where(gap > in_chunk, queries.astype(f32), 0.0).astype(bf16)
        ends = jnp.zeros((ROWS, state), jnp.int32)
        for c in range(ROWS // CHUNK):
            end = base + b * ROWS + (c + 1) * CHUNK - 1
            ends = jnp.where(offset // CHUNK == c, distance(end, lengths, FAR), ends)
        last_keys = jnp.where(CHUNK - 1 - in_chunk <= ends, keys.astype(f32), 0.0)
        keys_ref[:, here] = last_keys.T.astype(bf16)
        scores = dot_nt(queries, keys)
        gap_square = jnp.concatenate([gap] * (ROWS // LANES), 1)
        scores = jnp.where(lower & (row_in - col_in <= gap_square), scores, 0.0)
        high, low = high_low(scores)
        score_high_ref[here] = high
        score_low_ref[here] = low


def scan_columns(
    shards, width,
    lengths, pick_ref, rims_ref, gap_ref, score_high_ref, score_low_ref, kept_query_ref, keys_ref,
    inside_ref, outside_ref, expand_ref, factor_ref, rest_ref, taps_ref, *refs,
):
    blocks = refs[:shards]
    out_ref, state_ref, arrived, packed = refs[shards:]
    rows = pick_ref.shape[0]
    per = rows // shards
    base = lax.axis_index("seq") * rows
    for k in range(shards):
        arrived[k * per : (k + 1) * per] = blocks[k][:per]
    rim = jnp.concatenate([blocks[k][per:] for k in range(shards)], 0)
    packed[0:HALO] = dot(rims_ref[...], rim)[0:HALO]
    expand = expand_ref[...]
    state_ref[...] = jnp.zeros_like(state_ref)
    for b in range(rows // ROWS):
        here = slice(b * ROWS, (b + 1) * ROWS)
        packed[HALO + b * ROWS : HALO + (b + 1) * ROWS] = dot(pick_ref[here], arrived[...])
        gap = gap_ref[here]

        def shifted(lag):
            return packed[HALO + b * ROWS - lag : HALO + (b + 1) * ROWS - lag]

        conv = convolve(shifted, taps_ref[...], jnp.concatenate([gap] * (TILE // LANES), 1), width).astype(f32)
        scaled = conv * dot(inside_ref[here], expand)
        high, low = high_low(scaled)
        score_high, score_low = score_high_ref[here], score_low_ref[here]
        total = dot(score_high, high) + dot(score_low, high) + dot(score_high, low)
        outside = dot(outside_ref[here], expand)
        carry = state_ref[...]
        parts = []
        for c in range(ROWS // CHUNK):
            inner = slice(c * CHUNK, (c + 1) * CHUNK)
            place = slice(b * ROWS + c * CHUNK, b * ROWS + (c + 1) * CHUNK)
            carry_high, carry_low = high_low(carry)
            kept = kept_query_ref[place]
            parts.append(dot(kept, carry_high) + dot(kept, carry_low))
            keys = keys_ref[:, place]
            added = dot(keys, high[inner]) + dot(keys, low[inner])
            end = base + b * ROWS + (c + 1) * CHUNK - 1
            keep = jnp.where(distance(end, lengths, FAR) >= CHUNK, 1.0, 0.0)
            number = b * (ROWS // CHUNK) + c
            carry = (carry * keep + added) * factor_ref[number : number + 1]
        state_ref[...] = carry
        out_ref[here] = outside * (total + jnp.concatenate(parts, 0)) + rest_ref[1:2] * conv


def gate_columns(shards, pick_ref, query_ref, carried_ref, expand_ref, scan_ref, state_ref, *refs):
    blocks = refs[:shards]
    out_ref, total_ref, arrived, square_ref = refs[shards:]
    rows = pick_ref.shape[0]
    per = rows // shards
    for k in range(shards):
        arrived[k * per : (k + 1) * per] = blocks[k][...]

    @pl.when(pl.program_id(0) == 0)
    def _():
        square_ref[...] = jnp.zeros_like(square_ref)

    carry_high, carry_low = high_low(state_ref[...])
    for b in range(rows // ROWS):
        here = slice(b * ROWS, (b + 1) * ROWS)
        gate = dot(pick_ref[here], arrived[...])
        queries = query_ref[here]
        earlier = dot(queries, carry_high) + dot(queries, carry_low)
        outputs = scan_ref[here] + dot(carried_ref[here], expand_ref[...]) * earlier
        gated = outputs * silu(gate)
        out_ref[here] = gated
        squares = gated * gated
        part = squares[:, :LANES]
        for piece in range(1, TILE // LANES):
            part = part + squares[:, piece * LANES : (piece + 1) * LANES]
        square_ref[here] = square_ref[here] + part

    @pl.when(pl.program_id(0) == pl.num_programs(0) - 1)
    def _():
        for b in range(rows // ROWS):
            here = slice(b * ROWS, (b + 1) * ROWS)
            total_ref[:, here] = jnp.sum(square_ref[here].T, axis=0, keepdims=True)


def normalize(count, total_ref, gain_ref, *refs):
    pieces, out_ref = refs[:-1], refs[-1]
    scale = lax.rsqrt(total_ref[...] / count + 1e-05)
    scale = jnp.broadcast_to(scale, (LANES, scale.shape[1])).T
    first = 0
    for ref in pieces:
        for tile in range(ref.shape[1] // LANES):
            here = slice(first + tile * LANES, first + (tile + 1) * LANES)
            value = ref[:, tile * LANES : (tile + 1) * LANES] * scale * gain_ref[:, here]
            out_ref[:, here] = value.astype(bf16)
        first += ref.shape[1]


def moved(block, axis, steps):
    count = lax.axis_size(axis)
    return lax.ppermute(block, axis, [(i, (i + steps) % count) for i in range(count)])


def after(value, *others):
    return lax.optimization_barrier((value, *others))[0]


def cut(tiles, shares):
    cuts = sorted({0, *(round(tiles * share) for share in shares), tiles})
    return list(zip(cuts, cuts[1:]))


def body(xs, gate_in, bc_in, dt_in, placement, lengths, conv_x, conv_bc, a_log, dt_bias, d_skip, norm_gain):
    shards = lax.axis_size("seq")
    groups = lax.axis_size("head")
    rows, inner = xs.shape
    width = conv_x.shape[0]
    heads = a_log.shape[0]
    head_dim = inner // heads
    state = bc_in.shape[1] // 2
    per = rows // shards
    group = per + RIM
    tiles = inner // TILE
    chunks = rows // CHUNK
    parts = cut(tiles, SHARES)
    gate_parts = cut(tiles, GATE_SHARES)
    triple = jnp.stack([dt_bias, a_log, d_skip])
    lines = jnp.pad(jnp.concatenate([triple] * GROUPS, 1), ((0, 5), (0, LANES - GROUPS * heads)))

    place = placement.reshape(1, rows)
    thin = dt_in.T
    full = rows + shards * RIM
    thick = 2 * state + LANES
    first, last = parts[0]
    sent = call(
        functools.partial(send_order, shards, width),
        [shape(full, rows)] + [shape(group, thick)] * shards + [shape(group, (last - first) * TILE)] * shards,
        (place, bc_in, thin, xs),
        [whole(place), whole(bc_in), whole(thin), columns(rows)],
        [whole(shape(full, rows))] + [whole(shape(group, thick))] * shards + [columns(group)] * shards,
        grid=(last - first,),
        micros=7,
    )
    picks, small, x_send = sent[0], sent[1 : 1 + shards], [sent[1 + shards :]]
    small = [small[0]] + [moved(small[k], "seq", k) for k in range(1, shards)]
    arrived = [[x_send[0][0]] + [moved(x_send[0][k], "seq", k) for k in range(1, shards)]]

    for first, last in parts[1:]:
        x_send.append(
            call(
                functools.partial(gather_rows, shards, True),
                [shape(group, (last - first) * TILE)] * shards,
                (picks, xs),
                [whole(picks), columns(rows, start=first)],
                [columns(group)] * shards,
                grid=(last - first,),
                micros=2 * (last - first),
            )
        )
    def within(first, last):
        return pl.BlockSpec((per, TILE), lambda j: (0, jnp.clip(j - first, 0, last - first - 1)))

    gate_send = call(
        functools.partial(gather_parts, shards, gate_parts),
        [shape(per, (last - first) * TILE) for first, last in gate_parts for _ in range(shards)],
        (picks, gate_in),
        [whole(shape(rows, rows)), columns(rows)],
        [within(first, last) for first, last in gate_parts for _ in range(shards)],
        grid=(tiles,),
        micros=2 * tiles,
    )
    gate_send = [gate_send[number * shards : (number + 1) * shards] for number in range(len(gate_parts))]

    kept = [
        shape(rows, rows),
        shape(RIM, shards * RIM),
        shape(rows, LANES, dtype=jnp.int32),
        shape(rows, ROWS),
        shape(rows, ROWS),
        shape(rows, state),
        shape(rows, state),
        shape(state, rows),
        shape(rows, LANES),
        shape(rows, LANES),
        shape(rows, LANES),
        shape(LANES, inner),
        shape(chunks, inner, dtype=f32),
        shape(8, inner, dtype=f32),
    ]
    (
        pick, rims, gap, score_high, score_low, query, kept_query,
        keys, inside, outside, carried, expand, factor, rest,
    ) = call(
        functools.partial(prepare, shards, width, heads, head_dim),
        kept,
        (lengths, *small, conv_bc, lines),
        [smem()] + [whole(s) for s in small] + [whole(conv_bc), whole(lines)],
        [whole(s) for s in kept],
        scratch=[
            pltpu.VMEM((rows + HALO, 2 * state), f32),
            pltpu.VMEM((rows, LANES), f32),
            pltpu.VMEM((rows, LANES), f32),
        ],
        micros=8,
    )

    def stream(send, before, *others):
        return [send[0]] + [
            moved(after(send[k], before[k], *others), "seq", k) for k in range(1, shards)
        ]

    if len(parts) > 1:
        arrived.append(stream(x_send[1], arrived[0], rims, gate_send[0][0], x_send[-1][0]))

    scans, ends, states, gates = [], [], [], []
    for number, part in enumerate(parts):
        blocks = arrived[number]
        first, last = part
        size = (last - first) * TILE
        if ends:
            blocks = [after(blocks[0], ends[-1])] + blocks[1:]
        scanned, local_state = call(
            functools.partial(scan_columns, shards, width),
            [shape(rows, size, dtype=f32), shape(state, size, dtype=f32)],
            (
                lengths, pick, rims, gap, score_high, score_low, kept_query, keys, inside, outside,
                expand, factor, rest, conv_x, *blocks,
            ),
            [smem()]
            + [whole(a) for a in (pick, rims, gap, score_high, score_low, kept_query, keys, inside, outside)]
            + [columns(n, start=first) for n in (LANES, chunks, 8, width)]
            + [columns(group)] * shards,
            [columns(rows), columns(state)],
            grid=(last - first,),
            scratch=[pltpu.VMEM((rows, TILE), bf16), pltpu.VMEM((rows + HALO, TILE), f32)],
            micros=5 * (last - first),
        )
        scans.append(scanned)
        ends.append(local_state)
        if number + 2 < len(parts):
            arrived.append(stream(x_send[number + 2], arrived[number + 1], local_state))
        if not gates and number + 2 >= len(parts):
            gates.append(stream(gate_send[0], arrived[-1], local_state))
            for send in gate_send[1:]:
                gates.append(stream(send, gates[-1]))
        following = (arrived + gates)[number + 1]
        incoming = leaving = None
        for step in range(1, shards):
            leaving = after(local_state, following[1])
            if incoming is not None:
                leaving = leaving + rest[0:1, first * TILE : last * TILE] * incoming
            received = lax.ppermute(leaving, "seq", [(step - 1, step)])
            incoming = received if incoming is None else incoming + received
        states.append(incoming)

    outs, totals = [], []
    for tile in range(tiles):
        part = sum(tile >= last for _, last in parts)
        gate_part = sum(tile >= last for _, last in gate_parts)
        blocks = gates[gate_part]
        if gate_part + 1 < len(gates):
            blocks = [after(blocks[0], gates[gate_part + 1][1])] + blocks[1:]
        gated, total = call(
            functools.partial(gate_columns, shards),
            [shape(rows, TILE, dtype=f32), shape(1, rows, dtype=f32)],
            (pick, query, carried, expand, scans[part], states[part], *blocks),
            [whole(pick), whole(query), whole(carried), columns(LANES, start=tile)]
            + [columns(n, start=tile - parts[part][0]) for n in (rows, state)]
            + [columns(per, start=tile - gate_parts[gate_part][0])] * shards,
            [columns(rows), whole(shape(1, rows))],
            scratch=[pltpu.VMEM((rows, TILE), bf16), pltpu.VMEM((rows, LANES), f32)],
            micros=3,
        )
        outs.append(gated)
        totals.append(total)
    total = lax.psum(sum(totals), "head")
    gain = norm_gain.reshape(1, inner)
    return call(
        functools.partial(normalize, inner * groups),
        shape(rows, inner),
        (total, gain, *outs),
        [pl.BlockSpec((1, ROWS), lambda i: (0, i)), whole(gain)]
        + [pl.BlockSpec((ROWS, out.shape[1]), lambda i: (i, 0)) for out in outs],
        pl.BlockSpec((ROWS, inner), lambda i: (i, 0)),
        grid=(rows // ROWS,),
        micros=5,
    )


def solution(mesh):
    in_specs = (
        P(("parts", "seq"), "head"),
        P(("parts", "seq"), "head"),
        P(("parts", "seq"), None),
        P(("parts", "seq"), "head"),
        P(("parts", "seq")),
        P("parts"),
        P(None, "head"),
        P(),
        P("head"),
        P("head"),
        P("head"),
        P("head"),
    )
    out_specs = P(("parts", "seq"), "head")
    return jax.shard_map(body, mesh=mesh, in_specs=in_specs, out_specs=out_specs, check_vma=False)
```

time: 255 us -> 193 us (0.76)
  waiting for transfers between devices: 111 us -> 88.8 us
  Pallas kernels: 61.2 us -> 45.2 us
  between operations: 13.6 us -> 0.38 us
  other arithmetic: 12.5 us -> 0.5 us
  local copies, waits for them, and re-layouts: 5.76 us -> 8.72 us
    ppermute x12 -> x30, waiting for transfers between devices: 111 us -> 88.8 us  [the longest x21 78.1 us: moved(): lax.ppermute(block, axis, [(i, (i + steps) % count) for i in range(count)])]
    pallas_call x6 -> x14, Pallas kernels: 61.2 us -> 45.2 us  [call(): pl.pallas_call(kernel, grid=grid, in_specs=in_specs, out_specs=out_specs,...]
    convert_element_type x1 -> x0, other arithmetic: 4.49 us -> none  [body(): return result.astype(jnp.bfloat16)]
    unnamed x32 -> x34, local copies, waits for them, and re-layouts: 4.35 us -> 8.71 us
    add x4 -> x10, other arithmetic: 4.57 us -> 0.41 us  [the longest x6 0.31 us: body(): leaving = leaving + rest[0:1, first * TILE:last * TILE] * incoming]
    ppermute x12 -> x30, starting transfers between devices: 44.4 us -> 42.8 us  [the longest x21 34.7 us: moved(): lax.ppermute(block, axis, [(i, (i + steps) % count) for i in range(count)])]
  transfers between devices with their start and end apart: 13 -> 30, of which waited for: 7 -> 15; matrix products, arithmetic and copies ran while one was open for 1% -> 0% of each run, Pallas kernels for 6% -> 19%
where the time goes in v2:
time: 193 us; the launch traced here: 192 us
  waiting for transfers between devices  88.8 us (46%)
  Pallas kernels  45.2 us (23%)
  starting transfers between devices  42.8 us (22%)
  local copies, waits for them, and re-layouts  8.72 us (5%)
  blocking collectives  5.92 us (3%)
    ppermute x21, waiting for transfers between devices, moved(): lax.ppermute(block, axis, [(i, (i + steps) % count) for i in range(count)])  78.1 us
    pallas_call x14, Pallas kernels, call(): pl.pallas_call(kernel, grid=grid, in_specs=in_specs, out_specs=out_specs,...  45.2 us
    ppermute x21, starting transfers between devices, moved(): lax.ppermute(block, axis, [(i, (i + steps) % count) for i in range(count)])  34.7 us
    ppermute x9, waiting for transfers between devices, body(): received = lax.ppermute(leaving, 'seq', [(step - 1, step)])  10.7 us
    unnamed x34, local copies, waits for them, and re-layouts  8.71 us
    ppermute x9, starting transfers between devices, body(): received = lax.ppermute(leaving, 'seq', [(step - 1, step)])  8.08 us
    psum x1, blocking collectives, body(): total = lax.psum(sum(totals), 'head')  5.92 us
  transfers between devices with their start and end apart: 30, of which 15 were waited for; matrix products, arithmetic and copies ran while one was open for 0% of the time, Pallas kernels for 19%

profile of v2, /device:TPU:26, one launch (start us, length us, event | category | flops | bytes accessed | tf_op | source)
XLA Modules:
  0.0 192.3 jit_solution(15642041995790474435)
XLA Ops:
  0.0 1.7 copy-done.1
  1.7 1.0 copy-done.3
  2.8 0.8 copy-done.4
  3.5 0.7 copy-done.6
  4.2 3.8 %shard_map.118 = (bf16[1088,1024]{1,0:T(8,128)(2,1)S(1)}, bf16[272,384]{1,0:T(8,128)(2,1)S(1)}, bf16[272,384]{1,0:T(8,128)(2,1)S(1)}, bf16[272,384]{1,0:T(8,128)...) custom-call(s32[1,1024]{1,0:T(1,128)S(1)} %bitcast.9, ...), custom_call_target="tpu_custom_call" | custom-call | flops 8049999872 | tf_op jit(solution)/shard_map/pallas_call | solution.py:61
  8.0 0.3 collective-permute-start
  8.3 1.7 collective-permute-start.1
  10.0 0.4 collective-permute-start.2
  10.5 3.4 %collective-permute-start.3 = (bf16[272,512]{1,0:T(8,128)(2,1)S(1)}, bf16[272,512]{1,0:T(8,128)(2,1)S(1)}, u32[]{:S(2)}, u32[]{:S(2)}) collective-permute-start(bf16[272,512]{1,0:T(8,128)(2,1)S(1)} %get-tuple-element.105), channel_id=1, source_target_pairs={{0,4},{4,8},{8,12},{12,0},{1,5},{5,9},{9,13},{13,1},{2,6},{6,10},{... | collective-permute-start | bytes 835592 | tf_op jit(solution)/shard_map/ppermute | solution.py:389
  13.9 1.8 shard_map.121
  15.7 4.5 %shard_map.122 = (bf16[256,512]{1,0:T(8,128)(2,1)S(1)}, bf16[256,512]{1,0:T(8,128)(2,1)S(1)}, bf16[256,512]{1,0:T(8,128)(2,1)S(1)}, bf16[256,512]{1,0:T(8,128)(2...) custom-call(bf16[1088,1024]{1,0:T(8,128)(2,1)S(1)} %get-tuple-elemen, ...), custom_call_target="tpu_custom_call" | custom-call | flops 11500000256 | tf_op jit(solution)/shard_map/pallas_call | solution.py:61
  20.3 0.1 fusion.refs_5_
  20.4 0.8 shard_map.123
  21.2 4.4 %collective-permute-start.5 = (bf16[272,512]{1,0:T(8,128)(2,1)S(1)}, bf16[272,512]{1,0:T(8,128)(2,1)S(1)}, u32[]{:S(2)}, u32[]{:S(2)}) collective-permute-start(bf16[272,512]{1,0:T(8,128)(2,1)S(1)} %get-tuple-element.107), channel_id=1, source_target_pairs={{0,12},{4,0},{8,4},{12,8},{1,13},{5,1},{9,5},{13,9},{2,14},{6,2},{... | collective-permute-start | bytes 835592 | tf_op jit(solution)/shard_map/ppermute | solution.py:389
  25.6 4.8 %collective-permute-done.1.refs_2_ = bf16[272,384]{1,0:T(8,128)(2,1)S(1)} collective-permute-done((bf16[272,384]{1,0:T(8,128)(2,1)S(1)}, bf16[272,384]{1,0:T(8,128)(2,1)S(1)}, u32[]{:S(2)}, u32[]{:S(2)}) %collective-permute-start.1) | collective-permute-done | bytes 208928 | tf_op jit(solution)/shard_map/ppermute | solution.py:389
  30.4 5.3 %shard_map.119 = (bf16[1024,1024]{1,0:T(8,128)(2,1)S(1)}, bf16[16,64]{1,0:T(8,128)(2,1)S(1)}, s32[1024,128]{1,0:T(8,128)S(1)}, bf16[1024,256]{1,0:T(8,128)(2,1)S...) custom-call(s32[3]{0:T(128)S(1)} %copy-done.8, ...), custom_call_target="tpu_custom_call" | custom-call | flops 9200000000 | tf_op jit(solution)/shard_map/pallas_call | solution.py:61
  35.7 6.1 %collective-permute-done.5.refs_3_ = bf16[272,512]{1,0:T(8,128)(2,1)S(1)} collective-permute-done((bf16[272,512]{1,0:T(8,128)(2,1)S(1)}, bf16[272,512]{1,0:T(8,128)(2,1)S(1)}, u32[]{:S(2)}, u32[]{:S(2)}) %collective-permute-start.5) | collective-permute-done | bytes 278560 | tf_op jit(solution)/shard_map/ppermute | solution.py:389
  41.8 10.4 %collective-permute-done.4.refs_2_ = bf16[272,512]{1,0:T(8,128)(2,1)S(1)} collective-permute-done((bf16[272,512]{1,0:T(8,128)(2,1)S(1)}, bf16[272,512]{1,0:T(8,128)(2,1)S(1)}, u32[]{:S(2)}, u32[]{:S(2)}) %collective-permute-start.4) | collective-permute-done | bytes 278560 | tf_op jit(solution)/shard_map/ppermute | solution.py:389
  52.2 1.4 collective-permute-start.11
  53.6 2.0 %collective-permute-start.12 = (bf16[272,512]{1,0:T(8,128)(2,1)S(1)}, bf16[272,512]{1,0:T(8,128)(2,1)S(1)}, u32[]{:S(2)}, u32[]{:S(2)}) collective-permute-start(bf16[272,512]{1,0:T(8,128)(2,1)S(1)} %get-tuple-element.125), channel_id=1, source_target_pairs={{0,12},{4,0},{8,4},{12,8},{1,13},{5,1},{9,5},{13,9},{2,14},{6,2},{... | collective-permute-start | bytes 835592 | tf_op jit(solution)/shard_map/ppermute | solution.py:389
  55.6 8.1 %shard_map.120 = (f32[1024,512]{1,0:T(8,128)S(1)}, f32[128,512]{1,0:T(8,128)S(1)}) custom-call(s32[3]{0:T(128)S(1)} %copy-done.8, bf16[1024,1024]{1,0:T(8,128)(2,1)S(1)} %get-tuple-element.90.pick_ref, bf16[16,64]{1,0:T(8,128)(2,1)S(1)} %get-tuple-element.94.rims_ref, s32[1024,128]{1,0:T(8,128)S(1)} %get-tuple-element.95.gap_ref, ...), custom_call_target="tpu_custom_call" | custom-call | flops 11500000256 | tf_op jit(solution)/shard_map/pallas_call | solution.py:61
  63.7 9.9 %collective-permute-done.12.refs_3_ = bf16[272,512]{1,0:T(8,128)(2,1)S(1)} collective-permute-done((bf16[272,512]{1,0:T(8,128)(2,1)S(1)}, bf16[272,512]{1,0:T(8,128)(2,1)S(1)}, u32[]{:S(2)}, u32[]{:S(2)}) %collective-permute-start.12) | collective-permute-done | bytes 278560 | tf_op jit(solution)/shard_map/ppermute | solution.py:389
  73.6 4.7 %collective-permute-done.11.refs_2_ = bf16[272,512]{1,0:T(8,128)(2,1)S(1)} collective-permute-done((bf16[272,512]{1,0:T(8,128)(2,1)S(1)}, bf16[272,512]{1,0:T(8,128)(2,1)S(1)}, u32[]{:S(2)}, u32[]{:S(2)}) %collective-permute-start.11) | collective-permute-done | bytes 278560 | tf_op jit(solution)/shard_map/ppermute | solution.py:389
  78.3 0.6 collective-permute-start.15
  79.0 2.0 %collective-permute-start.17 = (bf16[272,256]{1,0:T(8,128)(2,1)S(1)}, bf16[272,256]{1,0:T(8,128)(2,1)S(1)}, u32[]{:S(2)}, u32[]{:S(2)}) collective-permute-start(bf16[272,256]{1,0:T(8,128)(2,1)S(1)} %get-tuple-element.136), channel_id=1, source_target_pairs={{0,12},{4,0},{8,4},{12,8},{1,13},{5,1},{9,5},{13,9},{2,14},{6,2},{... | collective-permute-start | bytes 417800 | tf_op jit(solution)/shard_map/ppermute | solution.py:389
  80.9 0.7 collective-permute-start.7
  81.6 8.1 %shard_map.124 = (f32[1024,512]{1,0:T(8,128)S(1)}, f32[128,512]{1,0:T(8,128)S(1)}) custom-call(s32[3]{0:T(128)S(1)} %copy-done.8, bf16[1024,1024]{1,0:T(8,128)(2,1)S(1)} %get-tuple-element.90.pick_ref, bf16[16,64]{1,0:T(8,128)(2,1)S(1)} %get-tuple-element.94.rims_ref, s32[1024,128]{1,0:T(8,128)S(1)} %get-tuple-element.95.gap_ref, ...), custom_call_target="tpu_custom_call" | custom-call | flops 11500000256 | tf_op jit(solution)/shard_map/pallas_call | solution.py:61
  89.7 1.1 collective-permute-done.17.refs_3_
  90.9 0.8 collective-permute-done.15.refs_2_
  91.7 3.2 %collective-permute-start.13 = (bf16[256,512]{1,0:T(8,128)(2,1)S(1)}, bf16[256,512]{1,0:T(8,128)(2,1)S(1)}, u32[]{:S(2)}, u32[]{:S(2)}) collective-permute-start(bf16[256,512]{1,0:T(8,128)(2,1)S(1)} %get-tuple-element.127), channel_id=1, source_target_pairs={{0,4},{4,8},{8,12},{12,0},{1,5},{5,9},{9,13},{13,1},{2,6},{6,10},{... | collective-permute-start | bytes 786440 | tf_op jit(solution)/shard_map/ppermute | solution.py:389
  94.9 0.7 collective-permute-start.18
  95.5 0.7 collective-permute-start.19
  96.2 4.2 %shard_map.129 = (f32[1024,256]{1,0:T(8,128)S(1)}, f32[128,256]{1,0:T(8,128)S(1)}) custom-call(s32[3]{0:T(128)S(1)} %copy-done.8, bf16[1024,1024]{1,0:T(8,128)(2,1)S(1)} %get-tuple-element.90.pick_ref, bf16[16,64]{1,0:T(8,128)(2,1)S(1)} %get-tuple-element.94.rims_ref, s32[1024,128]{1,0:T(8,128)S(1)} %get-tuple-element.95.gap_ref, ...), custom_call_target="tpu_custom_call" | custom-call | flops 5750000128 | tf_op jit(solution)/shard_map/pallas_call | solution.py:61
  100.5 0.7 collective-permute-start.8
  101.1 0.5 collective-permute-done.13.refs_1_
  101.7 0.7 collective-permute-start.25
  102.3 15.1 %collective-permute-done.16.refs_2_ = bf16[256,512]{1,0:T(8,128)(2,1)S(1)} collective-permute-done((bf16[256,512]{1,0:T(8,128)(2,1)S(1)}, bf16[256,512]{1,0:T(8,128)(2,1)S(1)}, u32[]{:S(2)}, u32[]{:S(2)}) %collective-permute-start.16) | collective-permute-done | bytes 262176 | tf_op jit(solution)/shard_map/ppermute | solution.py:389
  117.5 1.8 collective-permute-start.23
  119.3 0.3 collective-permute-start.24
  119.6 0.7 collective-permute-start.20
  120.3 0.7 collective-permute-start.26
  121.0 0.1 multiply_add_fusion.2
  121.1 1.3 collective-permute-start.9
  122.5 2.1 %collective-permute-done.14.refs_1_ = bf16[256,512]{1,0:T(8,128)(2,1)S(1)} collective-permute-done((bf16[256,512]{1,0:T(8,128)(2,1)S(1)}, bf16[256,512]{1,0:T(8,128)(2,1)S(1)}, u32[]{:S(2)}, u32[]{:S(2)}) %collective-permute-start.14) | collective-permute-done | bytes 262176 | tf_op jit(solution)/shard_map/ppermute | solution.py:389
  124.6 1.3 collective-permute-start.27
  125.8 19.7 %collective-permute-done.23.refs_2_ = bf16[256,512]{1,0:T(8,128)(2,1)S(1)} collective-permute-done((bf16[256,512]{1,0:T(8,128)(2,1)S(1)}, bf16[256,512]{1,0:T(8,128)(2,1)S(1)}, u32[]{:S(2)}, u32[]{:S(2)}) %collective-permute-start.23) | collective-permute-done | bytes 262176 | tf_op jit(solution)/shard_map/ppermute | solution.py:389
  145.6 12.6 %collective-permute-start.28 = (bf16[256,256]{1,0:T(8,128)(2,1)S(1)}, bf16[256,256]{1,0:T(8,128)(2,1)S(1)}, u32[]{:S(2)}, u32[]{:S(2)}) collective-permute-start(bf16[256,256]{1,0:T(8,128)(2,1)S(1)} %get-tuple-element.158), channel_id=1, source_target_pairs={{0,8},{4,12},{8,0},{12,4},{1,9},{5,13},{9,1},{13,5},{2,10},{6,14},... | collective-permute-start | bytes 393224 | tf_op jit(solution)/shard_map/ppermute | solution.py:389
  158.1 0.1 multiply_add_fusion
  158.2 7.0 %collective-permute-done.9 = f32[128,512]{1,0:T(8,128)S(1)} collective-permute-done((f32[128,512]{1,0:T(8,128)S(1)}, f32[128,512]{1,0:T(8,128)S(1)}, u32[]{:S(2)}, u32[]{:S(2)}) %collective-permute-start.9) | collective-permute-done | bytes 262176 | tf_op jit(solution)/shard_map/ppermute | solution.py:540
  165.2 1.5 collective-permute-start.21
  166.7 1.2 shard_map.126
  168.0 1.2 shard_map.125
  169.2 1.6 collective-permute-done.27
  170.8 2.8 %collective-permute-done.22.refs_1_ = bf16[256,256]{1,0:T(8,128)(2,1)S(1)} collective-permute-done((bf16[256,256]{1,0:T(8,128)(2,1)S(1)}, bf16[256,256]{1,0:T(8,128)(2,1)S(1)}, u32[]{:S(2)}, u32[]{:S(2)}) %collective-permute-start.22) | collective-permute-done | bytes 131104 | tf_op jit(solution)/shard_map/ppermute | solution.py:389
  173.6 1.3 shard_map.130
  174.9 1.0 copy-done.11
  175.9 2.1 %collective-permute-done.21 = f32[128,512]{1,0:T(8,128)S(1)} collective-permute-done((f32[128,512]{1,0:T(8,128)S(1)}, f32[128,512]{1,0:T(8,128)S(1)}, u32[]{:S(2)}, u32[]{:S(2)}) %collective-permute-start.21) | collective-permute-done | bytes 262176 | tf_op jit(solution)/shard_map/ppermute | solution.py:540
  178.0 1.2 shard_map.128
  179.3 1.2 shard_map.127
  180.5 1.0 copy-done.9
  181.5 5.9 %psum.7.total_ref = f32[1,1024]{1,0:T(1,128)S(1)} all-reduce(f32[1,1024]{1,0:T(1,128)S(1)} %add_add_fusion), channel_id=1, replica_groups=mesh['parts'=2,'seq'=4,'head'=4] {'head'}, use_global_device_ids=true, to_apply=%region_0.1 | all-reduce | flops 1024 | bytes 8192 | tf_op jit(solution)/shard_map/psum | solution.py:564
  187.4 1.2 copy-done.10
  188.6 1.2 copy-done.12
  189.9 2.4 %shard_map.131 = bf16[1024,1280]{1,0:T(8,128)(2,1)} custom-call(f32[1,1024]{1,0:T(1,128)S(1)} %psum.7.total_ref, f32[1,1280]{1,0:T(1,128)S(1)} %reshape.7.gain_ref, f32[1024,256]{1,0:T(8,128)S(1)} %get-tuple-element.162.refs_0_, f32[1024,256]{1,0:T(8,128)S(1)} %get-tuple-element.163.refs_1_, f32[1024,256]{1,0:T(8,128)S(1)} %copy-done.10, ...), custom_call_target="tpu_custom_call" | custom-call | flops 5750000128 | tf_op jit(solution)/shard_map/pallas_call | solution.py:61
  (59 shorter events, 0.4 us)
Async XLA Ops:
  0.0 1.7 copy-start.1
  1.7 1.0 copy-start.3
  2.8 0.8 copy-start.4
  3.5 0.7 copy-start.6
  4.2 9.6 %copy-start.13 = (f32[1280]{0:T(1024)S(1)}, f32[1280]{0:T(1024)}, u32[]{:S(2)}) copy-start(f32[1280]{0:T(1024)} %param.23) | copy-start | bytes 15364
  4.2 9.6 %copy-start.2 = (bf16[1024,1280]{1,0:T(8,128)(2,1)S(1)}, bf16[1024,1280]{1,0:T(8,128)(2,1)}, u32[]{:S(2)}) copy-start(bf16[1024,1280]{1,0:T(8,128)(2,1)} %x_ref.7) | copy-start | bytes 7864324
  8.0 13.1 %collective-permute-start = (bf16[272,384]{1,0:T(8,128)(2,1)S(1)}, bf16[272,384]{1,0:T(8,128)(2,1)S(1)}, u32[]{:S(2)}, u32[]{:S(2)}) collective-permute-start(bf16[272,384]{1,0:T(8,128)(2,1)S(1)} %get-tuple-element.87), channel_id=1, source_target_pairs={{0,4},{4,8},{8,12},{12,0},{1,5},{5,9},{9,13},{13,1},{2,6},{6,10},{... | collective-permute-start | bytes 626696 | tf_op jit(solution)/shard_map/ppermute | solution.py:389
  8.3 22.1 %collective-permute-start.1 = (bf16[272,384]{1,0:T(8,128)(2,1)S(1)}, bf16[272,384]{1,0:T(8,128)(2,1)S(1)}, u32[]{:S(2)}, u32[]{:S(2)}) collective-permute-start(bf16[272,384]{1,0:T(8,128)(2,1)S(1)} %get-tuple-element.88), channel_id=1, source_target_pairs={{0,8},{4,12},{8,0},{12,4},{1,9},{5,13},{9,1},{13,5},{2,10},{6,14},... | collective-permute-start | bytes 626696 | tf_op jit(solution)/shard_map/ppermute | solution.py:389
  10.0 20.4 %collective-permute-start.2 = (bf16[272,384]{1,0:T(8,128)(2,1)S(1)}, bf16[272,384]{1,0:T(8,128)(2,1)S(1)}, u32[]{:S(2)}, u32[]{:S(2)}) collective-permute-start(bf16[272,384]{1,0:T(8,128)(2,1)S(1)} %get-tuple-element.89), channel_id=1, source_target_pairs={{0,12},{4,0},{8,4},{12,8},{1,13},{5,1},{9,5},{13,9},{2,14},{6,2},{... | collective-permute-start | bytes 626696 | tf_op jit(solution)/shard_map/ppermute | solution.py:389
  10.5 41.8 %collective-permute-start.3 = (bf16[272,512]{1,0:T(8,128)(2,1)S(1)}, bf16[272,512]{1,0:T(8,128)(2,1)S(1)}, u32[]{:S(2)}, u32[]{:S(2)}) collective-permute-start(bf16[272,512]{1,0:T(8,128)(2,1)S(1)} %get-tuple-element.105), channel_id=1, source_target_pairs={{0,4},{4,8},{8,12},{12,0},{1,5},{5,9},{9,13},{13,1},{2,6},{6,10},{... | collective-permute-start | bytes 835592 | tf_op jit(solution)/shard_map/ppermute | solution.py:389
  13.8 38.4 %collective-permute-start.4 = (bf16[272,512]{1,0:T(8,128)(2,1)S(1)}, bf16[272,512]{1,0:T(8,128)(2,1)S(1)}, u32[]{:S(2)}, u32[]{:S(2)}) collective-permute-start(bf16[272,512]{1,0:T(8,128)(2,1)S(1)} %get-tuple-element.106), channel_id=1, source_target_pairs={{0,8},{4,12},{8,0},{12,4},{1,9},{5,13},{9,1},{13,5},{2,10},{6,14},... | collective-permute-start | bytes 835592 | tf_op jit(solution)/shard_map/ppermute | solution.py:389
  13.9 1.8 copy-start
  15.7 4.6 %copy-start.14 = (f32[16]{0:T(128)S(1)}, f32[16]{0:T(128)}, u32[]{:S(2)}) copy-start(f32[16]{0:T(128)} %param.22) | copy-start | bytes 196
  15.7 4.6 %copy-start.15 = (f32[16]{0:T(128)S(1)}, f32[16]{0:T(128)}, u32[]{:S(2)}) copy-start(f32[16]{0:T(128)} %param.20) | copy-start | bytes 196
  15.7 4.6 %copy-start.16 = (f32[16]{0:T(128)S(1)}, f32[16]{0:T(128)}, u32[]{:S(2)}) copy-start(f32[16]{0:T(128)} %param.21) | copy-start | bytes 196
  20.3 10.0 %copy-start.7 = (f32[4,256]{1,0:T(4,128)S(1)}, f32[4,256]{1,0:T(4,128)}, u32[]{:S(2)}) copy-start(f32[4,256]{1,0:T(4,128)} %refs_4_.1) | copy-start | bytes 12292
  20.3 10.0 %copy-start.8 = (s32[3]{0:T(128)S(1)}, s32[3]{0:T(128)}, u32[]{:S(2)}) copy-start(s32[3]{0:T(128)} %lengths.7) | copy-start | bytes 40
  21.2 20.7 %collective-permute-start.5 = (bf16[272,512]{1,0:T(8,128)(2,1)S(1)}, bf16[272,512]{1,0:T(8,128)(2,1)S(1)}, u32[]{:S(2)}, u32[]{:S(2)}) collective-permute-start(bf16[272,512]{1,0:T(8,128)(2,1)S(1)} %get-tuple-element.107), channel_id=1, source_target_pairs={{0,12},{4,0},{8,4},{12,8},{1,13},{5,1},{9,5},{13,9},{2,14},{6,2},{... | collective-permute-start | bytes 835592 | tf_op jit(solution)/shard_map/ppermute | solution.py:389
  30.4 25.2 %copy-start.5 = (f32[4,1280]{1,0:T(4,128)S(1)}, f32[4,1280]{1,0:T(4,128)}, u32[]{:S(2)}) copy-start(f32[4,1280]{1,0:T(4,128)} %taps_ref.5) | copy-start | bytes 61444
  52.2 26.1 %collective-permute-start.6 = (bf16[272,512]{1,0:T(8,128)(2,1)S(1)}, bf16[272,512]{1,0:T(8,128)(2,1)S(1)}, u32[]{:S(2)}, u32[]{:S(2)}) collective-permute-start(bf16[272,512]{1,0:T(8,128)(2,1)S(1)} %get-tuple-element.114), channel_id=1, source_target_pairs={{0,4},{4,8},{8,12},{12,0},{1,5},{5,9},{9,13},{13,1},{2,6},{6,10},{... | collective-permute-start | bytes 835592 | tf_op jit(solution)/shard_map/ppermute | solution.py:389
  52.2 26.1 %collective-permute-start.11 = (bf16[272,512]{1,0:T(8,128)(2,1)S(1)}, bf16[272,512]{1,0:T(8,128)(2,1)S(1)}, u32[]{:S(2)}, u32[]{:S(2)}) collective-permute-start(bf16[272,512]{1,0:T(8,128)(2,1)S(1)} %get-tuple-element.123), channel_id=1, source_target_pairs={{0,8},{4,12},{8,0},{12,4},{1,9},{5,13},{9,1},{13,5},{2,10},{6,14},... | collective-permute-start | bytes 835592 | tf_op jit(solution)/shard_map/ppermute | solution.py:389
  53.6 20.0 %collective-permute-start.12 = (bf16[272,512]{1,0:T(8,128)(2,1)S(1)}, bf16[272,512]{1,0:T(8,128)(2,1)S(1)}, u32[]{:S(2)}, u32[]{:S(2)}) collective-permute-start(bf16[272,512]{1,0:T(8,128)(2,1)S(1)} %get-tuple-element.125), channel_id=1, source_target_pairs={{0,12},{4,0},{8,4},{12,8},{1,13},{5,1},{9,5},{13,9},{2,14},{6,2},{... | collective-permute-start | bytes 835592 | tf_op jit(solution)/shard_map/ppermute | solution.py:389
  78.3 11.4 %collective-permute-start.10 = (bf16[272,256]{1,0:T(8,128)(2,1)S(1)}, bf16[272,256]{1,0:T(8,128)(2,1)S(1)}, u32[]{:S(2)}, u32[]{:S(2)}) collective-permute-start(bf16[272,256]{1,0:T(8,128)(2,1)S(1)} %get-tuple-element.119), channel_id=1, source_target_pairs={{0,4},{4,8},{8,12},{12,0},{1,5},{5,9},{9,13},{13,1},{2,6},{6,10},{... | collective-permute-start | bytes 417800 | tf_op jit(solution)/shard_map/ppermute | solution.py:389
  78.3 13.4 %collective-permute-start.15 = (bf16[272,256]{1,0:T(8,128)(2,1)S(1)}, bf16[272,256]{1,0:T(8,128)(2,1)S(1)}, u32[]{:S(2)}, u32[]{:S(2)}) collective-permute-start(bf16[272,256]{1,0:T(8,128)(2,1)S(1)} %get-tuple-element.132), channel_id=1, source_target_pairs={{0,8},{4,12},{8,0},{12,4},{1,9},{5,13},{9,1},{13,5},{2,10},{6,14},... | collective-permute-start | bytes 417800 | tf_op jit(solution)/shard_map/ppermute | solution.py:389
  79.0 11.9 %collective-permute-start.17 = (bf16[272,256]{1,0:T(8,128)(2,1)S(1)}, bf16[272,256]{1,0:T(8,128)(2,1)S(1)}, u32[]{:S(2)}, u32[]{:S(2)}) collective-permute-start(bf16[272,256]{1,0:T(8,128)(2,1)S(1)} %get-tuple-element.136), channel_id=1, source_target_pairs={{0,12},{4,0},{8,4},{12,8},{1,13},{5,1},{9,5},{13,9},{2,14},{6,2},{... | collective-permute-start | bytes 417800 | tf_op jit(solution)/shard_map/ppermute | solution.py:389
  80.9 19.5 %collective-permute-start.7 = (f32[128,512]{1,0:T(8,128)S(1)}, f32[128,512]{1,0:T(8,128)S(1)}, u32[]{:S(2)}, u32[]{:S(2)}) collective-permute-start(f32[128,512]{1,0:T(8,128)S(1)} %get-tuple-element.115), channel_id=1, source_target_pairs={{0,4},{1,5},{2,6},{3,7},{16,20},{17,21},{18,22},{19,23}} | collective-permute-start | bytes 786440 | tf_op jit(solution)/shard_map/ppermute | solution.py:540
  91.7 10.0 %collective-permute-start.13 = (bf16[256,512]{1,0:T(8,128)(2,1)S(1)}, bf16[256,512]{1,0:T(8,128)(2,1)S(1)}, u32[]{:S(2)}, u32[]{:S(2)}) collective-permute-start(bf16[256,512]{1,0:T(8,128)(2,1)S(1)} %get-tuple-element.127), channel_id=1, source_target_pairs={{0,4},{4,8},{8,12},{12,0},{1,5},{5,9},{9,13},{13,1},{2,6},{6,10},{... | collective-permute-start | bytes 786440 | tf_op jit(solution)/shard_map/ppermute | solution.py:389
  94.9 22.6 %collective-permute-start.16 = (bf16[256,512]{1,0:T(8,128)(2,1)S(1)}, bf16[256,512]{1,0:T(8,128)(2,1)S(1)}, u32[]{:S(2)}, u32[]{:S(2)}) collective-permute-start(bf16[256,512]{1,0:T(8,128)(2,1)S(1)} %get-tuple-element.133), channel_id=1, source_target_pairs={{0,8},{4,12},{8,0},{12,4},{1,9},{5,13},{9,1},{13,5},{2,10},{6,14},... | collective-permute-start | bytes 786440 | tf_op jit(solution)/shard_map/ppermute | solution.py:389
  94.9 22.6 %collective-permute-start.18 = (bf16[256,512]{1,0:T(8,128)(2,1)S(1)}, bf16[256,512]{1,0:T(8,128)(2,1)S(1)}, u32[]{:S(2)}, u32[]{:S(2)}) collective-permute-start(bf16[256,512]{1,0:T(8,128)(2,1)S(1)} %get-tuple-element.137), channel_id=1, source_target_pairs={{0,12},{4,0},{8,4},{12,8},{1,13},{5,1},{9,5},{13,9},{2,14},{6,2},{... | collective-permute-start | bytes 786440 | tf_op jit(solution)/shard_map/ppermute | solution.py:389
  95.5 23.7 %collective-permute-start.19 = (f32[128,512]{1,0:T(8,128)S(1)}, f32[128,512]{1,0:T(8,128)S(1)}, u32[]{:S(2)}, u32[]{:S(2)}) collective-permute-start(f32[128,512]{1,0:T(8,128)S(1)} %get-tuple-element.141), channel_id=1, source_target_pairs={{0,4},{1,5},{2,6},{3,7},{16,20},{17,21},{18,22},{19,23}} | collective-permute-start | bytes 786440 | tf_op jit(solution)/shard_map/ppermute | solution.py:540
  100.5 19.9 %collective-permute-start.8 = (f32[128,512]{1,0:T(8,128)S(1)}, f32[128,512]{1,0:T(8,128)S(1)}, u32[]{:S(2)}, u32[]{:S(2)}) collective-permute-start(f32[128,512]{1,0:T(8,128)S(1)} %multiply_add_fusion.3), channel_id=1, source_target_pairs={{4,8},{5,9},{6,10},{7,11},{20,24},{21,25},{22,26},{23,27}} | collective-permute-start | bytes 786440 | tf_op jit(solution)/shard_map/ppermute | solution.py:540
  101.7 17.9 %collective-permute-start.25 = (f32[128,256]{1,0:T(8,128)S(1)}, f32[128,256]{1,0:T(8,128)S(1)}, u32[]{:S(2)}, u32[]{:S(2)}) collective-permute-start(f32[128,256]{1,0:T(8,128)S(1)} %get-tuple-element.155), channel_id=1, source_target_pairs={{0,4},{1,5},{2,6},{3,7},{16,20},{17,21},{18,22},{19,23}} | collective-permute-start | bytes 393224 | tf_op jit(solution)/shard_map/ppermute | solution.py:540
  117.5 7.1 %collective-permute-start.14 = (bf16[256,512]{1,0:T(8,128)(2,1)S(1)}, bf16[256,512]{1,0:T(8,128)(2,1)S(1)}, u32[]{:S(2)}, u32[]{:S(2)}) collective-permute-start(bf16[256,512]{1,0:T(8,128)(2,1)S(1)} %get-tuple-element.128), channel_id=1, source_target_pairs={{0,4},{4,8},{8,12},{12,0},{1,5},{5,9},{9,13},{13,1},{2,6},{6,10},{... | collective-permute-start | bytes 786440 | tf_op jit(solution)/shard_map/ppermute | solution.py:389
  117.5 28.1 %collective-permute-start.23 = (bf16[256,512]{1,0:T(8,128)(2,1)S(1)}, bf16[256,512]{1,0:T(8,128)(2,1)S(1)}, u32[]{:S(2)}, u32[]{:S(2)}) collective-permute-start(bf16[256,512]{1,0:T(8,128)(2,1)S(1)} %get-tuple-element.147), channel_id=1, source_target_pairs={{0,8},{4,12},{8,0},{12,4},{1,9},{5,13},{9,1},{13,5},{2,10},{6,14},... | collective-permute-start | bytes 786440 | tf_op jit(solution)/shard_map/ppermute | solution.py:389
  119.3 26.3 %collective-permute-start.24 = (bf16[256,512]{1,0:T(8,128)(2,1)S(1)}, bf16[256,512]{1,0:T(8,128)(2,1)S(1)}, u32[]{:S(2)}, u32[]{:S(2)}) collective-permute-start(bf16[256,512]{1,0:T(8,128)(2,1)S(1)} %get-tuple-element.149), channel_id=1, source_target_pairs={{0,12},{4,0},{8,4},{12,8},{1,13},{5,1},{9,5},{13,9},{2,14},{6,2},{... | collective-permute-start | bytes 786440 | tf_op jit(solution)/shard_map/ppermute | solution.py:389
  119.6 38.5 %collective-permute-start.20 = (f32[128,512]{1,0:T(8,128)S(1)}, f32[128,512]{1,0:T(8,128)S(1)}, u32[]{:S(2)}, u32[]{:S(2)}) collective-permute-start(f32[128,512]{1,0:T(8,128)S(1)} %multiply_add_fusion.1), channel_id=1, source_target_pairs={{4,8},{5,9},{6,10},{7,11},{20,24},{21,25},{22,26},{23,27}} | collective-permute-start | bytes 786440 | tf_op jit(solution)/shard_map/ppermute | solution.py:540
  120.3 0.8 collective-permute-start.26
  121.1 44.1 %collective-permute-start.9 = (f32[128,512]{1,0:T(8,128)S(1)}, f32[128,512]{1,0:T(8,128)S(1)}, u32[]{:S(2)}, u32[]{:S(2)}) collective-permute-start(f32[128,512]{1,0:T(8,128)S(1)} %get-tuple-element.167), channel_id=1, source_target_pairs={{8,12},{9,13},{10,14},{11,15},{24,28},{25,29},{26,30},{27,31}} | collective-permute-start | bytes 786440 | tf_op jit(solution)/shard_map/ppermute | solution.py:540
  124.6 46.2 %collective-permute-start.27 = (f32[128,256]{1,0:T(8,128)S(1)}, f32[128,256]{1,0:T(8,128)S(1)}, u32[]{:S(2)}, u32[]{:S(2)}) collective-permute-start(f32[128,256]{1,0:T(8,128)S(1)} %get-tuple-element.171), channel_id=1, source_target_pairs={{8,12},{9,13},{10,14},{11,15},{24,28},{25,29},{26,30},{27,31}} | collective-permute-start | bytes 393224 | tf_op jit(solution)/shard_map/ppermute | solution.py:540
  145.6 28.1 %collective-permute-start.22 = (bf16[256,256]{1,0:T(8,128)(2,1)S(1)}, bf16[256,256]{1,0:T(8,128)(2,1)S(1)}, u32[]{:S(2)}, u32[]{:S(2)}) collective-permute-start(bf16[256,256]{1,0:T(8,128)(2,1)S(1)} %get-tuple-element.144), channel_id=1, source_target_pairs={{0,4},{4,8},{8,12},{12,0},{1,5},{5,9},{9,13},{13,1},{2,6},{6,10},{... | collective-permute-start | bytes 393224 | tf_op jit(solution)/shard_map/ppermute | solution.py:389
  145.6 28.0 %collective-permute-start.28 = (bf16[256,256]{1,0:T(8,128)(2,1)S(1)}, bf16[256,256]{1,0:T(8,128)(2,1)S(1)}, u32[]{:S(2)}, u32[]{:S(2)}) collective-permute-start(bf16[256,256]{1,0:T(8,128)(2,1)S(1)} %get-tuple-element.158), channel_id=1, source_target_pairs={{0,8},{4,12},{8,0},{12,4},{1,9},{5,13},{9,1},{13,5},{2,10},{6,14},... | collective-permute-start | bytes 393224 | tf_op jit(solution)/shard_map/ppermute | solution.py:389
  158.1 15.5 %collective-permute-start.29 = (bf16[256,256]{1,0:T(8,128)(2,1)S(1)}, bf16[256,256]{1,0:T(8,128)(2,1)S(1)}, u32[]{:S(2)}, u32[]{:S(2)}) collective-permute-start(bf16[256,256]{1,0:T(8,128)(2,1)S(1)} %get-tuple-element.160), channel_id=1, source_target_pairs={{0,12},{4,0},{8,4},{12,8},{1,13},{5,1},{9,5},{13,9},{2,14},{6,2},{... | collective-permute-start | bytes 393224 | tf_op jit(solution)/shard_map/ppermute | solution.py:389
  165.2 12.8 %collective-permute-start.21 = (f32[128,512]{1,0:T(8,128)S(1)}, f32[128,512]{1,0:T(8,128)S(1)}, u32[]{:S(2)}, u32[]{:S(2)}) collective-permute-start(f32[128,512]{1,0:T(8,128)S(1)} %get-tuple-element.169), channel_id=1, source_target_pairs={{8,12},{9,13},{10,14},{11,15},{24,28},{25,29},{26,30},{27,31}} | collective-permute-start | bytes 786440 | tf_op jit(solution)/shard_map/ppermute | solution.py:540
  174.9 1.0 copy-start.11
  180.5 1.0 copy-start.9
  187.4 1.2 copy-start.10
  188.6 1.2 copy-start.12

commit v3 on v2

--- a/solution.py
+++ b/solution.py
@@ -13,7 +13,7 @@
 LANES = 128
 RIM = 16
 SHARES = (0.4, 0.8)
-GATE_SHARES = (0.4, 0.8)
+GATE_SHARES = (0.6,)
 HALO = 8
 GROUPS = 3
 FAR = 1 << 28
@@ -87,12 +87,12 @@
     return jax.ShapeDtypeStruct(dims, dtype)
 
 
-def send_order(shards, width, place_ref, bc_ref, dt_ref, x_ref, pick_ref, *refs):
+def send_order(shards, width, quarter, place_ref, bc_ref, dt_ref, x_ref, pick_ref, *refs):
     small_refs, x_refs = refs[:shards], refs[shards:]
     rows = place_ref.shape[1]
     per = rows // shards
     heads = dt_ref.shape[0]
-    wide = bc_ref.shape[1]
+    both = bc_ref.shape[1]
 
     @pl.when(pl.program_id(0) == 0)
     def _():
@@ -116,9 +116,13 @@
         local = jnp.sum(jnp.where(mine, (place - first + 1).astype(f32), 0.0), axis=0, keepdims=True)
         high = jnp.floor(local * (1.0 / 64.0))
         low = local - 64.0 * high
-        line = iota((LANES - heads, rows), 0)
+        line = iota((LANES - quarter - heads, rows), 0)
         digits = jnp.where(line == 0, high, jnp.where(line == 1, low, 0.0)).astype(bf16)
-        thin = jnp.concatenate([dt_ref[...], digits], 0)
+        thin = jnp.concatenate([jnp.zeros((quarter, rows), bf16), dt_ref[...], digits], 0)
+        own = lax.axis_index("head") * quarter
+        lane = iota((both, LANES), 1)
+        taken = ones_where((iota((both, LANES), 0) == lane + own) & (lane < quarter))
+        thick = dot(bc_ref[...], taken).astype(bf16)
         for k in range(shards):
             pick = ones_where(iota((per, rows), 0) + k * per == target)
             pick_ref[k * per : (k + 1) * per] = pick
@@ -126,10 +130,8 @@
             row = iota((RIM, rows), 0)
             rim = ones_where((row < width - 1) & (place == row + (dest * rows - (width - 1))))
             pick_ref[rows + k * RIM : rows + (k + 1) * RIM] = rim
-            small_refs[k][:per, :wide] = dot(pick, bc_ref[...]).astype(bf16)
-            small_refs[k][per:, :wide] = dot(rim, bc_ref[...]).astype(bf16)
-            small_refs[k][:per, wide:] = dot_nt(pick, thin).astype(bf16)
-            small_refs[k][per:, wide:] = dot_nt(rim, thin).astype(bf16)
+            small_refs[k][:per] = (dot(pick, thick) + dot_nt(pick, thin)).astype(bf16)
+            small_refs[k][per:] = (dot(rim, thick) + dot_nt(rim, thin)).astype(bf16)
 
     gather_rows(shards, True, pick_ref, x_ref, *x_refs)
 
@@ -175,34 +177,53 @@
 
 
 def prepare(
-    shards, width, heads, head_dim, lengths, *refs
+    shards, groups, width, heads, head_dim, lengths, first_ref, taps_ref, lines_ref, *refs
 ):
-    own_refs = refs[:shards]
     (
-        taps_ref, lines_ref,
         pick_ref, rims_ref, gap_ref, score_high_ref, score_low_ref, query_ref, kept_query_ref,
         keys_ref, inside_ref, outside_ref, carried_ref, expand_ref, factor_ref, rest_ref,
         packed, log_sums, steps,
-    ) = refs[shards:]
+    ) = refs[-17:]
+    others = refs[:-17]
     rows = pick_ref.shape[0]
     per = rows // shards
+    group = per + RIM
     state = query_ref.shape[1]
     base = lax.axis_index("seq") * rows
-    own_main = jnp.concatenate([ref[:per] for ref in own_refs], 0)
-    own_rim = jnp.concatenate([ref[per:] for ref in own_refs], 0)
+    sources = [first_ref]
+    flips = [0]
+    for ref in others:
+        flips = flips + [flip ^ (groups // (2 * len(flips))) for flip in flips]
+        sources = sources + [ref.at[n * shards * group : (n + 1) * shards * group] for n in range(len(sources))]
+    quarter = 2 * state // len(sources)
+
+    def main(ref):
+        return jnp.concatenate([ref[k * group : k * group + per] for k in range(shards)], 0)
+
+    def rim(ref):
+        return jnp.concatenate([ref[k * group + per : (k + 1) * group] for k in range(shards)], 0)
+
+    own_main = main(first_ref)
     lane = iota((8, LANES), 1)
-    weights = jnp.where(lane == heads, 64.0, jnp.where(lane == heads + 1, 1.0, 0.0)).astype(bf16)
-    slots = dot_nt(weights, own_main[:, 2 * state :])[0:1].astype(jnp.int32) - 1
-    rim_slots = dot_nt(weights, own_rim[:, 2 * state :])[0:1].astype(jnp.int32) - 1 - rows + HALO
+    high_lane = quarter + heads
+    weights = jnp.where(lane == high_lane, 64.0, jnp.where(lane == high_lane + 1, 1.0, 0.0)).astype(bf16)
+    slots = dot_nt(weights, own_main)[0:1].astype(jnp.int32) - 1
+    rim_slots = dot_nt(weights, rim(first_ref))[0:1].astype(jnp.int32) - 1 - rows + HALO
     rim_pick = ones_where(iota((RIM, shards * RIM), 0) == rim_slots)
     rims_ref[...] = rim_pick
-    bc_main = own_main[:, : 2 * state]
-    own_main = own_main[:, 2 * state :]
-    packed[0:HALO] = dot(rim_pick, own_rim[:, : 2 * state])[0:HALO]
-    lane_of = iota((LANES, LANES), 0)
+    me = lax.axis_index("head")
+    bc_main, bc_rim = 0.0, 0.0
+    for flip, ref in zip(flips, sources):
+        lane = iota((LANES, 2 * state), 0)
+        spread = ones_where((lane < quarter) & (lane + (me ^ flip) * quarter == iota((LANES, 2 * state), 1)))
+        bc_main = bc_main + dot(main(ref), spread)
+        bc_rim = bc_rim + dot(rim(ref), spread)
+    bc_main = bc_main.astype(bf16)
+    packed[0:HALO] = dot(rim_pick, bc_rim.astype(bf16))[0:HALO]
+    lane_of = iota((LANES, LANES), 0) - quarter
     wide = iota((LANES, LANES), 1)
     copy_dt = ones_where(
-        (lane_of < heads)
+        (lane_of >= 0) & (lane_of < heads)
         & ((lane_of == wide) | (lane_of + heads == wide) | (lane_of + 2 * heads == wide))
     )
     decay_rate = -jnp.exp(lines_ref[1:2])
@@ -418,21 +439,28 @@
     place = placement.reshape(1, rows)
     thin = dt_in.T
     full = rows + shards * RIM
-    thick = 2 * state + LANES
+    quarter = 2 * state // groups
     first, last = parts[0]
     sent = call(
-        functools.partial(send_order, shards, width),
-        [shape(full, rows)] + [shape(group, thick)] * shards + [shape(group, (last - first) * TILE)] * shards,
+        functools.partial(send_order, shards, width, quarter),
+        [shape(full, rows)] + [shape(group, LANES)] * shards + [shape(group, (last - first) * TILE)] * shards,
         (place, bc_in, thin, xs),
         [whole(place), whole(bc_in), whole(thin), columns(rows)],
-        [whole(shape(full, rows))] + [whole(shape(group, thick))] * shards + [columns(group)] * shards,
+        [whole(shape(full, rows))] + [whole(shape(group, LANES))] * shards + [columns(group)] * shards,
         grid=(last - first,),
         micros=7,
+        limit=56,
     )
     picks, small, x_send = sent[0], sent[1 : 1 + shards], [sent[1 + shards :]]
     small = [small[0]] + [moved(small[k], "seq", k) for k in range(1, shards)]
     arrived = [[x_send[0][0]] + [moved(x_send[0][k], "seq", k) for k in range(1, shards)]]
 
+    small = [jnp.concatenate(small, 0)]
+    mask = groups // 2
+    while mask:
+        held = jnp.concatenate(small, 0) if len(small) > 1 else small[0]
+        small.append(lax.ppermute(held, "head", [(i, i ^ mask) for i in range(groups)]))
+        mask //= 2
     for first, last in parts[1:]:
         x_send.append(
             call(
@@ -479,10 +507,10 @@
         pick, rims, gap, score_high, score_low, query, kept_query,
         keys, inside, outside, carried, expand, factor, rest,
     ) = call(
-        functools.partial(prepare, shards, width, heads, head_dim),
+        functools.partial(prepare, shards, groups, width, heads, head_dim),
         kept,
-        (lengths, *small, conv_bc, lines),
-        [smem()] + [whole(s) for s in small] + [whole(conv_bc), whole(lines)],
+        (lengths, small[0], conv_bc, lines, *small[1:]),
+        [smem()] + [whole(s) for s in (small[0], conv_bc, lines, *small[1:])],
         [whole(s) for s in kept],
         scratch=[
             pltpu.VMEM((rows + HALO, 2 * state), f32),

time: 193 us -> 175 us (0.907)
  waiting for transfers between devices: 88.8 us -> 69.2 us
  Pallas kernels: 45.2 us -> 48.7 us
  local copies, waits for them, and re-layouts: 8.72 us -> 6.19 us
    ppermute x21 -> x18, waiting for transfers between devices: 78.1 us -> 56.4 us  [moved(): lax.ppermute(block, axis, [(i, (i + steps) % count) for i in range(count)])]
    pallas_call x14, Pallas kernels: 45.2 us -> 48.7 us  [call(): pl.pallas_call(kernel, grid=grid, in_specs=in_specs, out_specs=out_specs,...]
    unnamed x34, local copies, waits for them, and re-layouts: 8.71 us -> 6.14 us
    ppermute x9, waiting for transfers between devices: 10.7 us -> 12.8 us  [body(): received = lax.ppermute(leaving, 'seq', [(step - 1, step)])]
    ppermute x21 -> x18, starting transfers between devices: 34.7 us -> 34.8 us  [moved(): lax.ppermute(block, axis, [(i, (i + steps) % count) for i in range(count)])]
  transfers between devices with their start and end apart: 30 -> 29, of which waited for: 15 -> 13; matrix products, arithmetic and copies ran while one was open for 0% -> 1% of each run, Pallas kernels for 19% -> 22%
where the time goes in v3:
time: 175 us; the launch traced here: 174 us
  waiting for transfers between devices  69.2 us (40%)
  Pallas kernels  48.7 us (28%)
  starting transfers between devices  43.5 us (25%)
  local copies, waits for them, and re-layouts  6.19 us (4%)
  blocking collectives  5.68 us (3%)
    ppermute x18, waiting for transfers between devices, moved(): lax.ppermute(block, axis, [(i, (i + steps) % count) for i in range(count)])  56.4 us
    pallas_call x14, Pallas kernels, call(): pl.pallas_call(kernel, grid=grid, in_specs=in_specs, out_specs=out_specs,...  48.7 us
    ppermute x18, starting transfers between devices, moved(): lax.ppermute(block, axis, [(i, (i + steps) % count) for i in range(count)])  34.8 us
    ppermute x9, waiting for transfers between devices, body(): received = lax.ppermute(leaving, 'seq', [(step - 1, step)])  12.8 us
    ppermute x9, starting transfers between devices, body(): received = lax.ppermute(leaving, 'seq', [(step - 1, step)])  8.11 us
    unnamed x34, local copies, waits for them, and re-layouts  6.14 us
    psum x1, blocking collectives, body(): total = lax.psum(sum(totals), 'head')  5.68 us
  transfers between devices with their start and end apart: 29, of which 13 were waited for; matrix products, arithmetic and copies ran while one was open for 1% of the time, Pallas kernels for 22%

profile of v3, /device:TPU:26, one launch (start us, length us, event | category | flops | bytes accessed | tf_op | source)
XLA Modules:
  0.0 174.3 jit_solution(18431688267689306251)
XLA Ops:
  0.0 6.1 %shard_map.118 = (bf16[1088,1024]{1,0:T(8,128)(2,1)}, bf16[272,128]{1,0:T(8,128)(2,1)}, bf16[272,128]{1,0:T(8,128)(2,1)}, bf16[272,128]{1,0:T(8,128)(2,1)}, bf16...) custom-call(s32[1,1024]{1,0:T(1,128)} %bitcast.18, ...), custom_call_target="tpu_custom_call" | custom-call | flops 8049999872 | tf_op jit(solution)/shard_map/pallas_call | solution.py:61
  6.1 0.2 collective-permute-start
  6.4 1.7 collective-permute-start.1
  8.1 0.5 collective-permute-start.2
  8.5 3.4 %collective-permute-start.5 = (bf16[272,512]{1,0:T(8,128)(2,1)}, bf16[272,512]{1,0:T(8,128)(2,1)S(1)}, u32[]{:S(2)}, u32[]{:S(2)}) collective-permute-start(bf16[272,512]{1,0:T(8,128)(2,1)} %get-tuple-element.97), channel_id=1, source_target_pairs={{0,4},{4,8},{8,12},{12,0},{1,5},{5,9},{9,13},{13,1},{2,6},{6,10},{... | collective-permute-start | bytes 835592 | tf_op jit(solution)/shard_map/ppermute | solution.py:410
  11.9 0.9 constant_dynamic-update-slice_fusion.8
  12.8 1.3 collective-permute-start.7
  14.1 1.7 collective-permute-done.1
  15.8 0.6 collective-permute-start.3
  16.4 1.6 copy-done.5
  18.1 4.5 %shard_map.122 = (bf16[256,768]{1,0:T(8,128)(2,1)S(1)}, bf16[256,768]{1,0:T(8,128)(2,1)S(1)}, bf16[256,768]{1,0:T(8,128)(2,1)S(1)}, bf16[256,768]{1,0:T(8,128)(2...) custom-call(bf16[1088,1024]{1,0:T(8,128)(2,1)S(1)} %copy-done.5, ...), custom_call_target="tpu_custom_call" | custom-call | flops 11500000256 | tf_op jit(solution)/shard_map/pallas_call | solution.py:61
  22.6 0.0 copy-start.11
  22.6 0.0 copy-start.12
  22.6 0.0 copy-start.13
  22.6 0.0 copy-start.14
  22.7 0.1 collective-permute-start.4
  22.7 0.8 shard_map.123
  23.6 0.1 fusion.lines_ref
  23.7 1.8 %shard_map.121 = (bf16[272,512]{1,0:T(8,128)(2,1)S(1)}, bf16[272,512]{1,0:T(8,128)(2,1)S(1)}, bf16[272,512]{1,0:T(8,128)(2,1)S(1)}, bf16[272,512]{1,0:T(8,128)(2,1)S(1)}) custom-call(bf16[1088,1024]{1,0:T(8,128)(2,1)S(1)} %copy-done.5, bf16[1024,1280]{1,0:T(8,128)(2,1)S(1)} %copy-done.1), custom_call_target="tpu_custom_call" | custom-call | flops 4600000000 | tf_op jit(solution)/shard_map/pallas_call | solution.py:61
  25.5 6.2 %shard_map.119 = (bf16[1024,1024]{1,0:T(8,128)(2,1)S(1)}, bf16[16,64]{1,0:T(8,128)(2,1)S(1)}, s32[1024,128]{1,0:T(8,128)S(1)}, bf16[1024,256]{1,0:T(8,128)(2,1)S...) custom-call(s32[3]{0:T(128)S(1)} %copy-done.4, ...), custom_call_target="tpu_custom_call" | custom-call | flops 9200000000 | tf_op jit(solution)/shard_map/pallas_call | solution.py:61
  31.8 0.4 collective-permute-done.7.refs_3_
  32.2 6.7 %collective-permute-done.6.refs_2_ = bf16[272,512]{1,0:T(8,128)(2,1)S(1)} collective-permute-done((bf16[272,512]{1,0:T(8,128)(2,1)}, bf16[272,512]{1,0:T(8,128)(2,1)S(1)}, u32[]{:S(2)}, u32[]{:S(2)}) %collective-permute-start.6) | collective-permute-done | bytes 278560 | tf_op jit(solution)/shard_map/ppermute | solution.py:410
  38.9 5.8 %collective-permute-start.13 = (bf16[272,512]{1,0:T(8,128)(2,1)S(1)}, bf16[272,512]{1,0:T(8,128)(2,1)S(1)}, u32[]{:S(2)}, u32[]{:S(2)}) collective-permute-start(bf16[272,512]{1,0:T(8,128)(2,1)S(1)} %get-tuple-element.115), channel_id=1, source_target_pairs={{0,8},{4,12},{8,0},{12,4},{1,9},{5,13},{9,1},{13,5},{2,10},{6,14},... | collective-permute-start | bytes 835592 | tf_op jit(solution)/shard_map/ppermute | solution.py:410
  44.6 1.9 %collective-permute-start.14 = (bf16[272,512]{1,0:T(8,128)(2,1)S(1)}, bf16[272,512]{1,0:T(8,128)(2,1)S(1)}, u32[]{:S(2)}, u32[]{:S(2)}) collective-permute-start(bf16[272,512]{1,0:T(8,128)(2,1)S(1)} %get-tuple-element.117), channel_id=1, source_target_pairs={{0,12},{4,0},{8,4},{12,8},{1,13},{5,1},{9,5},{13,9},{2,14},{6,2},{... | collective-permute-start | bytes 835592 | tf_op jit(solution)/shard_map/ppermute | solution.py:410
  46.6 8.1 %shard_map.120 = (f32[1024,512]{1,0:T(8,128)S(1)}, f32[128,512]{1,0:T(8,128)S(1)}) custom-call(s32[3]{0:T(128)S(1)} %copy-done.4, bf16[1024,1024]{1,0:T(8,128)(2,1)S(1)} %get-tuple-element.82.pick_ref, bf16[16,64]{1,0:T(8,128)(2,1)S(1)} %get-tuple-element.86.rims_ref, s32[1024,128]{1,0:T(8,128)S(1)} %get-tuple-element.87.gap_ref, ...), custom_call_target="tpu_custom_call" | custom-call | flops 11500000256 | tf_op jit(solution)/shard_map/pallas_call | solution.py:61
  54.7 10.3 %collective-permute-done.14.refs_3_ = bf16[272,512]{1,0:T(8,128)(2,1)S(1)} collective-permute-done((bf16[272,512]{1,0:T(8,128)(2,1)S(1)}, bf16[272,512]{1,0:T(8,128)(2,1)S(1)}, u32[]{:S(2)}, u32[]{:S(2)}) %collective-permute-start.14) | collective-permute-done | bytes 278560 | tf_op jit(solution)/shard_map/ppermute | solution.py:410
  65.1 4.7 %collective-permute-done.13.refs_2_ = bf16[272,512]{1,0:T(8,128)(2,1)S(1)} collective-permute-done((bf16[272,512]{1,0:T(8,128)(2,1)S(1)}, bf16[272,512]{1,0:T(8,128)(2,1)S(1)}, u32[]{:S(2)}, u32[]{:S(2)}) %collective-permute-start.13) | collective-permute-done | bytes 278560 | tf_op jit(solution)/shard_map/ppermute | solution.py:410
  69.8 2.0 %collective-permute-start.19 = (bf16[272,256]{1,0:T(8,128)(2,1)S(1)}, bf16[272,256]{1,0:T(8,128)(2,1)S(1)}, u32[]{:S(2)}, u32[]{:S(2)}) collective-permute-start(bf16[272,256]{1,0:T(8,128)(2,1)S(1)} %get-tuple-element.128), channel_id=1, source_target_pairs={{0,12},{4,0},{8,4},{12,8},{1,13},{5,1},{9,5},{13,9},{2,14},{6,2},{... | collective-permute-start | bytes 417800 | tf_op jit(solution)/shard_map/ppermute | solution.py:410
  71.8 0.7 collective-permute-start.9
  72.5 8.2 %shard_map.124 = (f32[1024,512]{1,0:T(8,128)S(1)}, f32[128,512]{1,0:T(8,128)S(1)}) custom-call(s32[3]{0:T(128)S(1)} %copy-done.4, bf16[1024,1024]{1,0:T(8,128)(2,1)S(1)} %get-tuple-element.82.pick_ref, bf16[16,64]{1,0:T(8,128)(2,1)S(1)} %get-tuple-element.86.rims_ref, s32[1024,128]{1,0:T(8,128)S(1)} %get-tuple-element.87.gap_ref, ...), custom_call_target="tpu_custom_call" | custom-call | flops 11500000256 | tf_op jit(solution)/shard_map/pallas_call | solution.py:61
  80.7 0.7 collective-permute-start.21
  81.4 0.3 collective-permute-done.19.refs_3_
  81.7 0.5 collective-permute-done.17.refs_2_
  82.2 5.5 %collective-permute-start.15 = (bf16[256,768]{1,0:T(8,128)(2,1)S(1)}, bf16[256,768]{1,0:T(8,128)(2,1)S(1)}, u32[]{:S(2)}, u32[]{:S(2)}) collective-permute-start(bf16[256,768]{1,0:T(8,128)(2,1)S(1)} %get-tuple-element.119), channel_id=1, source_target_pairs={{0,4},{4,8},{8,12},{12,0},{1,5},{5,9},{9,13},{13,1},{2,6},{6,10},{... | collective-permute-start | bytes 1179656 | tf_op jit(solution)/shard_map/ppermute | solution.py:410
  87.7 0.6 collective-permute-start.20
  88.4 0.7 collective-permute-start.10
  89.2 0.7 collective-permute-start.22
  89.8 4.2 %shard_map.129 = (f32[1024,256]{1,0:T(8,128)S(1)}, f32[128,256]{1,0:T(8,128)S(1)}) custom-call(s32[3]{0:T(128)S(1)} %copy-done.4, bf16[1024,1024]{1,0:T(8,128)(2,1)S(1)} %get-tuple-element.82.pick_ref, bf16[16,64]{1,0:T(8,128)(2,1)S(1)} %get-tuple-element.86.rims_ref, s32[1024,128]{1,0:T(8,128)S(1)} %get-tuple-element.87.gap_ref, ...), custom_call_target="tpu_custom_call" | custom-call | flops 5750000128 | tf_op jit(solution)/shard_map/pallas_call | solution.py:61
  94.1 0.1 multiply_add_fusion.2
  94.2 1.3 collective-permute-start.11
  95.5 1.9 %collective-permute-done.15.refs_1_ = bf16[256,768]{1,0:T(8,128)(2,1)S(1)} collective-permute-done((bf16[256,768]{1,0:T(8,128)(2,1)S(1)}, bf16[256,768]{1,0:T(8,128)(2,1)S(1)}, u32[]{:S(2)}, u32[]{:S(2)}) %collective-permute-start.15) | collective-permute-done | bytes 393248 | tf_op jit(solution)/shard_map/ppermute | solution.py:410
  97.3 0.7 collective-permute-start.26
  98.0 22.8 %collective-permute-done.18.refs_2_ = bf16[256,768]{1,0:T(8,128)(2,1)S(1)} collective-permute-done((bf16[256,768]{1,0:T(8,128)(2,1)S(1)}, bf16[256,768]{1,0:T(8,128)(2,1)S(1)}, u32[]{:S(2)}, u32[]{:S(2)}) %collective-permute-start.18) | collective-permute-done | bytes 393248 | tf_op jit(solution)/shard_map/ppermute | solution.py:410
  120.8 9.4 %collective-permute-start.16 = (bf16[256,512]{1,0:T(8,128)(2,1)S(1)}, bf16[256,512]{1,0:T(8,128)(2,1)S(1)}, u32[]{:S(2)}, u32[]{:S(2)}) collective-permute-start(bf16[256,512]{1,0:T(8,128)(2,1)S(1)} %get-tuple-element.120), channel_id=1, source_target_pairs={{0,4},{4,8},{8,12},{12,0},{1,5},{5,9},{9,13},{13,1},{2,6},{6,10},{... | collective-permute-start | bytes 786440 | tf_op jit(solution)/shard_map/ppermute | solution.py:410
  130.2 0.4 collective-permute-start.24
  130.6 2.0 %collective-permute-start.25 = (bf16[256,512]{1,0:T(8,128)(2,1)S(1)}, bf16[256,512]{1,0:T(8,128)(2,1)S(1)}, u32[]{:S(2)}, u32[]{:S(2)}) collective-permute-start(bf16[256,512]{1,0:T(8,128)(2,1)S(1)} %get-tuple-element.139), channel_id=1, source_target_pairs={{0,12},{4,0},{8,4},{12,8},{1,13},{5,1},{9,5},{13,9},{2,14},{6,2},{... | collective-permute-start | bytes 786440 | tf_op jit(solution)/shard_map/ppermute | solution.py:410
  132.6 0.1 multiply_add_fusion
  132.7 1.3 collective-permute-start.23
  134.1 1.5 collective-permute-done.11
  135.6 0.9 collective-permute-start.27
  136.5 7.1 %collective-permute-done.16.refs_1_ = bf16[256,512]{1,0:T(8,128)(2,1)S(1)} collective-permute-done((bf16[256,512]{1,0:T(8,128)(2,1)S(1)}, bf16[256,512]{1,0:T(8,128)(2,1)S(1)}, u32[]{:S(2)}, u32[]{:S(2)}) %collective-permute-start.16) | collective-permute-done | bytes 262176 | tf_op jit(solution)/shard_map/ppermute | solution.py:410
  143.6 1.3 shard_map.126
  144.9 1.3 shard_map.125
  146.2 1.3 collective-permute-start.28
  147.5 8.2 %collective-permute-done.23 = f32[128,512]{1,0:T(8,128)S(1)} collective-permute-done((f32[128,512]{1,0:T(8,128)S(1)}, f32[128,512]{1,0:T(8,128)S(1)}, u32[]{:S(2)}, u32[]{:S(2)}) %collective-permute-start.23) | collective-permute-done | bytes 262176 | tf_op jit(solution)/shard_map/ppermute | solution.py:568
  155.7 1.3 shard_map.127
  157.0 1.3 shard_map.128
  158.3 3.1 %collective-permute-done.28 = f32[128,256]{1,0:T(8,128)S(1)} collective-permute-done((f32[128,256]{1,0:T(8,128)S(1)}, f32[128,256]{1,0:T(8,128)S(1)}, u32[]{:S(2)}, u32[]{:S(2)}) %collective-permute-start.28) | collective-permute-done | bytes 131104 | tf_op jit(solution)/shard_map/ppermute | solution.py:568
  161.4 1.3 shard_map.130
  162.7 1.0 copy-done.8
  163.7 5.7 %psum.7.total_ref = f32[1,1024]{1,0:T(1,128)S(1)} all-reduce(f32[1,1024]{1,0:T(1,128)S(1)} %add_add_fusion), channel_id=1, replica_groups=mesh['parts'=2,'seq'=4,'head'=4] {'head'}, use_global_device_ids=true, to_apply=%region_0.1 | all-reduce | flops 1024 | bytes 8192 | tf_op jit(solution)/shard_map/psum | solution.py:592
  169.4 1.2 copy-done.7
  170.6 1.2 copy-done.9
  171.9 2.4 %shard_map.131 = bf16[1024,1280]{1,0:T(8,128)(2,1)} custom-call(f32[1,1024]{1,0:T(1,128)S(1)} %psum.7.total_ref, f32[1,1280]{1,0:T(1,128)S(1)} %reshape.7.gain_ref, f32[1024,256]{1,0:T(8,128)S(1)} %get-tuple-element.146.refs_0_, f32[1024,256]{1,0:T(8,128)S(1)} %get-tuple-element.147.refs_1_, f32[1024,256]{1,0:T(8,128)S(1)} %get-tuple-element.148.refs_2_, ...), custom_call_target="tpu_custom_call" | custom-call | flops 5750000128 | tf_op jit(solution)/shard_map/pallas_call | solution.py:61
  (58 shorter events, 0.5 us)
Async XLA Ops:
  0.0 16.4 %copy-start = (bf16[1024,1280]{1,0:T(8,128)(2,1)S(1)}, bf16[1024,1280]{1,0:T(8,128)(2,1)}, u32[]{:S(2)}) copy-start(bf16[1024,1280]{1,0:T(8,128)(2,1)} %x_ref.6) | copy-start | bytes 7864324
  6.1 6.6 %collective-permute-start = (bf16[272,128]{1,0:T(8,128)(2,1)}, bf16[272,128]{1,0:T(8,128)(2,1)S(1)}, u32[]{:S(2)}, u32[]{:S(2)}) collective-permute-start(bf16[272,128]{1,0:T(8,128)(2,1)} %get-tuple-element.79), channel_id=1, source_target_pairs={{0,4},{4,8},{8,12},{12,0},{1,5},{5,9},{9,13},{13,1},{2,6},{6,10},{... | collective-permute-start | bytes 208904 | tf_op jit(solution)/shard_map/ppermute | solution.py:410
  6.4 9.4 %collective-permute-start.1 = (bf16[272,128]{1,0:T(8,128)(2,1)}, bf16[272,128]{1,0:T(8,128)(2,1)S(1)}, u32[]{:S(2)}, u32[]{:S(2)}) collective-permute-start(bf16[272,128]{1,0:T(8,128)(2,1)} %get-tuple-element.80), channel_id=1, source_target_pairs={{0,8},{4,12},{8,0},{12,4},{1,9},{5,13},{9,1},{13,5},{2,10},{6,14},... | collective-permute-start | bytes 208904 | tf_op jit(solution)/shard_map/ppermute | solution.py:410
  8.1 7.7 %collective-permute-start.2 = (bf16[272,128]{1,0:T(8,128)(2,1)}, bf16[272,128]{1,0:T(8,128)(2,1)S(1)}, u32[]{:S(2)}, u32[]{:S(2)}) collective-permute-start(bf16[272,128]{1,0:T(8,128)(2,1)} %get-tuple-element.81), channel_id=1, source_target_pairs={{0,12},{4,0},{8,4},{12,8},{1,13},{5,1},{9,5},{13,9},{2,14},{6,2},{... | collective-permute-start | bytes 208904 | tf_op jit(solution)/shard_map/ppermute | solution.py:410
  8.5 30.3 %collective-permute-start.5 = (bf16[272,512]{1,0:T(8,128)(2,1)}, bf16[272,512]{1,0:T(8,128)(2,1)S(1)}, u32[]{:S(2)}, u32[]{:S(2)}) collective-permute-start(bf16[272,512]{1,0:T(8,128)(2,1)} %get-tuple-element.97), channel_id=1, source_target_pairs={{0,4},{4,8},{8,12},{12,0},{1,5},{5,9},{9,13},{13,1},{2,6},{6,10},{... | collective-permute-start | bytes 835592 | tf_op jit(solution)/shard_map/ppermute | solution.py:410
  11.9 27.0 %collective-permute-start.6 = (bf16[272,512]{1,0:T(8,128)(2,1)}, bf16[272,512]{1,0:T(8,128)(2,1)S(1)}, u32[]{:S(2)}, u32[]{:S(2)}) collective-permute-start(bf16[272,512]{1,0:T(8,128)(2,1)} %get-tuple-element.98), channel_id=1, source_target_pairs={{0,8},{4,12},{8,0},{12,4},{1,9},{5,13},{9,1},{13,5},{2,10},{6,14},... | collective-permute-start | bytes 835592 | tf_op jit(solution)/shard_map/ppermute | solution.py:410
  12.8 19.4 %collective-permute-start.7 = (bf16[272,512]{1,0:T(8,128)(2,1)}, bf16[272,512]{1,0:T(8,128)(2,1)S(1)}, u32[]{:S(2)}, u32[]{:S(2)}) collective-permute-start(bf16[272,512]{1,0:T(8,128)(2,1)} %get-tuple-element.99), channel_id=1, source_target_pairs={{0,12},{4,0},{8,4},{12,8},{1,13},{5,1},{9,5},{13,9},{2,14},{6,2},{... | collective-permute-start | bytes 835592 | tf_op jit(solution)/shard_map/ppermute | solution.py:410
  15.8 6.7 %collective-permute-start.3 = (bf16[1088,128]{1,0:T(8,128)(2,1)S(1)}, bf16[1088,128]{1,0:T(8,128)(2,1)S(1)}, u32[]{:S(2)}, u32[]{:S(2)}) collective-permute-start(bf16[1088,128]{1,0:T(8,128)(2,1)S(1)} %get-tuple-element.158.first_ref), channel_id=1, source_target_pairs={{0,2},{1,3},{2,0},{3,1},{4,6},{5,7},{6,4},{7,5},{8,10},{9,11},{10,... | collective-permute-start | bytes 835592 | tf_op jit(solution)/shard_map/ppermute | solution.py:462
  16.4 1.6 copy-start.5
  18.1 4.7 %copy-start.1 = (bf16[1024,1280]{1,0:T(8,128)(2,1)S(1)}, bf16[1024,1280]{1,0:T(8,128)(2,1)}, u32[]{:S(2)}) copy-start(bf16[1024,1280]{1,0:T(8,128)(2,1)} %x_ref.7) | copy-start | bytes 7864324
  22.6 0.9 copy-start.11
  22.6 0.9 copy-start.12
  22.6 0.9 copy-start.13
  22.6 0.9 copy-start.14
  22.7 2.9 %collective-permute-start.4 = (bf16[2176,128]{1,0:T(8,128)(2,1)S(1)}, bf16[2176,128]{1,0:T(8,128)(2,1)S(1)}, u32[]{:S(2)}, u32[]{:S(2)}) collective-permute-start(bf16[2176,128]{1,0:T(8,128)(2,1)S(1)} %constant_dynamic-update-slice_fusion.4), channel_id=1, source_target_pairs={{0,1},{1,0},{2,3},{3,2},{4,5},{5,4},{6,7},{7,6},{8,9},{9,8},{10,11... | collective-permute-start | bytes 1671176 | tf_op jit(solution)/shard_map/ppermute | solution.py:462
  23.7 1.8 %copy-start.3 = (f32[4,256]{1,0:T(4,128)S(1)}, f32[4,256]{1,0:T(4,128)}, u32[]{:S(2)}) copy-start(f32[4,256]{1,0:T(4,128)} %taps_ref.4) | copy-start | bytes 12292
  23.7 1.9 %copy-start.4 = (s32[3]{0:T(128)S(1)}, s32[3]{0:T(128)}, u32[]{:S(2)}) copy-start(s32[3]{0:T(128)} %lengths.7) | copy-start | bytes 40
  25.5 21.1 %copy-start.2 = (f32[4,1280]{1,0:T(4,128)S(1)}, f32[4,1280]{1,0:T(4,128)}, u32[]{:S(2)}) copy-start(f32[4,1280]{1,0:T(4,128)} %taps_ref.7) | copy-start | bytes 61444
  25.5 21.1 %copy-start.10 = (bf16[272,512]{1,0:T(8,128)(2,1)S(1)}, bf16[272,512]{1,0:T(8,128)(2,1)}, u32[]{:S(2)}) copy-start(bf16[272,512]{1,0:T(8,128)(2,1)} %get-tuple-element.96.refs_0_) | copy-start | bytes 835588
  38.9 30.9 %collective-permute-start.8 = (bf16[272,512]{1,0:T(8,128)(2,1)S(1)}, bf16[272,512]{1,0:T(8,128)(2,1)S(1)}, u32[]{:S(2)}, u32[]{:S(2)}) collective-permute-start(bf16[272,512]{1,0:T(8,128)(2,1)S(1)} %get-tuple-element.106), channel_id=1, source_target_pairs={{0,4},{4,8},{8,12},{12,0},{1,5},{5,9},{9,13},{13,1},{2,6},{6,10},{... | collective-permute-start | bytes 835592 | tf_op jit(solution)/shard_map/ppermute | solution.py:410
  38.9 30.9 %collective-permute-start.13 = (bf16[272,512]{1,0:T(8,128)(2,1)S(1)}, bf16[272,512]{1,0:T(8,128)(2,1)S(1)}, u32[]{:S(2)}, u32[]{:S(2)}) collective-permute-start(bf16[272,512]{1,0:T(8,128)(2,1)S(1)} %get-tuple-element.115), channel_id=1, source_target_pairs={{0,8},{4,12},{8,0},{12,4},{1,9},{5,13},{9,1},{13,5},{2,10},{6,14},... | collective-permute-start | bytes 835592 | tf_op jit(solution)/shard_map/ppermute | solution.py:410
  44.6 20.4 %collective-permute-start.14 = (bf16[272,512]{1,0:T(8,128)(2,1)S(1)}, bf16[272,512]{1,0:T(8,128)(2,1)S(1)}, u32[]{:S(2)}, u32[]{:S(2)}) collective-permute-start(bf16[272,512]{1,0:T(8,128)(2,1)S(1)} %get-tuple-element.117), channel_id=1, source_target_pairs={{0,12},{4,0},{8,4},{12,8},{1,13},{5,1},{9,5},{13,9},{2,14},{6,2},{... | collective-permute-start | bytes 835592 | tf_op jit(solution)/shard_map/ppermute | solution.py:410
  69.8 10.9 %collective-permute-start.12 = (bf16[272,256]{1,0:T(8,128)(2,1)S(1)}, bf16[272,256]{1,0:T(8,128)(2,1)S(1)}, u32[]{:S(2)}, u32[]{:S(2)}) collective-permute-start(bf16[272,256]{1,0:T(8,128)(2,1)S(1)} %get-tuple-element.111), channel_id=1, source_target_pairs={{0,4},{4,8},{8,12},{12,0},{1,5},{5,9},{9,13},{13,1},{2,6},{6,10},{... | collective-permute-start | bytes 417800 | tf_op jit(solution)/shard_map/ppermute | solution.py:410
  69.8 12.4 %collective-permute-start.17 = (bf16[272,256]{1,0:T(8,128)(2,1)S(1)}, bf16[272,256]{1,0:T(8,128)(2,1)S(1)}, u32[]{:S(2)}, u32[]{:S(2)}) collective-permute-start(bf16[272,256]{1,0:T(8,128)(2,1)S(1)} %get-tuple-element.124), channel_id=1, source_target_pairs={{0,8},{4,12},{8,0},{12,4},{1,9},{5,13},{9,1},{13,5},{2,10},{6,14},... | collective-permute-start | bytes 417800 | tf_op jit(solution)/shard_map/ppermute | solution.py:410
  69.8 11.9 %collective-permute-start.19 = (bf16[272,256]{1,0:T(8,128)(2,1)S(1)}, bf16[272,256]{1,0:T(8,128)(2,1)S(1)}, u32[]{:S(2)}, u32[]{:S(2)}) collective-permute-start(bf16[272,256]{1,0:T(8,128)(2,1)S(1)} %get-tuple-element.128), channel_id=1, source_target_pairs={{0,12},{4,0},{8,4},{12,8},{1,13},{5,1},{9,5},{13,9},{2,14},{6,2},{... | collective-permute-start | bytes 417800 | tf_op jit(solution)/shard_map/ppermute | solution.py:410
  71.8 16.5 %collective-permute-start.9 = (f32[128,512]{1,0:T(8,128)S(1)}, f32[128,512]{1,0:T(8,128)S(1)}, u32[]{:S(2)}, u32[]{:S(2)}) collective-permute-start(f32[128,512]{1,0:T(8,128)S(1)} %get-tuple-element.107), channel_id=1, source_target_pairs={{0,4},{1,5},{2,6},{3,7},{16,20},{17,21},{18,22},{19,23}} | collective-permute-start | bytes 786440 | tf_op jit(solution)/shard_map/ppermute | solution.py:568
  80.7 8.4 %collective-permute-start.21 = (f32[128,512]{1,0:T(8,128)S(1)}, f32[128,512]{1,0:T(8,128)S(1)}, u32[]{:S(2)}, u32[]{:S(2)}) collective-permute-start(f32[128,512]{1,0:T(8,128)S(1)} %get-tuple-element.133), channel_id=1, source_target_pairs={{0,4},{1,5},{2,6},{3,7},{16,20},{17,21},{18,22},{19,23}} | collective-permute-start | bytes 786440 | tf_op jit(solution)/shard_map/ppermute | solution.py:568
  82.2 15.1 %collective-permute-start.15 = (bf16[256,768]{1,0:T(8,128)(2,1)S(1)}, bf16[256,768]{1,0:T(8,128)(2,1)S(1)}, u32[]{:S(2)}, u32[]{:S(2)}) collective-permute-start(bf16[256,768]{1,0:T(8,128)(2,1)S(1)} %get-tuple-element.119), channel_id=1, source_target_pairs={{0,4},{4,8},{8,12},{12,0},{1,5},{5,9},{9,13},{13,1},{2,6},{6,10},{... | collective-permute-start | bytes 1179656 | tf_op jit(solution)/shard_map/ppermute | solution.py:410
  87.7 33.1 %collective-permute-start.18 = (bf16[256,768]{1,0:T(8,128)(2,1)S(1)}, bf16[256,768]{1,0:T(8,128)(2,1)S(1)}, u32[]{:S(2)}, u32[]{:S(2)}) collective-permute-start(bf16[256,768]{1,0:T(8,128)(2,1)S(1)} %get-tuple-element.125), channel_id=1, source_target_pairs={{0,8},{4,12},{8,0},{12,4},{1,9},{5,13},{9,1},{13,5},{2,10},{6,14},... | collective-permute-start | bytes 1179656 | tf_op jit(solution)/shard_map/ppermute | solution.py:410
  87.7 42.5 %collective-permute-start.20 = (bf16[256,768]{1,0:T(8,128)(2,1)S(1)}, bf16[256,768]{1,0:T(8,128)(2,1)S(1)}, u32[]{:S(2)}, u32[]{:S(2)}) collective-permute-start(bf16[256,768]{1,0:T(8,128)(2,1)S(1)} %get-tuple-element.129), channel_id=1, source_target_pairs={{0,12},{4,0},{8,4},{12,8},{1,13},{5,1},{9,5},{13,9},{2,14},{6,2},{... | collective-permute-start | bytes 1179656 | tf_op jit(solution)/shard_map/ppermute | solution.py:410
  88.4 5.7 %collective-permute-start.10 = (f32[128,512]{1,0:T(8,128)S(1)}, f32[128,512]{1,0:T(8,128)S(1)}, u32[]{:S(2)}, u32[]{:S(2)}) collective-permute-start(f32[128,512]{1,0:T(8,128)S(1)} %multiply_add_fusion.3), channel_id=1, source_target_pairs={{4,8},{5,9},{6,10},{7,11},{20,24},{21,25},{22,26},{23,27}} | collective-permute-start | bytes 786440 | tf_op jit(solution)/shard_map/ppermute | solution.py:568
  89.2 41.5 %collective-permute-start.22 = (f32[128,512]{1,0:T(8,128)S(1)}, f32[128,512]{1,0:T(8,128)S(1)}, u32[]{:S(2)}, u32[]{:S(2)}) collective-permute-start(f32[128,512]{1,0:T(8,128)S(1)} %multiply_add_fusion.1), channel_id=1, source_target_pairs={{4,8},{5,9},{6,10},{7,11},{20,24},{21,25},{22,26},{23,27}} | collective-permute-start | bytes 786440 | tf_op jit(solution)/shard_map/ppermute | solution.py:568
  94.2 41.4 %collective-permute-start.11 = (f32[128,512]{1,0:T(8,128)S(1)}, f32[128,512]{1,0:T(8,128)S(1)}, u32[]{:S(2)}, u32[]{:S(2)}) collective-permute-start(f32[128,512]{1,0:T(8,128)S(1)} %get-tuple-element.151), channel_id=1, source_target_pairs={{8,12},{9,13},{10,14},{11,15},{24,28},{25,29},{26,30},{27,31}} | collective-permute-start | bytes 786440 | tf_op jit(solution)/shard_map/ppermute | solution.py:568
  97.3 35.4 %collective-permute-start.26 = (f32[128,256]{1,0:T(8,128)S(1)}, f32[128,256]{1,0:T(8,128)S(1)}, u32[]{:S(2)}, u32[]{:S(2)}) collective-permute-start(f32[128,256]{1,0:T(8,128)S(1)} %get-tuple-element.144), channel_id=1, source_target_pairs={{0,4},{1,5},{2,6},{3,7},{16,20},{17,21},{18,22},{19,23}} | collective-permute-start | bytes 393224 | tf_op jit(solution)/shard_map/ppermute | solution.py:568
  120.8 22.8 %collective-permute-start.16 = (bf16[256,512]{1,0:T(8,128)(2,1)S(1)}, bf16[256,512]{1,0:T(8,128)(2,1)S(1)}, u32[]{:S(2)}, u32[]{:S(2)}) collective-permute-start(bf16[256,512]{1,0:T(8,128)(2,1)S(1)} %get-tuple-element.120), channel_id=1, source_target_pairs={{0,4},{4,8},{8,12},{12,0},{1,5},{5,9},{9,13},{13,1},{2,6},{6,10},{... | collective-permute-start | bytes 786440 | tf_op jit(solution)/shard_map/ppermute | solution.py:410
  130.2 26.8 %collective-permute-start.24 = (bf16[256,512]{1,0:T(8,128)(2,1)S(1)}, bf16[256,512]{1,0:T(8,128)(2,1)S(1)}, u32[]{:S(2)}, u32[]{:S(2)}) collective-permute-start(bf16[256,512]{1,0:T(8,128)(2,1)S(1)} %get-tuple-element.137), channel_id=1, source_target_pairs={{0,8},{4,12},{8,0},{12,4},{1,9},{5,13},{9,1},{13,5},{2,10},{6,14},... | collective-permute-start | bytes 786440 | tf_op jit(solution)/shard_map/ppermute | solution.py:410
  130.6 26.4 %collective-permute-start.25 = (bf16[256,512]{1,0:T(8,128)(2,1)S(1)}, bf16[256,512]{1,0:T(8,128)(2,1)S(1)}, u32[]{:S(2)}, u32[]{:S(2)}) collective-permute-start(bf16[256,512]{1,0:T(8,128)(2,1)S(1)} %get-tuple-element.139), channel_id=1, source_target_pairs={{0,12},{4,0},{8,4},{12,8},{1,13},{5,1},{9,5},{13,9},{2,14},{6,2},{... | collective-permute-start | bytes 786440 | tf_op jit(solution)/shard_map/ppermute | solution.py:410
  132.7 23.0 %collective-permute-start.23 = (f32[128,512]{1,0:T(8,128)S(1)}, f32[128,512]{1,0:T(8,128)S(1)}, u32[]{:S(2)}, u32[]{:S(2)}) collective-permute-start(f32[128,512]{1,0:T(8,128)S(1)} %get-tuple-element.153), channel_id=1, source_target_pairs={{8,12},{9,13},{10,14},{11,15},{24,28},{25,29},{26,30},{27,31}} | collective-permute-start | bytes 786440 | tf_op jit(solution)/shard_map/ppermute | solution.py:568
  135.6 10.6 %collective-permute-start.27 = (f32[128,256]{1,0:T(8,128)S(1)}, f32[128,256]{1,0:T(8,128)S(1)}, u32[]{:S(2)}, u32[]{:S(2)}) collective-permute-start(f32[128,256]{1,0:T(8,128)S(1)} %multiply_add_fusion.5), channel_id=1, source_target_pairs={{4,8},{5,9},{6,10},{7,11},{20,24},{21,25},{22,26},{23,27}} | collective-permute-start | bytes 393224 | tf_op jit(solution)/shard_map/ppermute | solution.py:568
  146.2 15.1 %collective-permute-start.28 = (f32[128,256]{1,0:T(8,128)S(1)}, f32[128,256]{1,0:T(8,128)S(1)}, u32[]{:S(2)}, u32[]{:S(2)}) collective-permute-start(f32[128,256]{1,0:T(8,128)S(1)} %get-tuple-element.155), channel_id=1, source_target_pairs={{8,12},{9,13},{10,14},{11,15},{24,28},{25,29},{26,30},{27,31}} | collective-permute-start | bytes 393224 | tf_op jit(solution)/shard_map/ppermute | solution.py:568
  158.3 4.4 %copy-start.6 = (f32[1024,256]{1,0:T(8,128)}, f32[1024,256]{1,0:T(8,128)S(1)}, u32[]{:S(2)}) copy-start(f32[1024,256]{1,0:T(8,128)S(1)} %get-tuple-element.149.refs_3_) | copy-start | bytes 3145732
  162.7 1.0 copy-start.8
  169.4 1.2 copy-start.7
  170.6 1.2 copy-start.9

commit v4 on v3

--- a/solution.py
+++ b/solution.py
@@ -12,8 +12,10 @@
 TILE = 256
 LANES = 128
 RIM = 16
-SHARES = (0.4, 0.8)
+SHARES = (0.4,)
 GATE_SHARES = (0.6,)
+WINDOW = 2
+TINY = 2.0**-100
 HALO = 8
 GROUPS = 3
 FAR = 1 << 28
@@ -316,7 +318,7 @@
     inside_ref, outside_ref, expand_ref, factor_ref, rest_ref, taps_ref, *refs,
 ):
     blocks = refs[:shards]
-    out_ref, state_ref, arrived, packed = refs[shards:]
+    out_ref, state_ref, size_ref, arrived, packed = refs[shards:]
     rows = pick_ref.shape[0]
     per = rows // shards
     base = lax.axis_index("seq") * rows
@@ -356,9 +358,11 @@
             carry = (carry * keep + added) * factor_ref[number : number + 1]
         state_ref[...] = carry
         out_ref[here] = outside * (total + jnp.concatenate(parts, 0)) + rest_ref[1:2] * conv
-
-
-def gate_columns(shards, pick_ref, query_ref, carried_ref, expand_ref, scan_ref, state_ref, *refs):
+    largest = jnp.max(jnp.abs(state_ref[...]), axis=0, keepdims=True)
+    size_ref[...] = jnp.broadcast_to(jnp.maximum(largest, TINY), size_ref.shape)
+
+
+def gate_columns(shards, sum_ref, pick_ref, query_ref, carried_ref, expand_ref, scan_ref, state_ref, *refs):
     blocks = refs[:shards]
     out_ref, total_ref, arrived, square_ref = refs[shards:]
     rows = pick_ref.shape[0]
@@ -389,12 +393,16 @@
     def _():
         for b in range(rows // ROWS):
             here = slice(b * ROWS, (b + 1) * ROWS)
-            total_ref[:, here] = jnp.sum(square_ref[here].T, axis=0, keepdims=True)
-
-
-def normalize(count, total_ref, gain_ref, *refs):
-    pieces, out_ref = refs[:-1], refs[-1]
-    scale = lax.rsqrt(total_ref[...] / count + 1e-05)
+            total_ref[:, here] = sum_ref[:, here] + jnp.sum(square_ref[here].T, axis=0, keepdims=True)
+
+
+def normalize(count, groups, *refs):
+    pieces, out_ref = refs[groups + 1 : -1], refs[-1]
+    gain_ref = refs[groups]
+    scale = refs[0][...]
+    for ref in refs[1:groups]:
+        scale = scale + ref[...]
+    scale = lax.rsqrt(scale / count + 1e-05)
     scale = jnp.broadcast_to(scale, (LANES, scale.shape[1])).T
     first = 0
     for ref in pieces:
@@ -412,6 +420,18 @@
 
 def after(value, *others):
     return lax.optimization_barrier((value, *others))[0]
+
+
+def packed_state(state, bound):
+    power = jnp.ceil(jnp.log2(bound))
+    rows = jnp.broadcast_to(power, (8, state.shape[1]))
+    return jnp.concatenate([state * jnp.exp2(-power), rows], 0).astype(jnp.float16)
+
+
+def unpacked(packet):
+    wide = packet.astype(f32)
+    scale = jnp.exp2(wide[-1:])
+    return wide[:-8] * scale, scale
 
 
 def cut(tiles, shares):
@@ -520,13 +540,15 @@
         micros=8,
     )
 
+    distances = sorted(range(1, shards), key=lambda k: (abs(2 * k - shards), k))
+
     def stream(send, before, *others):
         return [send[0]] + [
             moved(after(send[k], before[k], *others), "seq", k) for k in range(1, shards)
         ]
 
     if len(parts) > 1:
-        arrived.append(stream(x_send[1], arrived[0], rims, gate_send[0][0], x_send[-1][0]))
+        arrived.append(stream(x_send[1], arrived[0], gate_send[0][0], x_send[-1][0]))
 
     scans, ends, states, gates = [], [], [], []
     for number, part in enumerate(parts):
@@ -535,9 +557,9 @@
         size = (last - first) * TILE
         if ends:
             blocks = [after(blocks[0], ends[-1])] + blocks[1:]
-        scanned, local_state = call(
+        scanned, local_state, largest = call(
             functools.partial(scan_columns, shards, width),
-            [shape(rows, size, dtype=f32), shape(state, size, dtype=f32)],
+            [shape(rows, size, dtype=f32), shape(state, size, dtype=f32), shape(8, size, dtype=f32)],
             (
                 lengths, pick, rims, gap, score_high, score_low, kept_query, keys, inside, outside,
                 expand, factor, rest, conv_x, *blocks,
@@ -546,7 +568,7 @@
             + [whole(a) for a in (pick, rims, gap, score_high, score_low, kept_query, keys, inside, outside)]
             + [columns(n, start=first) for n in (LANES, chunks, 8, width)]
             + [columns(group)] * shards,
-            [columns(rows), columns(state)],
+            [columns(rows), columns(state), columns(8)],
             grid=(last - first,),
             scratch=[pltpu.VMEM((rows, TILE), bf16), pltpu.VMEM((rows + HALO, TILE), f32)],
             micros=5 * (last - first),
@@ -556,31 +578,38 @@
         if number + 2 < len(parts):
             arrived.append(stream(x_send[number + 2], arrived[number + 1], local_state))
         if not gates and number + 2 >= len(parts):
-            gates.append(stream(gate_send[0], arrived[-1], local_state))
-            for send in gate_send[1:]:
-                gates.append(stream(send, gates[-1]))
-        following = (arrived + gates)[number + 1]
-        incoming = leaving = None
+            started = [(arrived[-1][k], local_state) for k in distances[:WINDOW]]
+            for send in gate_send:
+                gates.append([send[0]] + [None] * (shards - 1))
+                for k in distances:
+                    block = moved(after(send[k], *started[-WINDOW]), "seq", k)
+                    gates[-1][k] = block
+                    started.append((block,))
+        following = (arrived + gates)[number + 1][distances[0]]
+        local_state = after(local_state, following)
+        passing = rest[0:1, first * TILE : last * TILE]
+        packet = None
         for step in range(1, shards):
-            leaving = after(local_state, following[1])
-            if incoming is not None:
-                leaving = leaving + rest[0:1, first * TILE : last * TILE] * incoming
-            received = lax.ppermute(leaving, "seq", [(step - 1, step)])
-            incoming = received if incoming is None else incoming + received
-        states.append(incoming)
-
-    outs, totals = [], []
+            leaving, bound = local_state, largest[0:1]
+            if packet is not None:
+                incoming, reach = unpacked(packet)
+                leaving, bound = leaving + passing * incoming, bound + passing * reach
+            received = lax.ppermute(packed_state(leaving, bound), "seq", [(step - 1, step)])
+            packet = received if packet is None else packet + received
+        states.append(unpacked(packet)[0])
+
+    outs, totals = [], [jnp.zeros((1, rows), f32)]
     for tile in range(tiles):
         part = sum(tile >= last for _, last in parts)
         gate_part = sum(tile >= last for _, last in gate_parts)
         blocks = gates[gate_part]
         if gate_part + 1 < len(gates):
-            blocks = [after(blocks[0], gates[gate_part + 1][1])] + blocks[1:]
+            blocks = [after(blocks[0], gates[gate_part + 1][distances[0]])] + blocks[1:]
         gated, total = call(
             functools.partial(gate_columns, shards),
             [shape(rows, TILE, dtype=f32), shape(1, rows, dtype=f32)],
-            (pick, query, carried, expand, scans[part], states[part], *blocks),
-            [whole(pick), whole(query), whole(carried), columns(LANES, start=tile)]
+            (totals[-1], pick, query, carried, expand, scans[part], states[part], *blocks),
+            [whole(totals[-1]), whole(pick), whole(query), whole(carried), columns(LANES, start=tile)]
             + [columns(n, start=tile - parts[part][0]) for n in (rows, state)]
             + [columns(per, start=tile - gate_parts[gate_part][0])] * shards,
             [columns(rows), whole(shape(1, rows))],
@@ -589,13 +618,13 @@
         )
         outs.append(gated)
         totals.append(total)
-    total = lax.psum(sum(totals), "head")
+    total = [totals[-1]] + [moved(totals[-1], "head", k) for k in range(1, groups)]
     gain = norm_gain.reshape(1, inner)
     return call(
-        functools.partial(normalize, inner * groups),
+        functools.partial(normalize, inner * groups, groups),
         shape(rows, inner),
-        (total, gain, *outs),
-        [pl.BlockSpec((1, ROWS), lambda i: (0, i)), whole(gain)]
+        (*total, gain, *outs),
+        [pl.BlockSpec((1, ROWS), lambda i: (0, i))] * groups + [whole(gain)]
         + [pl.BlockSpec((ROWS, out.shape[1]), lambda i: (i, 0)) for out in outs],
         pl.BlockSpec((ROWS, inner), lambda i: (i, 0)),
         grid=(rows // ROWS,),

time: 175 us -> 161 us (0.920)
  waiting for transfers between devices: 69.2 us -> 55.5 us
  starting transfers between devices: 43.5 us -> 50.9 us
  blocking collectives: 5.68 us -> 0 us
  local copies, waits for them, and re-layouts: 6.19 us -> 2.76 us
    ppermute x18, waiting for transfers between devices: 56.4 us -> 40.3 us  [moved(): lax.ppermute(block, axis, [(i, (i + steps) % count) for i in range(count)])]
    ppermute x18, starting transfers between devices: 34.8 us -> 44.9 us  [moved(): lax.ppermute(block, axis, [(i, (i + steps) % count) for i in range(count)])]
    psum x1 -> x0, blocking collectives: 5.68 us -> none  [body(): total = lax.psum(sum(totals), 'head')]
    unnamed x34 -> x28, local copies, waits for them, and re-layouts: 6.14 us -> 2.66 us
    ppermute x9 -> x6, starting transfers between devices: 8.11 us -> 5.27 us  [body(): lax.ppermute(packed_state(leaving, bound), 'seq', [(step - 1, step)])]
    ppermute x9 -> x6, waiting for transfers between devices: 12.8 us -> 15.2 us  [body(): lax.ppermute(packed_state(leaving, bound), 'seq', [(step - 1, step)])]
    pallas_call x14 -> x12, Pallas kernels: 48.7 us -> 48.3 us  [call(): pl.pallas_call(kernel, grid=grid, in_specs=in_specs, out_specs=out_specs,...]
  transfers between devices with their start and end apart: 29 -> 26, of which waited for: 13 -> 11; matrix products, arithmetic and copies ran while one was open for 1% -> 2% of each run, Pallas kernels for 22% -> 23%
where the time goes in v4:
time: 161 us; the launch traced here: 159 us
  waiting for transfers between devices  55.5 us (34%)
  starting transfers between devices  50.9 us (32%)
  Pallas kernels  48.3 us (30%)
  local copies, waits for them, and re-layouts  2.76 us (2%)
    pallas_call x12, Pallas kernels, call(): pl.pallas_call(kernel, grid=grid, in_specs=in_specs, out_specs=out_specs,...  48.3 us
    ppermute x18, starting transfers between devices, moved(): lax.ppermute(block, axis, [(i, (i + steps) % count) for i in range(count)])  44.9 us
    ppermute x18, waiting for transfers between devices, moved(): lax.ppermute(block, axis, [(i, (i + steps) % count) for i in range(count)])  40.3 us
    ppermute x6, waiting for transfers between devices, body(): lax.ppermute(packed_state(leaving, bound), 'seq', [(step - 1, step)])  15.2 us
    ppermute x6, starting transfers between devices, body(): lax.ppermute(packed_state(leaving, bound), 'seq', [(step - 1, step)])  5.27 us
  transfers between devices with their start and end apart: 26, of which 11 were waited for; matrix products, arithmetic and copies ran while one was open for 2% of the time, Pallas kernels for 23%

profile of v4, /device:TPU:26, one launch (start us, length us, event | category | flops | bytes accessed | tf_op | source)
XLA Modules:
  0.0 159.5 jit_solution(401566844174784650)
XLA Ops:
  0.0 6.1 %shard_map.118 = (bf16[1088,1024]{1,0:T(8,128)(2,1)}, bf16[272,128]{1,0:T(8,128)(2,1)}, bf16[272,128]{1,0:T(8,128)(2,1)}, bf16[272,128]{1,0:T(8,128)(2,1)}, bf16...) custom-call(s32[1,1024]{1,0:T(1,128)} %bitcast.24, ...), custom_call_target="tpu_custom_call" | custom-call | flops 8049999872 | tf_op jit(solution)/shard_map/pallas_call | solution.py:63
  6.1 0.2 collective-permute-start
  6.4 1.7 %collective-permute-start.1 = (bf16[272,128]{1,0:T(8,128)(2,1)}, bf16[272,128]{1,0:T(8,128)(2,1)S(1)}, u32[]{:S(2)}, u32[]{:S(2)}) collective-permute-start(bf16[272,128]{1,0:T(8,128)(2,1)} %get-tuple-element.71), channel_id=1, source_target_pairs={{0,8},{4,12},{8,0},{12,4},{1,9},{5,13},{9,1},{13,5},{2,10},{6,14},... | collective-permute-start | bytes 208904 | tf_op jit(solution)/shard_map/ppermute | solution.py:418
  8.1 0.5 collective-permute-start.2
  8.5 3.4 %collective-permute-start.5 = (bf16[272,512]{1,0:T(8,128)(2,1)}, bf16[272,512]{1,0:T(8,128)(2,1)S(1)}, u32[]{:S(2)}, u32[]{:S(2)}) collective-permute-start(bf16[272,512]{1,0:T(8,128)(2,1)} %get-tuple-element.88), channel_id=1, source_target_pairs={{0,4},{4,8},{8,12},{12,0},{1,5},{5,9},{9,13},{13,1},{2,6},{6,10},{... | collective-permute-start | bytes 835592 | tf_op jit(solution)/shard_map/ppermute | solution.py:418
  11.9 0.9 constant_dynamic-update-slice_fusion.8
  12.8 1.3 collective-permute-start.7
  14.1 1.7 %collective-permute-done.1 = bf16[272,128]{1,0:T(8,128)(2,1)S(1)} collective-permute-done((bf16[272,128]{1,0:T(8,128)(2,1)}, bf16[272,128]{1,0:T(8,128)(2,1)S(1)}, u32[]{:S(2)}, u32[]{:S(2)}) %collective-permute-start.1) | collective-permute-done | bytes 69664 | tf_op jit(solution)/shard_map/ppermute | solution.py:418
  15.8 0.6 collective-permute-start.3
  16.4 1.6 %copy-done.5 = bf16[1088,1024]{1,0:T(8,128)(2,1)S(1)} copy-done((bf16[1088,1024]{1,0:T(8,128)(2,1)S(1)}, bf16[1088,1024]{1,0:T(8,128)(2,1)}, u32[]{:S(2)}) %copy-start.5) | copy-done | bytes 2228248
  18.1 4.5 %shard_map.122 = (bf16[256,768]{1,0:T(8,128)(2,1)S(1)}, bf16[256,768]{1,0:T(8,128)(2,1)S(1)}, bf16[256,768]{1,0:T(8,128)(2,1)S(1)}, bf16[256,768]{1,0:T(8,128)(2...) custom-call(bf16[1088,1024]{1,0:T(8,128)(2,1)S(1)} %copy-done.5, ...), custom_call_target="tpu_custom_call" | custom-call | flops 11500000256 | tf_op jit(solution)/shard_map/pallas_call | solution.py:63
  22.6 0.0 copy-start.9
  22.6 0.0 copy-start.10
  22.6 0.0 copy-start.11
  22.6 0.0 copy-start.3
  22.6 0.0 copy-start.4
  22.7 0.1 collective-permute-start.4
  22.8 2.7 %shard_map.121 = (bf16[272,768]{1,0:T(8,128)(2,1)S(1)}, bf16[272,768]{1,0:T(8,128)(2,1)S(1)}, bf16[272,768]{1,0:T(8,128)(2,1)S(1)}, bf16[272,768]{1,0:T(8,128)(2,1)S(1)}) custom-call(bf16[1088,1024]{1,0:T(8,128)(2,1)S(1)} %copy-done.6, bf16[1024,1280]{1,0:T(8,128)(2,1)S(1)} %copy-done.1), custom_call_target="tpu_custom_call" | custom-call | flops 6899999744 | tf_op jit(solution)/shard_map/pallas_call | solution.py:63
  25.5 0.1 fusion.16.lines_ref
  25.5 13.3 %collective-permute-done.6.refs_2_ = bf16[272,512]{1,0:T(8,128)(2,1)S(1)} collective-permute-done((bf16[272,512]{1,0:T(8,128)(2,1)}, bf16[272,512]{1,0:T(8,128)(2,1)S(1)}, u32[]{:S(2)}, u32[]{:S(2)}) %collective-permute-start.6) | collective-permute-done | bytes 278560 | tf_op jit(solution)/shard_map/ppermute | solution.py:418
  38.9 0.0 copy-start.2
  38.9 2.0 %collective-permute-start.17 = (bf16[272,768]{1,0:T(8,128)(2,1)S(1)}, bf16[272,768]{1,0:T(8,128)(2,1)S(1)}, u32[]{:S(2)}, u32[]{:S(2)}) collective-permute-start(bf16[272,768]{1,0:T(8,128)(2,1)S(1)} %get-tuple-element.115), channel_id=1, source_target_pairs={{0,12},{4,0},{8,4},{12,8},{1,13},{5,1},{9,5},{13,9},{2,14},{6,2},{... | collective-permute-start | bytes 1253384 | tf_op jit(solution)/shard_map/ppermute | solution.py:418
  40.9 6.2 %shard_map.119 = (bf16[1024,1024]{1,0:T(8,128)(2,1)S(1)}, bf16[16,64]{1,0:T(8,128)(2,1)S(1)}, s32[1024,128]{1,0:T(8,128)S(1)}, bf16[1024,256]{1,0:T(8,128)(2,1)S...) custom-call(s32[3]{0:T(128)S(1)} %copy-done.4, ...), custom_call_target="tpu_custom_call" | custom-call | flops 9200000000 | tf_op jit(solution)/shard_map/pallas_call | solution.py:63
  47.2 8.2 %shard_map.120 = (f32[1024,512]{1,0:T(8,128)S(1)}, f32[128,512]{1,0:T(8,128)S(1)}, f32[8,512]{1,0:T(8,128)S(1)}) custom-call(s32[3]{0:T(128)S(1)} %copy-done.4, bf16[1024,1024]{1,0:T(8,128)(2,1)S(1)} %get-tuple-element.73.pick_ref, bf16[16,64]{1,0:T(8,128)(2,1)S(1)} %get-tuple-element.77.rims_ref, s32[1024,128]{1,0:T(8,128)S(1)} %get-tuple-element.78.gap_ref, ...), custom_call_target="tpu_custom_call" | custom-call | flops 11500000256 | tf_op jit(solution)/shard_map/pallas_call | solution.py:63
  55.4 2.5 %collective-permute-done.8.refs_2_ = bf16[272,768]{1,0:T(8,128)(2,1)S(1)} collective-permute-done((bf16[272,768]{1,0:T(8,128)(2,1)S(1)}, bf16[272,768]{1,0:T(8,128)(2,1)S(1)}, u32[]{:S(2)}, u32[]{:S(2)}) %collective-permute-start.8) | collective-permute-done | bytes 417824 | tf_op jit(solution)/shard_map/ppermute | solution.py:418
  58.0 0.7 collective-permute-start.9
  58.7 9.3 %collective-permute-done.12.refs_1_ = bf16[272,768]{1,0:T(8,128)(2,1)S(1)} collective-permute-done((bf16[272,768]{1,0:T(8,128)(2,1)S(1)}, bf16[272,768]{1,0:T(8,128)(2,1)S(1)}, u32[]{:S(2)}, u32[]{:S(2)}) %collective-permute-start.12) | collective-permute-done | bytes 417824 | tf_op jit(solution)/shard_map/ppermute | solution.py:418
  68.0 1.6 %collective-permute-start.13 = (bf16[256,768]{1,0:T(8,128)(2,1)S(1)}, bf16[256,768]{1,0:T(8,128)(2,1)S(1)}, u32[]{:S(2)}, u32[]{:S(2)}) collective-permute-start(bf16[256,768]{1,0:T(8,128)(2,1)S(1)} %get-tuple-element.104), channel_id=1, source_target_pairs={{0,4},{4,8},{8,12},{12,0},{1,5},{5,9},{9,13},{13,1},{2,6},{6,10},{... | collective-permute-start | bytes 1179656 | tf_op jit(solution)/shard_map/ppermute | solution.py:418
  69.6 7.7 %collective-permute-start.15 = (bf16[256,768]{1,0:T(8,128)(2,1)S(1)}, bf16[256,768]{1,0:T(8,128)(2,1)S(1)}, u32[]{:S(2)}, u32[]{:S(2)}) collective-permute-start(bf16[256,768]{1,0:T(8,128)(2,1)S(1)} %get-tuple-element.108), channel_id=1, source_target_pairs={{0,8},{4,12},{8,0},{12,4},{1,9},{5,13},{9,1},{13,5},{2,10},{6,14},... | collective-permute-start | bytes 1179656 | tf_op jit(solution)/shard_map/ppermute | solution.py:418
  77.3 12.0 %shard_map.125 = (f32[1024,768]{1,0:T(8,128)S(1)}, f32[128,768]{1,0:T(8,128)S(1)}, f32[8,768]{1,0:T(8,128)S(1)}) custom-call(s32[3]{0:T(128)S(1)} %copy-done.4, bf16[1024,1024]{1,0:T(8,128)(2,1)S(1)} %get-tuple-element.73.pick_ref, bf16[16,64]{1,0:T(8,128)(2,1)S(1)} %get-tuple-element.77.rims_ref, s32[1024,128]{1,0:T(8,128)S(1)} %get-tuple-element.78.gap_ref, ...), custom_call_target="tpu_custom_call" | custom-call | flops 17250000896 | tf_op jit(solution)/shard_map/pallas_call | solution.py:63
  89.4 0.1 fusion.15
  89.5 0.7 collective-permute-start.10
  90.4 0.1 fusion.11
  90.5 1.3 collective-permute-start.11
  91.8 18.3 %collective-permute-start.14 = (bf16[256,512]{1,0:T(8,128)(2,1)S(1)}, bf16[256,512]{1,0:T(8,128)(2,1)S(1)}, u32[]{:S(2)}, u32[]{:S(2)}) collective-permute-start(bf16[256,512]{1,0:T(8,128)(2,1)S(1)} %get-tuple-element.105), channel_id=1, source_target_pairs={{0,8},{4,12},{8,0},{12,4},{1,9},{5,13},{9,1},{13,5},{2,10},{6,14},... | collective-permute-start | bytes 786440 | tf_op jit(solution)/shard_map/ppermute | solution.py:418
  110.2 1.7 %collective-permute-start.16 = (bf16[256,768]{1,0:T(8,128)(2,1)S(1)}, bf16[256,768]{1,0:T(8,128)(2,1)S(1)}, u32[]{:S(2)}, u32[]{:S(2)}) collective-permute-start(bf16[256,768]{1,0:T(8,128)(2,1)S(1)} %get-tuple-element.110), channel_id=1, source_target_pairs={{0,12},{4,0},{8,4},{12,8},{1,13},{5,1},{9,5},{13,9},{2,14},{6,2},{... | collective-permute-start | bytes 1179656 | tf_op jit(solution)/shard_map/ppermute | solution.py:418
  111.9 0.1 pad_maximum_fusion
  112.0 0.7 collective-permute-start.18
  112.7 3.8 %collective-permute-done.11 = f16[136,512]{1,0:T(8,128)(2,1)S(1)} collective-permute-done((f16[136,512]{1,0:T(8,128)(2,1)S(1)}, f16[136,512]{1,0:T(8,128)(2,1)S(1)}, u32[]{:S(2)}, u32[]{:S(2)}) %collective-permute-start.11) | collective-permute-done | bytes 139296 | tf_op jit(solution)/shard_map/ppermute | solution.py:597
  116.6 0.1 fusion.7
  116.7 0.1 pad_maximum_fusion.1
  116.8 0.7 collective-permute-start.19
  117.5 11.4 %collective-permute-done.14.refs_2_ = bf16[256,512]{1,0:T(8,128)(2,1)S(1)} collective-permute-done((bf16[256,512]{1,0:T(8,128)(2,1)S(1)}, bf16[256,512]{1,0:T(8,128)(2,1)S(1)}, u32[]{:S(2)}, u32[]{:S(2)}) %collective-permute-start.14) | collective-permute-done | bytes 262176 | tf_op jit(solution)/shard_map/ppermute | solution.py:418
  128.9 0.8 collective-permute-done.16.refs_3_
  129.7 3.6 %collective-permute-start.21 = (bf16[256,512]{1,0:T(8,128)(2,1)S(1)}, bf16[256,512]{1,0:T(8,128)(2,1)S(1)}, u32[]{:S(2)}, u32[]{:S(2)}) collective-permute-start(bf16[256,512]{1,0:T(8,128)(2,1)S(1)} %get-tuple-element.123), channel_id=1, source_target_pairs={{0,4},{4,8},{8,12},{12,0},{1,5},{5,9},{9,13},{13,1},{2,6},{6,10},{... | collective-permute-start | bytes 786440 | tf_op jit(solution)/shard_map/ppermute | solution.py:418
  133.3 1.2 shard_map.123
  134.6 0.1 fusion.27
  134.7 0.1 fusion.3
  134.8 0.1 pad_maximum_fusion.2
  134.9 1.3 collective-permute-start.20
  136.2 1.2 shard_map.124
  137.4 11.4 %collective-permute-done.20 = f16[136,768]{1,0:T(8,128)(2,1)S(1)} collective-permute-done((f16[136,768]{1,0:T(8,128)(2,1)S(1)}, f16[136,768]{1,0:T(8,128)(2,1)S(1)}, u32[]{:S(2)}, u32[]{:S(2)}) %collective-permute-start.20) | collective-permute-done | bytes 208928 | tf_op jit(solution)/shard_map/ppermute | solution.py:597
  148.9 0.1 add_convert_fusion
  149.0 1.2 shard_map.126
  150.3 1.2 shard_map.127
  151.5 0.0 copy-start.8
  151.5 1.3 shard_map.128
  152.8 0.1 collective-permute-start.23
  152.9 1.5 collective-permute-start.24
  154.4 1.4 collective-permute-start.25
  155.8 0.1 collective-permute-done.23.refs_1_
  155.9 0.7 collective-permute-done.24.refs_2_
  156.5 0.5 collective-permute-done.25.refs_3_
  157.1 2.4 %shard_map.129 = bf16[1024,1280]{1,0:T(8,128)(2,1)} custom-call(f32[1,1024]{1,0:T(1,128)S(1)} %get-tuple-element.127.refs_0_, f32[1,1024]{1,0:T(1,128)S(1)} %collective-permute-done.23.refs_1_, f32[1,1024]{1,0:T(1,128)S(1)} %collective-permute-done.24.refs_2_, f32[1,1024]{1,0:T(1,128)S(1)} %collective-permute-done.25.refs_3_, f32[1,1280]{1,0:T(1,128)S(1)} %reshape.7.refs_4_, ...), custom_call_target="tpu_custom_call" | custom-call | flops 5750000128 | tf_op jit(solution)/shard_map/pallas_call | solution.py:63
  (72 shorter events, 1.0 us)
Async XLA Ops:
  0.0 16.4 %copy-start = (bf16[1024,1280]{1,0:T(8,128)(2,1)S(1)}, bf16[1024,1280]{1,0:T(8,128)(2,1)}, u32[]{:S(2)}) copy-start(bf16[1024,1280]{1,0:T(8,128)(2,1)} %x_ref.5) | copy-start | bytes 7864324
  6.1 6.7 %collective-permute-start = (bf16[272,128]{1,0:T(8,128)(2,1)}, bf16[272,128]{1,0:T(8,128)(2,1)S(1)}, u32[]{:S(2)}, u32[]{:S(2)}) collective-permute-start(bf16[272,128]{1,0:T(8,128)(2,1)} %get-tuple-element.70), channel_id=1, source_target_pairs={{0,4},{4,8},{8,12},{12,0},{1,5},{5,9},{9,13},{13,1},{2,6},{6,10},{... | collective-permute-start | bytes 208904 | tf_op jit(solution)/shard_map/ppermute | solution.py:418
  6.4 9.4 %collective-permute-start.1 = (bf16[272,128]{1,0:T(8,128)(2,1)}, bf16[272,128]{1,0:T(8,128)(2,1)S(1)}, u32[]{:S(2)}, u32[]{:S(2)}) collective-permute-start(bf16[272,128]{1,0:T(8,128)(2,1)} %get-tuple-element.71), channel_id=1, source_target_pairs={{0,8},{4,12},{8,0},{12,4},{1,9},{5,13},{9,1},{13,5},{2,10},{6,14},... | collective-permute-start | bytes 208904 | tf_op jit(solution)/shard_map/ppermute | solution.py:418
  8.1 7.7 %collective-permute-start.2 = (bf16[272,128]{1,0:T(8,128)(2,1)}, bf16[272,128]{1,0:T(8,128)(2,1)S(1)}, u32[]{:S(2)}, u32[]{:S(2)}) collective-permute-start(bf16[272,128]{1,0:T(8,128)(2,1)} %get-tuple-element.72), channel_id=1, source_target_pairs={{0,12},{4,0},{8,4},{12,8},{1,13},{5,1},{9,5},{13,9},{2,14},{6,2},{... | collective-permute-start | bytes 208904 | tf_op jit(solution)/shard_map/ppermute | solution.py:418
  8.5 30.4 %collective-permute-start.5 = (bf16[272,512]{1,0:T(8,128)(2,1)}, bf16[272,512]{1,0:T(8,128)(2,1)S(1)}, u32[]{:S(2)}, u32[]{:S(2)}) collective-permute-start(bf16[272,512]{1,0:T(8,128)(2,1)} %get-tuple-element.88), channel_id=1, source_target_pairs={{0,4},{4,8},{8,12},{12,0},{1,5},{5,9},{9,13},{13,1},{2,6},{6,10},{... | collective-permute-start | bytes 835592 | tf_op jit(solution)/shard_map/ppermute | solution.py:418
  11.9 27.0 %collective-permute-start.6 = (bf16[272,512]{1,0:T(8,128)(2,1)}, bf16[272,512]{1,0:T(8,128)(2,1)S(1)}, u32[]{:S(2)}, u32[]{:S(2)}) collective-permute-start(bf16[272,512]{1,0:T(8,128)(2,1)} %get-tuple-element.89), channel_id=1, source_target_pairs={{0,8},{4,12},{8,0},{12,4},{1,9},{5,13},{9,1},{13,5},{2,10},{6,14},... | collective-permute-start | bytes 835592 | tf_op jit(solution)/shard_map/ppermute | solution.py:418
  12.8 26.1 %collective-permute-start.7 = (bf16[272,512]{1,0:T(8,128)(2,1)}, bf16[272,512]{1,0:T(8,128)(2,1)S(1)}, u32[]{:S(2)}, u32[]{:S(2)}) collective-permute-start(bf16[272,512]{1,0:T(8,128)(2,1)} %get-tuple-element.90), channel_id=1, source_target_pairs={{0,12},{4,0},{8,4},{12,8},{1,13},{5,1},{9,5},{13,9},{2,14},{6,2},{... | collective-permute-start | bytes 835592 | tf_op jit(solution)/shard_map/ppermute | solution.py:418
  15.8 6.7 %collective-permute-start.3 = (bf16[1088,128]{1,0:T(8,128)(2,1)S(1)}, bf16[1088,128]{1,0:T(8,128)(2,1)S(1)}, u32[]{:S(2)}, u32[]{:S(2)}) collective-permute-start(bf16[1088,128]{1,0:T(8,128)(2,1)S(1)} %get-tuple-element.152.first_ref), channel_id=1, source_target_pairs={{0,2},{1,3},{2,0},{3,1},{4,6},{5,7},{6,4},{7,5},{8,10},{9,11},{10,... | collective-permute-start | bytes 835592 | tf_op jit(solution)/shard_map/ppermute | solution.py:482
  16.4 1.6 %copy-start.5 = (bf16[1088,1024]{1,0:T(8,128)(2,1)S(1)}, bf16[1088,1024]{1,0:T(8,128)(2,1)}, u32[]{:S(2)}) copy-start(bf16[1088,1024]{1,0:T(8,128)(2,1)} %get-tuple-element.93.pick_ref) | copy-start | bytes 6684676
  18.1 4.7 %copy-start.1 = (bf16[1024,1280]{1,0:T(8,128)(2,1)S(1)}, bf16[1024,1280]{1,0:T(8,128)(2,1)}, u32[]{:S(2)}) copy-start(bf16[1024,1280]{1,0:T(8,128)(2,1)} %x_ref.4) | copy-start | bytes 7864324
  18.1 4.7 %copy-start.6 = (bf16[1088,1024]{1,0:T(8,128)(2,1)S(1)}, bf16[1088,1024]{1,0:T(8,128)(2,1)}, u32[]{:S(2)}) copy-start(bf16[1088,1024]{1,0:T(8,128)(2,1)} %get-tuple-element.93.pick_ref) | copy-start | bytes 6684676
  22.6 2.8 %copy-start.9 = (f32[16]{0:T(128)S(1)}, f32[16]{0:T(128)}, u32[]{:S(2)}) copy-start(f32[16]{0:T(128)} %param.22) | copy-start | bytes 196
  22.6 2.8 %copy-start.10 = (f32[16]{0:T(128)S(1)}, f32[16]{0:T(128)}, u32[]{:S(2)}) copy-start(f32[16]{0:T(128)} %param.20) | copy-start | bytes 196
  22.6 2.8 %copy-start.11 = (f32[16]{0:T(128)S(1)}, f32[16]{0:T(128)}, u32[]{:S(2)}) copy-start(f32[16]{0:T(128)} %param.21) | copy-start | bytes 196
  22.6 18.3 %copy-start.3 = (f32[4,256]{1,0:T(4,128)S(1)}, f32[4,256]{1,0:T(4,128)}, u32[]{:S(2)}) copy-start(f32[4,256]{1,0:T(4,128)} %taps_ref.3) | copy-start | bytes 12292
  22.6 18.3 %copy-start.4 = (s32[3]{0:T(128)S(1)}, s32[3]{0:T(128)}, u32[]{:S(2)}) copy-start(s32[3]{0:T(128)} %lengths.5) | copy-start | bytes 40
  22.7 18.2 %collective-permute-start.4 = (bf16[2176,128]{1,0:T(8,128)(2,1)S(1)}, bf16[2176,128]{1,0:T(8,128)(2,1)S(1)}, u32[]{:S(2)}, u32[]{:S(2)}) collective-permute-start(bf16[2176,128]{1,0:T(8,128)(2,1)S(1)} %constant_dynamic-update-slice_fusion.4), channel_id=1, source_target_pairs={{0,1},{1,0},{2,3},{3,2},{4,5},{5,4},{6,7},{7,6},{8,9},{9,8},{10,11... | collective-permute-start | bytes 1671176 | tf_op jit(solution)/shard_map/ppermute | solution.py:482
  38.9 19.1 %collective-permute-start.8 = (bf16[272,768]{1,0:T(8,128)(2,1)S(1)}, bf16[272,768]{1,0:T(8,128)(2,1)S(1)}, u32[]{:S(2)}, u32[]{:S(2)}) collective-permute-start(bf16[272,768]{1,0:T(8,128)(2,1)S(1)} %get-tuple-element.97), channel_id=1, source_target_pairs={{0,8},{4,12},{8,0},{12,4},{1,9},{5,13},{9,1},{13,5},{2,10},{6,14},... | collective-permute-start | bytes 1253384 | tf_op jit(solution)/shard_map/ppermute | solution.py:418
  38.9 29.1 %collective-permute-start.12 = (bf16[272,768]{1,0:T(8,128)(2,1)S(1)}, bf16[272,768]{1,0:T(8,128)(2,1)S(1)}, u32[]{:S(2)}, u32[]{:S(2)}) collective-permute-start(bf16[272,768]{1,0:T(8,128)(2,1)S(1)} %get-tuple-element.103), channel_id=1, source_target_pairs={{0,4},{4,8},{8,12},{12,0},{1,5},{5,9},{9,13},{13,1},{2,6},{6,10},{... | collective-permute-start | bytes 1253384 | tf_op jit(solution)/shard_map/ppermute | solution.py:418
  38.9 8.3 %copy-start.2 = (f32[4,1280]{1,0:T(4,128)S(1)}, f32[4,1280]{1,0:T(4,128)}, u32[]{:S(2)}) copy-start(f32[4,1280]{1,0:T(4,128)} %taps_ref.5) | copy-start | bytes 61444
  38.9 8.3 %copy-start.7 = (bf16[272,512]{1,0:T(8,128)(2,1)S(1)}, bf16[272,512]{1,0:T(8,128)(2,1)}, u32[]{:S(2)}) copy-start(bf16[272,512]{1,0:T(8,128)(2,1)} %get-tuple-element.87.refs_0_) | copy-start | bytes 835588
  38.9 38.4 %collective-permute-start.17 = (bf16[272,768]{1,0:T(8,128)(2,1)S(1)}, bf16[272,768]{1,0:T(8,128)(2,1)S(1)}, u32[]{:S(2)}, u32[]{:S(2)}) collective-permute-start(bf16[272,768]{1,0:T(8,128)(2,1)S(1)} %get-tuple-element.115), channel_id=1, source_target_pairs={{0,12},{4,0},{8,4},{12,8},{1,13},{5,1},{9,5},{13,9},{2,14},{6,2},{... | collective-permute-start | bytes 1253384 | tf_op jit(solution)/shard_map/ppermute | solution.py:418
  58.0 31.3 %collective-permute-start.9 = (f16[136,512]{1,0:T(8,128)(2,1)S(1)}, f16[136,512]{1,0:T(8,128)(2,1)S(1)}, u32[]{:S(2)}, u32[]{:S(2)}) collective-permute-start(f16[136,512]{1,0:T(8,128)(2,1)S(1)} %pad_maximum_fusion.3), channel_id=1, source_target_pairs={{0,4},{1,5},{2,6},{3,7},{16,20},{17,21},{18,22},{19,23}} | collective-permute-start | bytes 417800 | tf_op jit(solution)/shard_map/ppermute | solution.py:597
  68.0 23.8 %collective-permute-start.13 = (bf16[256,768]{1,0:T(8,128)(2,1)S(1)}, bf16[256,768]{1,0:T(8,128)(2,1)S(1)}, u32[]{:S(2)}, u32[]{:S(2)}) collective-permute-start(bf16[256,768]{1,0:T(8,128)(2,1)S(1)} %get-tuple-element.104), channel_id=1, source_target_pairs={{0,4},{4,8},{8,12},{12,0},{1,5},{5,9},{9,13},{13,1},{2,6},{6,10},{... | collective-permute-start | bytes 1179656 | tf_op jit(solution)/shard_map/ppermute | solution.py:418
  69.6 40.5 %collective-permute-start.15 = (bf16[256,768]{1,0:T(8,128)(2,1)S(1)}, bf16[256,768]{1,0:T(8,128)(2,1)S(1)}, u32[]{:S(2)}, u32[]{:S(2)}) collective-permute-start(bf16[256,768]{1,0:T(8,128)(2,1)S(1)} %get-tuple-element.108), channel_id=1, source_target_pairs={{0,8},{4,12},{8,0},{12,4},{1,9},{5,13},{9,1},{13,5},{2,10},{6,14},... | collective-permute-start | bytes 1179656 | tf_op jit(solution)/shard_map/ppermute | solution.py:418
  89.5 0.7 collective-permute-start.10
  90.5 25.9 %collective-permute-start.11 = (f16[136,512]{1,0:T(8,128)(2,1)S(1)}, f16[136,512]{1,0:T(8,128)(2,1)S(1)}, u32[]{:S(2)}, u32[]{:S(2)}) collective-permute-start(f16[136,512]{1,0:T(8,128)(2,1)S(1)} %pad_maximum_fusion.5), channel_id=1, source_target_pairs={{8,12},{9,13},{10,14},{11,15},{24,28},{25,29},{26,30},{27,31}} | collective-permute-start | bytes 417800 | tf_op jit(solution)/shard_map/ppermute | solution.py:597
  91.8 37.1 %collective-permute-start.14 = (bf16[256,512]{1,0:T(8,128)(2,1)S(1)}, bf16[256,512]{1,0:T(8,128)(2,1)S(1)}, u32[]{:S(2)}, u32[]{:S(2)}) collective-permute-start(bf16[256,512]{1,0:T(8,128)(2,1)S(1)} %get-tuple-element.105), channel_id=1, source_target_pairs={{0,8},{4,12},{8,0},{12,4},{1,9},{5,13},{9,1},{13,5},{2,10},{6,14},... | collective-permute-start | bytes 786440 | tf_op jit(solution)/shard_map/ppermute | solution.py:418
  110.2 19.6 %collective-permute-start.16 = (bf16[256,768]{1,0:T(8,128)(2,1)S(1)}, bf16[256,768]{1,0:T(8,128)(2,1)S(1)}, u32[]{:S(2)}, u32[]{:S(2)}) collective-permute-start(bf16[256,768]{1,0:T(8,128)(2,1)S(1)} %get-tuple-element.110), channel_id=1, source_target_pairs={{0,12},{4,0},{8,4},{12,8},{1,13},{5,1},{9,5},{13,9},{2,14},{6,2},{... | collective-permute-start | bytes 1179656 | tf_op jit(solution)/shard_map/ppermute | solution.py:418
  112.0 4.5 %collective-permute-start.18 = (f16[136,768]{1,0:T(8,128)(2,1)S(1)}, f16[136,768]{1,0:T(8,128)(2,1)S(1)}, u32[]{:S(2)}, u32[]{:S(2)}) collective-permute-start(f16[136,768]{1,0:T(8,128)(2,1)S(1)} %pad_maximum_fusion), channel_id=1, source_target_pairs={{0,4},{1,5},{2,6},{3,7},{16,20},{17,21},{18,22},{19,23}} | collective-permute-start | bytes 626696 | tf_op jit(solution)/shard_map/ppermute | solution.py:597
  116.8 17.8 %collective-permute-start.19 = (f16[136,768]{1,0:T(8,128)(2,1)S(1)}, f16[136,768]{1,0:T(8,128)(2,1)S(1)}, u32[]{:S(2)}, u32[]{:S(2)}) collective-permute-start(f16[136,768]{1,0:T(8,128)(2,1)S(1)} %pad_maximum_fusion.1), channel_id=1, source_target_pairs={{4,8},{5,9},{6,10},{7,11},{20,24},{21,25},{22,26},{23,27}} | collective-permute-start | bytes 626696 | tf_op jit(solution)/shard_map/ppermute | solution.py:597
  128.9 21.4 %collective-permute-start.22 = (bf16[256,512]{1,0:T(8,128)(2,1)S(1)}, bf16[256,512]{1,0:T(8,128)(2,1)S(1)}, u32[]{:S(2)}, u32[]{:S(2)}) collective-permute-start(bf16[256,512]{1,0:T(8,128)(2,1)S(1)} %get-tuple-element.125), channel_id=1, source_target_pairs={{0,12},{4,0},{8,4},{12,8},{1,13},{5,1},{9,5},{13,9},{2,14},{6,2},{... | collective-permute-start | bytes 786440 | tf_op jit(solution)/shard_map/ppermute | solution.py:418
  129.7 20.6 %collective-permute-start.21 = (bf16[256,512]{1,0:T(8,128)(2,1)S(1)}, bf16[256,512]{1,0:T(8,128)(2,1)S(1)}, u32[]{:S(2)}, u32[]{:S(2)}) collective-permute-start(bf16[256,512]{1,0:T(8,128)(2,1)S(1)} %get-tuple-element.123), channel_id=1, source_target_pairs={{0,4},{4,8},{8,12},{12,0},{1,5},{5,9},{9,13},{13,1},{2,6},{6,10},{... | collective-permute-start | bytes 786440 | tf_op jit(solution)/shard_map/ppermute | solution.py:418
  134.9 14.0 %collective-permute-start.20 = (f16[136,768]{1,0:T(8,128)(2,1)S(1)}, f16[136,768]{1,0:T(8,128)(2,1)S(1)}, u32[]{:S(2)}, u32[]{:S(2)}) collective-permute-start(f16[136,768]{1,0:T(8,128)(2,1)S(1)} %pad_maximum_fusion.2), channel_id=1, source_target_pairs={{8,12},{9,13},{10,14},{11,15},{24,28},{25,29},{26,30},{27,31}} | collective-permute-start | bytes 626696 | tf_op jit(solution)/shard_map/ppermute | solution.py:597
  151.5 4.2 %copy-start.8 = (f32[1280]{0:T(1024)S(1)}, f32[1280]{0:T(1024)}, u32[]{:S(2)}) copy-start(f32[1280]{0:T(1024)} %param.23) | copy-start | bytes 15364
  152.8 3.1 %collective-permute-start.23 = (f32[1,1024]{1,0:T(1,128)S(1)}, f32[1,1024]{1,0:T(1,128)S(1)}, u32[]{:S(2)}, u32[]{:S(2)}) collective-permute-start(f32[1,1024]{1,0:T(1,128)S(1)} %get-tuple-element.127.refs_0_), channel_id=1, source_target_pairs={{0,1},{1,2},{2,3},{3,0},{4,5},{5,6},{6,7},{7,4},{8,9},{9,10},{10,1... | collective-permute-start | bytes 12296 | tf_op jit(solution)/shard_map/ppermute | solution.py:418
  152.9 3.7 %collective-permute-start.24 = (f32[1,1024]{1,0:T(1,128)S(1)}, f32[1,1024]{1,0:T(1,128)S(1)}, u32[]{:S(2)}, u32[]{:S(2)}) collective-permute-start(f32[1,1024]{1,0:T(1,128)S(1)} %get-tuple-element.127.refs_0_), channel_id=1, source_target_pairs={{0,2},{1,3},{2,0},{3,1},{4,6},{5,7},{6,4},{7,5},{8,10},{9,11},{10,... | collective-permute-start | bytes 12296 | tf_op jit(solution)/shard_map/ppermute | solution.py:418
  154.4 2.7 %collective-permute-start.25 = (f32[1,1024]{1,0:T(1,128)S(1)}, f32[1,1024]{1,0:T(1,128)S(1)}, u32[]{:S(2)}, u32[]{:S(2)}) collective-permute-start(f32[1,1024]{1,0:T(1,128)S(1)} %get-tuple-element.127.refs_0_), channel_id=1, source_target_pairs={{0,3},{1,0},{2,1},{3,2},{4,7},{5,4},{6,5},{7,6},{8,11},{9,8},{10,9... | collective-permute-start | bytes 12296 | tf_op jit(solution)/shard_map/ppermute | solution.py:418

commit v5 on v4

--- a/solution.py
+++ b/solution.py
@@ -473,7 +473,18 @@
     )
     picks, small, x_send = sent[0], sent[1 : 1 + shards], [sent[1 + shards :]]
     small = [small[0]] + [moved(small[k], "seq", k) for k in range(1, shards)]
-    arrived = [[x_send[0][0]] + [moved(x_send[0][k], "seq", k) for k in range(1, shards)]]
+    distances = list(range(shards - 1, 0, -1))
+    started = []
+
+    def queued(send, *others):
+        received = [send[0]] + [None] * (shards - 1)
+        for k in distances:
+            waits = [started[-WINDOW]] if len(started) >= shards - 1 else []
+            received[k] = moved(after(send[k], *waits, *others), "seq", k)
+            started.append(received[k])
+        return received
+
+    arrived = [queued(x_send[0])]
 
     small = [jnp.concatenate(small, 0)]
     mask = groups // 2
@@ -540,15 +551,8 @@
         micros=8,
     )
 
-    distances = sorted(range(1, shards), key=lambda k: (abs(2 * k - shards), k))
-
-    def stream(send, before, *others):
-        return [send[0]] + [
-            moved(after(send[k], before[k], *others), "seq", k) for k in range(1, shards)
-        ]
-
     if len(parts) > 1:
-        arrived.append(stream(x_send[1], arrived[0], gate_send[0][0], x_send[-1][0]))
+        arrived.append(queued(x_send[1], gate_send[0][0], x_send[-1][0]))
 
     scans, ends, states, gates = [], [], [], []
     for number, part in enumerate(parts):
@@ -576,15 +580,9 @@
         scans.append(scanned)
         ends.append(local_state)
         if number + 2 < len(parts):
-            arrived.append(stream(x_send[number + 2], arrived[number + 1], local_state))
+            arrived.append(queued(x_send[number + 2], local_state))
         if not gates and number + 2 >= len(parts):
-            started = [(arrived[-1][k], local_state) for k in distances[:WINDOW]]
-            for send in gate_send:
-                gates.append([send[0]] + [None] * (shards - 1))
-                for k in distances:
-                    block = moved(after(send[k], *started[-WINDOW]), "seq", k)
-                    gates[-1][k] = block
-                    started.append((block,))
+            gates = [queued(send, local_state) for send in gate_send]
         following = (arrived + gates)[number + 1][distances[0]]
         local_state = after(local_state, following)
         passing = rest[0:1, first * TILE : last * TILE]

time: 161 us -> 155 us (0.963)
  starting transfers between devices: 50.9 us -> 32.9 us
  waiting for transfers between devices: 55.5 us -> 67.2 us
    ppermute x18, starting transfers between devices: 44.9 us -> 26.8 us  [moved(): lax.ppermute(block, axis, [(i, (i + steps) % count) for i in range(count)])]
    ppermute x6, waiting for transfers between devices: 15.2 us -> 25.2 us  [body(): lax.ppermute(packed_state(leaving, bound), 'seq', [(step - 1, step)])]
    ppermute x18, waiting for transfers between devices: 40.3 us -> 42 us  [moved(): lax.ppermute(block, axis, [(i, (i + steps) % count) for i in range(count)])]
  transfers between devices with their start and end apart: 26 -> 26, of which waited for: 11 -> 10; matrix products, arithmetic and copies ran while one was open for 2% -> 2% of each run, Pallas kernels for 23% -> 24%
where the time goes in v5:
time: 155 us; the launch traced here: 153 us
  waiting for transfers between devices  67.2 us (43%)
  Pallas kernels  48.4 us (31%)
  starting transfers between devices  32.9 us (21%)
  local copies, waits for them, and re-layouts  2.76 us (2%)
    pallas_call x12, Pallas kernels, call(): pl.pallas_call(kernel, grid=grid, in_specs=in_specs, out_specs=out_specs,...  48.4 us
    ppermute x18, waiting for transfers between devices, moved(): lax.ppermute(block, axis, [(i, (i + steps) % count) for i in range(count)])  42 us
    ppermute x18, starting transfers between devices, moved(): lax.ppermute(block, axis, [(i, (i + steps) % count) for i in range(count)])  26.8 us
    ppermute x6, waiting for transfers between devices, body(): lax.ppermute(packed_state(leaving, bound), 'seq', [(step - 1, step)])  25.2 us
    ppermute x6, starting transfers between devices, body(): lax.ppermute(packed_state(leaving, bound), 'seq', [(step - 1, step)])  5.49 us
  transfers between devices with their start and end apart: 26, of which 10 were waited for; matrix products, arithmetic and copies ran while one was open for 2% of the time, Pallas kernels for 24%

profile of v5, /device:TPU:26, one launch (start us, length us, event | category | flops | bytes accessed | tf_op | source)
XLA Modules:
  0.0 153.4 jit_solution(17204667526085068354)
XLA Ops:
  0.0 6.1 %shard_map.118 = (bf16[1088,1024]{1,0:T(8,128)(2,1)}, bf16[272,128]{1,0:T(8,128)(2,1)}, bf16[272,128]{1,0:T(8,128)(2,1)}, bf16[272,128]{1,0:T(8,128)(2,1)}, bf16...) custom-call(s32[1,1024]{1,0:T(1,128)} %bitcast.24, ...), custom_call_target="tpu_custom_call" | custom-call | flops 8049999872 | tf_op jit(solution)/shard_map/pallas_call | solution.py:63
  6.1 0.2 collective-permute-start
  6.4 1.7 %collective-permute-start.1 = (bf16[272,128]{1,0:T(8,128)(2,1)}, bf16[272,128]{1,0:T(8,128)(2,1)S(1)}, u32[]{:S(2)}, u32[]{:S(2)}) collective-permute-start(bf16[272,128]{1,0:T(8,128)(2,1)} %get-tuple-element.71), channel_id=1, source_target_pairs={{0,8},{4,12},{8,0},{12,4},{1,9},{5,13},{9,1},{13,5},{2,10},{6,14},... | collective-permute-start | bytes 208904 | tf_op jit(solution)/shard_map/ppermute | solution.py:418
  8.1 0.5 collective-permute-start.2
  8.5 3.4 %collective-permute-start.5 = (bf16[272,512]{1,0:T(8,128)(2,1)}, bf16[272,512]{1,0:T(8,128)(2,1)S(1)}, u32[]{:S(2)}, u32[]{:S(2)}) collective-permute-start(bf16[272,512]{1,0:T(8,128)(2,1)} %get-tuple-element.88), channel_id=1, source_target_pairs={{0,4},{4,8},{8,12},{12,0},{1,5},{5,9},{9,13},{13,1},{2,6},{6,10},{... | collective-permute-start | bytes 835592 | tf_op jit(solution)/shard_map/ppermute | solution.py:418
  11.9 0.9 constant_dynamic-update-slice_fusion.8
  12.8 1.3 collective-permute-start.7
  14.1 1.7 %collective-permute-done.1 = bf16[272,128]{1,0:T(8,128)(2,1)S(1)} collective-permute-done((bf16[272,128]{1,0:T(8,128)(2,1)}, bf16[272,128]{1,0:T(8,128)(2,1)S(1)}, u32[]{:S(2)}, u32[]{:S(2)}) %collective-permute-start.1) | collective-permute-done | bytes 69664 | tf_op jit(solution)/shard_map/ppermute | solution.py:418
  15.8 0.6 collective-permute-start.3
  16.4 1.6 %copy-done.5 = bf16[1088,1024]{1,0:T(8,128)(2,1)S(1)} copy-done((bf16[1088,1024]{1,0:T(8,128)(2,1)S(1)}, bf16[1088,1024]{1,0:T(8,128)(2,1)}, u32[]{:S(2)}) %copy-start.5) | copy-done | bytes 2228248
  18.1 4.5 %shard_map.122 = (bf16[256,768]{1,0:T(8,128)(2,1)S(1)}, bf16[256,768]{1,0:T(8,128)(2,1)S(1)}, bf16[256,768]{1,0:T(8,128)(2,1)S(1)}, bf16[256,768]{1,0:T(8,128)(2...) custom-call(bf16[1088,1024]{1,0:T(8,128)(2,1)S(1)} %copy-done.5, ...), custom_call_target="tpu_custom_call" | custom-call | flops 11500000256 | tf_op jit(solution)/shard_map/pallas_call | solution.py:63
  22.6 0.0 copy-start.9
  22.7 0.0 copy-start.10
  22.7 0.0 copy-start.11
  22.7 0.0 copy-start.3
  22.7 0.0 copy-start.4
  22.7 0.1 collective-permute-start.4
  22.8 2.7 %shard_map.121 = (bf16[272,768]{1,0:T(8,128)(2,1)S(1)}, bf16[272,768]{1,0:T(8,128)(2,1)S(1)}, bf16[272,768]{1,0:T(8,128)(2,1)S(1)}, bf16[272,768]{1,0:T(8,128)(2,1)S(1)}) custom-call(bf16[1088,1024]{1,0:T(8,128)(2,1)S(1)} %copy-done.6, bf16[1024,1280]{1,0:T(8,128)(2,1)S(1)} %copy-done.1), custom_call_target="tpu_custom_call" | custom-call | flops 6899999744 | tf_op jit(solution)/shard_map/pallas_call | solution.py:63
  25.5 0.1 fusion.16.lines_ref
  25.6 13.3 %collective-permute-done.6.refs_2_ = bf16[272,512]{1,0:T(8,128)(2,1)S(1)} collective-permute-done((bf16[272,512]{1,0:T(8,128)(2,1)}, bf16[272,512]{1,0:T(8,128)(2,1)S(1)}, u32[]{:S(2)}, u32[]{:S(2)}) %collective-permute-start.6) | collective-permute-done | bytes 278560 | tf_op jit(solution)/shard_map/ppermute | solution.py:418
  38.9 0.0 collective-permute-start.8
  38.9 0.1 collective-permute-start.15
  39.0 6.2 %shard_map.119 = (bf16[1024,1024]{1,0:T(8,128)(2,1)S(1)}, bf16[16,64]{1,0:T(8,128)(2,1)S(1)}, s32[1024,128]{1,0:T(8,128)S(1)}, bf16[1024,256]{1,0:T(8,128)(2,1)S...) custom-call(s32[3]{0:T(128)S(1)} %copy-done.4, ...), custom_call_target="tpu_custom_call" | custom-call | flops 9200000000 | tf_op jit(solution)/shard_map/pallas_call | solution.py:63
  45.2 8.2 %shard_map.120 = (f32[1024,512]{1,0:T(8,128)S(1)}, f32[128,512]{1,0:T(8,128)S(1)}, f32[8,512]{1,0:T(8,128)S(1)}) custom-call(s32[3]{0:T(128)S(1)} %copy-done.4, bf16[1024,1024]{1,0:T(8,128)(2,1)S(1)} %get-tuple-element.73.pick_ref, bf16[16,64]{1,0:T(8,128)(2,1)S(1)} %get-tuple-element.77.rims_ref, s32[1024,128]{1,0:T(8,128)S(1)} %get-tuple-element.78.gap_ref, ...), custom_call_target="tpu_custom_call" | custom-call | flops 11500000256 | tf_op jit(solution)/shard_map/pallas_call | solution.py:63
  53.6 0.7 collective-permute-start.9
  54.3 5.7 %collective-permute-start.12 = (bf16[272,768]{1,0:T(8,128)(2,1)S(1)}, bf16[272,768]{1,0:T(8,128)(2,1)S(1)}, u32[]{:S(2)}, u32[]{:S(2)}) collective-permute-start(bf16[272,768]{1,0:T(8,128)(2,1)S(1)} %get-tuple-element.103), channel_id=1, source_target_pairs={{0,4},{4,8},{8,12},{12,0},{1,5},{5,9},{9,13},{13,1},{2,6},{6,10},{... | collective-permute-start | bytes 1253384 | tf_op jit(solution)/shard_map/ppermute | solution.py:418
  59.9 9.7 %collective-permute-done.15.refs_2_ = bf16[272,768]{1,0:T(8,128)(2,1)S(1)} collective-permute-done((bf16[272,768]{1,0:T(8,128)(2,1)S(1)}, bf16[272,768]{1,0:T(8,128)(2,1)S(1)}, u32[]{:S(2)}, u32[]{:S(2)}) %collective-permute-start.15) | collective-permute-done | bytes 417824 | tf_op jit(solution)/shard_map/ppermute | solution.py:418
  69.6 5.8 %collective-permute-start.16 = (bf16[256,768]{1,0:T(8,128)(2,1)S(1)}, bf16[256,768]{1,0:T(8,128)(2,1)S(1)}, u32[]{:S(2)}, u32[]{:S(2)}) collective-permute-start(bf16[256,768]{1,0:T(8,128)(2,1)S(1)} %get-tuple-element.111), channel_id=1, source_target_pairs={{0,12},{4,0},{8,4},{12,8},{1,13},{5,1},{9,5},{13,9},{2,14},{6,2},{... | collective-permute-start | bytes 1179656 | tf_op jit(solution)/shard_map/ppermute | solution.py:418
  75.6 0.1 fusion.15
  75.7 0.9 collective-permute-start.10
  76.6 4.1 %collective-permute-start.13 = (bf16[256,768]{1,0:T(8,128)(2,1)S(1)}, bf16[256,768]{1,0:T(8,128)(2,1)S(1)}, u32[]{:S(2)}, u32[]{:S(2)}) collective-permute-start(bf16[256,768]{1,0:T(8,128)(2,1)S(1)} %get-tuple-element.104), channel_id=1, source_target_pairs={{0,8},{4,12},{8,0},{12,4},{1,9},{5,13},{9,1},{13,5},{2,10},{6,14},... | collective-permute-start | bytes 1179656 | tf_op jit(solution)/shard_map/ppermute | solution.py:418
  80.7 12.0 %shard_map.125 = (f32[1024,768]{1,0:T(8,128)S(1)}, f32[128,768]{1,0:T(8,128)S(1)}, f32[8,768]{1,0:T(8,128)S(1)}) custom-call(s32[3]{0:T(128)S(1)} %copy-done.4, bf16[1024,1024]{1,0:T(8,128)(2,1)S(1)} %get-tuple-element.73.pick_ref, bf16[16,64]{1,0:T(8,128)(2,1)S(1)} %get-tuple-element.77.rims_ref, s32[1024,128]{1,0:T(8,128)S(1)} %get-tuple-element.78.gap_ref, ...), custom_call_target="tpu_custom_call" | custom-call | flops 17250000896 | tf_op jit(solution)/shard_map/pallas_call | solution.py:63
  92.9 0.1 fusion.11
  93.0 1.3 collective-permute-start.11
  94.3 0.1 collective-permute-start.17
  94.4 0.1 pad_maximum_fusion
  94.5 0.7 collective-permute-start.18
  95.2 15.0 %collective-permute-done.11 = f16[136,512]{1,0:T(8,128)(2,1)S(1)} collective-permute-done((f16[136,512]{1,0:T(8,128)(2,1)S(1)}, f16[136,512]{1,0:T(8,128)(2,1)S(1)}, u32[]{:S(2)}, u32[]{:S(2)}) %collective-permute-start.11) | collective-permute-done | bytes 139296 | tf_op jit(solution)/shard_map/ppermute | solution.py:595
  110.3 0.1 fusion.7
  110.4 0.1 pad_maximum_fusion.1
  110.5 0.7 collective-permute-start.19
  111.2 0.2 collective-permute-start.14
  111.4 12.7 %collective-permute-done.17.refs_1_ = bf16[256,768]{1,0:T(8,128)(2,1)S(1)} collective-permute-done((bf16[256,768]{1,0:T(8,128)(2,1)S(1)}, bf16[256,768]{1,0:T(8,128)(2,1)S(1)}, u32[]{:S(2)}, u32[]{:S(2)}) %collective-permute-start.17) | collective-permute-done | bytes 393248 | tf_op jit(solution)/shard_map/ppermute | solution.py:418
  124.1 0.1 fusion.27
  124.3 0.1 fusion.3
  124.4 0.1 pad_maximum_fusion.2
  124.5 1.3 collective-permute-start.20
  125.8 1.3 collective-permute-start.21
  127.1 1.3 shard_map.123
  128.4 1.3 shard_map.124
  129.6 10.3 %collective-permute-done.20 = f16[136,768]{1,0:T(8,128)(2,1)S(1)} collective-permute-done((f16[136,768]{1,0:T(8,128)(2,1)S(1)}, f16[136,768]{1,0:T(8,128)(2,1)S(1)}, u32[]{:S(2)}, u32[]{:S(2)}) %collective-permute-start.20) | collective-permute-done | bytes 208928 | tf_op jit(solution)/shard_map/ppermute | solution.py:595
  139.9 0.1 add_convert_fusion
  140.0 1.3 shard_map.126
  141.3 3.3 %collective-permute-done.21.refs_1_ = bf16[256,512]{1,0:T(8,128)(2,1)S(1)} collective-permute-done((bf16[256,512]{1,0:T(8,128)(2,1)S(1)}, bf16[256,512]{1,0:T(8,128)(2,1)S(1)}, u32[]{:S(2)}, u32[]{:S(2)}) %collective-permute-start.21) | collective-permute-done | bytes 262176 | tf_op jit(solution)/shard_map/ppermute | solution.py:418
  144.6 1.2 shard_map.127
  145.8 0.0 copy-start.8
  145.9 1.2 shard_map.128
  147.1 0.1 collective-permute-start.23
  147.2 1.1 collective-permute-start.24
  148.2 1.4 collective-permute-start.25
  149.6 0.6 collective-permute-done.23.refs_1_
  150.2 0.7 collective-permute-done.24.refs_2_
  150.8 0.1 collective-permute-done.25.refs_3_
  150.9 2.4 %shard_map.129 = bf16[1024,1280]{1,0:T(8,128)(2,1)} custom-call(f32[1,1024]{1,0:T(1,128)S(1)} %get-tuple-element.127.refs_0_, f32[1,1024]{1,0:T(1,128)S(1)} %collective-permute-done.23.refs_1_, f32[1,1024]{1,0:T(1,128)S(1)} %collective-permute-done.24.refs_2_, f32[1,1024]{1,0:T(1,128)S(1)} %collective-permute-done.25.refs_3_, f32[1,1280]{1,0:T(1,128)S(1)} %reshape.7.refs_4_, ...), custom_call_target="tpu_custom_call" | custom-call | flops 5750000128 | tf_op jit(solution)/shard_map/pallas_call | solution.py:63
  (72 shorter events, 1.0 us)
Async XLA Ops:
  0.0 16.4 %copy-start = (bf16[1024,1280]{1,0:T(8,128)(2,1)S(1)}, bf16[1024,1280]{1,0:T(8,128)(2,1)}, u32[]{:S(2)}) copy-start(bf16[1024,1280]{1,0:T(8,128)(2,1)} %x_ref.5) | copy-start | bytes 7864324
  6.1 6.7 %collective-permute-start = (bf16[272,128]{1,0:T(8,128)(2,1)}, bf16[272,128]{1,0:T(8,128)(2,1)S(1)}, u32[]{:S(2)}, u32[]{:S(2)}) collective-permute-start(bf16[272,128]{1,0:T(8,128)(2,1)} %get-tuple-element.70), channel_id=1, source_target_pairs={{0,4},{4,8},{8,12},{12,0},{1,5},{5,9},{9,13},{13,1},{2,6},{6,10},{... | collective-permute-start | bytes 208904 | tf_op jit(solution)/shard_map/ppermute | solution.py:418
  6.4 9.4 %collective-permute-start.1 = (bf16[272,128]{1,0:T(8,128)(2,1)}, bf16[272,128]{1,0:T(8,128)(2,1)S(1)}, u32[]{:S(2)}, u32[]{:S(2)}) collective-permute-start(bf16[272,128]{1,0:T(8,128)(2,1)} %get-tuple-element.71), channel_id=1, source_target_pairs={{0,8},{4,12},{8,0},{12,4},{1,9},{5,13},{9,1},{13,5},{2,10},{6,14},... | collective-permute-start | bytes 208904 | tf_op jit(solution)/shard_map/ppermute | solution.py:418
  8.1 7.7 %collective-permute-start.2 = (bf16[272,128]{1,0:T(8,128)(2,1)}, bf16[272,128]{1,0:T(8,128)(2,1)S(1)}, u32[]{:S(2)}, u32[]{:S(2)}) collective-permute-start(bf16[272,128]{1,0:T(8,128)(2,1)} %get-tuple-element.72), channel_id=1, source_target_pairs={{0,12},{4,0},{8,4},{12,8},{1,13},{5,1},{9,5},{13,9},{2,14},{6,2},{... | collective-permute-start | bytes 208904 | tf_op jit(solution)/shard_map/ppermute | solution.py:418
  8.5 30.4 %collective-permute-start.5 = (bf16[272,512]{1,0:T(8,128)(2,1)}, bf16[272,512]{1,0:T(8,128)(2,1)S(1)}, u32[]{:S(2)}, u32[]{:S(2)}) collective-permute-start(bf16[272,512]{1,0:T(8,128)(2,1)} %get-tuple-element.88), channel_id=1, source_target_pairs={{0,4},{4,8},{8,12},{12,0},{1,5},{5,9},{9,13},{13,1},{2,6},{6,10},{... | collective-permute-start | bytes 835592 | tf_op jit(solution)/shard_map/ppermute | solution.py:418
  11.9 27.0 %collective-permute-start.6 = (bf16[272,512]{1,0:T(8,128)(2,1)}, bf16[272,512]{1,0:T(8,128)(2,1)S(1)}, u32[]{:S(2)}, u32[]{:S(2)}) collective-permute-start(bf16[272,512]{1,0:T(8,128)(2,1)} %get-tuple-element.89), channel_id=1, source_target_pairs={{0,8},{4,12},{8,0},{12,4},{1,9},{5,13},{9,1},{13,5},{2,10},{6,14},... | collective-permute-start | bytes 835592 | tf_op jit(solution)/shard_map/ppermute | solution.py:418
  12.8 32.4 %collective-permute-start.7 = (bf16[272,512]{1,0:T(8,128)(2,1)}, bf16[272,512]{1,0:T(8,128)(2,1)S(1)}, u32[]{:S(2)}, u32[]{:S(2)}) collective-permute-start(bf16[272,512]{1,0:T(8,128)(2,1)} %get-tuple-element.90), channel_id=1, source_target_pairs={{0,12},{4,0},{8,4},{12,8},{1,13},{5,1},{9,5},{13,9},{2,14},{6,2},{... | collective-permute-start | bytes 835592 | tf_op jit(solution)/shard_map/ppermute | solution.py:418
  15.8 6.8 %collective-permute-start.3 = (bf16[1088,128]{1,0:T(8,128)(2,1)S(1)}, bf16[1088,128]{1,0:T(8,128)(2,1)S(1)}, u32[]{:S(2)}, u32[]{:S(2)}) collective-permute-start(bf16[1088,128]{1,0:T(8,128)(2,1)S(1)} %get-tuple-element.152.first_ref), channel_id=1, source_target_pairs={{0,2},{1,3},{2,0},{3,1},{4,6},{5,7},{6,4},{7,5},{8,10},{9,11},{10,... | collective-permute-start | bytes 835592 | tf_op jit(solution)/shard_map/ppermute | solution.py:493
  16.4 1.6 %copy-start.5 = (bf16[1088,1024]{1,0:T(8,128)(2,1)S(1)}, bf16[1088,1024]{1,0:T(8,128)(2,1)}, u32[]{:S(2)}) copy-start(bf16[1088,1024]{1,0:T(8,128)(2,1)} %get-tuple-element.93.pick_ref) | copy-start | bytes 6684676
  18.1 4.7 %copy-start.1 = (bf16[1024,1280]{1,0:T(8,128)(2,1)S(1)}, bf16[1024,1280]{1,0:T(8,128)(2,1)}, u32[]{:S(2)}) copy-start(bf16[1024,1280]{1,0:T(8,128)(2,1)} %x_ref.4) | copy-start | bytes 7864324
  18.1 4.7 %copy-start.6 = (bf16[1088,1024]{1,0:T(8,128)(2,1)S(1)}, bf16[1088,1024]{1,0:T(8,128)(2,1)}, u32[]{:S(2)}) copy-start(bf16[1088,1024]{1,0:T(8,128)(2,1)} %get-tuple-element.93.pick_ref) | copy-start | bytes 6684676
  22.6 2.8 %copy-start.9 = (f32[16]{0:T(128)S(1)}, f32[16]{0:T(128)}, u32[]{:S(2)}) copy-start(f32[16]{0:T(128)} %param.22) | copy-start | bytes 196
  22.7 2.8 %copy-start.10 = (f32[16]{0:T(128)S(1)}, f32[16]{0:T(128)}, u32[]{:S(2)}) copy-start(f32[16]{0:T(128)} %param.20) | copy-start | bytes 196
  22.7 2.8 %copy-start.11 = (f32[16]{0:T(128)S(1)}, f32[16]{0:T(128)}, u32[]{:S(2)}) copy-start(f32[16]{0:T(128)} %param.21) | copy-start | bytes 196
  22.7 16.3 %copy-start.3 = (f32[4,256]{1,0:T(4,128)S(1)}, f32[4,256]{1,0:T(4,128)}, u32[]{:S(2)}) copy-start(f32[4,256]{1,0:T(4,128)} %taps_ref.3) | copy-start | bytes 12292
  22.7 16.3 %copy-start.4 = (s32[3]{0:T(128)S(1)}, s32[3]{0:T(128)}, u32[]{:S(2)}) copy-start(s32[3]{0:T(128)} %lengths.5) | copy-start | bytes 40
  22.7 16.3 %collective-permute-start.4 = (bf16[2176,128]{1,0:T(8,128)(2,1)S(1)}, bf16[2176,128]{1,0:T(8,128)(2,1)S(1)}, u32[]{:S(2)}, u32[]{:S(2)}) collective-permute-start(bf16[2176,128]{1,0:T(8,128)(2,1)S(1)} %constant_dynamic-update-slice_fusion.4), channel_id=1, source_target_pairs={{0,1},{1,0},{2,3},{3,2},{4,5},{5,4},{6,7},{7,6},{8,9},{9,8},{10,11... | collective-permute-start | bytes 1671176 | tf_op jit(solution)/shard_map/ppermute | solution.py:493
  38.9 14.6 %collective-permute-start.8 = (bf16[272,768]{1,0:T(8,128)(2,1)S(1)}, bf16[272,768]{1,0:T(8,128)(2,1)S(1)}, u32[]{:S(2)}, u32[]{:S(2)}) collective-permute-start(bf16[272,768]{1,0:T(8,128)(2,1)S(1)} %get-tuple-element.97), channel_id=1, source_target_pairs={{0,12},{4,0},{8,4},{12,8},{1,13},{5,1},{9,5},{13,9},{2,14},{6,2},{... | collective-permute-start | bytes 1253384 | tf_op jit(solution)/shard_map/ppermute | solution.py:418
  38.9 6.4 %copy-start.2 = (f32[4,1280]{1,0:T(4,128)S(1)}, f32[4,1280]{1,0:T(4,128)}, u32[]{:S(2)}) copy-start(f32[4,1280]{1,0:T(4,128)} %taps_ref.5) | copy-start | bytes 61444
  38.9 6.4 %copy-start.7 = (bf16[272,512]{1,0:T(8,128)(2,1)S(1)}, bf16[272,512]{1,0:T(8,128)(2,1)}, u32[]{:S(2)}) copy-start(bf16[272,512]{1,0:T(8,128)(2,1)} %get-tuple-element.87.refs_0_) | copy-start | bytes 835588
  38.9 30.8 %collective-permute-start.15 = (bf16[272,768]{1,0:T(8,128)(2,1)S(1)}, bf16[272,768]{1,0:T(8,128)(2,1)S(1)}, u32[]{:S(2)}, u32[]{:S(2)}) collective-permute-start(bf16[272,768]{1,0:T(8,128)(2,1)S(1)} %get-tuple-element.110), channel_id=1, source_target_pairs={{0,8},{4,12},{8,0},{12,4},{1,9},{5,13},{9,1},{13,5},{2,10},{6,14},... | collective-permute-start | bytes 1253384 | tf_op jit(solution)/shard_map/ppermute | solution.py:418
  53.6 21.9 %collective-permute-start.9 = (f16[136,512]{1,0:T(8,128)(2,1)S(1)}, f16[136,512]{1,0:T(8,128)(2,1)S(1)}, u32[]{:S(2)}, u32[]{:S(2)}) collective-permute-start(f16[136,512]{1,0:T(8,128)(2,1)S(1)} %pad_maximum_fusion.3), channel_id=1, source_target_pairs={{0,4},{1,5},{2,6},{3,7},{16,20},{17,21},{18,22},{19,23}} | collective-permute-start | bytes 417800 | tf_op jit(solution)/shard_map/ppermute | solution.py:595
  54.3 22.3 %collective-permute-start.12 = (bf16[272,768]{1,0:T(8,128)(2,1)S(1)}, bf16[272,768]{1,0:T(8,128)(2,1)S(1)}, u32[]{:S(2)}, u32[]{:S(2)}) collective-permute-start(bf16[272,768]{1,0:T(8,128)(2,1)S(1)} %get-tuple-element.103), channel_id=1, source_target_pairs={{0,4},{4,8},{8,12},{12,0},{1,5},{5,9},{9,13},{13,1},{2,6},{6,10},{... | collective-permute-start | bytes 1253384 | tf_op jit(solution)/shard_map/ppermute | solution.py:418
  69.6 24.7 %collective-permute-start.16 = (bf16[256,768]{1,0:T(8,128)(2,1)S(1)}, bf16[256,768]{1,0:T(8,128)(2,1)S(1)}, u32[]{:S(2)}, u32[]{:S(2)}) collective-permute-start(bf16[256,768]{1,0:T(8,128)(2,1)S(1)} %get-tuple-element.111), channel_id=1, source_target_pairs={{0,12},{4,0},{8,4},{12,8},{1,13},{5,1},{9,5},{13,9},{2,14},{6,2},{... | collective-permute-start | bytes 1179656 | tf_op jit(solution)/shard_map/ppermute | solution.py:418
  75.7 17.1 %collective-permute-start.10 = (f16[136,512]{1,0:T(8,128)(2,1)S(1)}, f16[136,512]{1,0:T(8,128)(2,1)S(1)}, u32[]{:S(2)}, u32[]{:S(2)}) collective-permute-start(f16[136,512]{1,0:T(8,128)(2,1)S(1)} %pad_maximum_fusion.4), channel_id=1, source_target_pairs={{4,8},{5,9},{6,10},{7,11},{20,24},{21,25},{22,26},{23,27}} | collective-permute-start | bytes 417800 | tf_op jit(solution)/shard_map/ppermute | solution.py:595
  76.6 34.6 %collective-permute-start.13 = (bf16[256,768]{1,0:T(8,128)(2,1)S(1)}, bf16[256,768]{1,0:T(8,128)(2,1)S(1)}, u32[]{:S(2)}, u32[]{:S(2)}) collective-permute-start(bf16[256,768]{1,0:T(8,128)(2,1)S(1)} %get-tuple-element.104), channel_id=1, source_target_pairs={{0,8},{4,12},{8,0},{12,4},{1,9},{5,13},{9,1},{13,5},{2,10},{6,14},... | collective-permute-start | bytes 1179656 | tf_op jit(solution)/shard_map/ppermute | solution.py:418
  93.0 17.1 %collective-permute-start.11 = (f16[136,512]{1,0:T(8,128)(2,1)S(1)}, f16[136,512]{1,0:T(8,128)(2,1)S(1)}, u32[]{:S(2)}, u32[]{:S(2)}) collective-permute-start(f16[136,512]{1,0:T(8,128)(2,1)S(1)} %pad_maximum_fusion.5), channel_id=1, source_target_pairs={{8,12},{9,13},{10,14},{11,15},{24,28},{25,29},{26,30},{27,31}} | collective-permute-start | bytes 417800 | tf_op jit(solution)/shard_map/ppermute | solution.py:595
  94.3 29.8 %collective-permute-start.17 = (bf16[256,768]{1,0:T(8,128)(2,1)S(1)}, bf16[256,768]{1,0:T(8,128)(2,1)S(1)}, u32[]{:S(2)}, u32[]{:S(2)}) collective-permute-start(bf16[256,768]{1,0:T(8,128)(2,1)S(1)} %get-tuple-element.112), channel_id=1, source_target_pairs={{0,4},{4,8},{8,12},{12,0},{1,5},{5,9},{9,13},{13,1},{2,6},{6,10},{... | collective-permute-start | bytes 1179656 | tf_op jit(solution)/shard_map/ppermute | solution.py:418
  94.5 15.7 %collective-permute-start.18 = (f16[136,768]{1,0:T(8,128)(2,1)S(1)}, f16[136,768]{1,0:T(8,128)(2,1)S(1)}, u32[]{:S(2)}, u32[]{:S(2)}) collective-permute-start(f16[136,768]{1,0:T(8,128)(2,1)S(1)} %pad_maximum_fusion), channel_id=1, source_target_pairs={{0,4},{1,5},{2,6},{3,7},{16,20},{17,21},{18,22},{19,23}} | collective-permute-start | bytes 626696 | tf_op jit(solution)/shard_map/ppermute | solution.py:595
  110.5 13.6 %collective-permute-start.19 = (f16[136,768]{1,0:T(8,128)(2,1)S(1)}, f16[136,768]{1,0:T(8,128)(2,1)S(1)}, u32[]{:S(2)}, u32[]{:S(2)}) collective-permute-start(f16[136,768]{1,0:T(8,128)(2,1)S(1)} %pad_maximum_fusion.1), channel_id=1, source_target_pairs={{4,8},{5,9},{6,10},{7,11},{20,24},{21,25},{22,26},{23,27}} | collective-permute-start | bytes 626696 | tf_op jit(solution)/shard_map/ppermute | solution.py:595
  111.2 14.5 %collective-permute-start.14 = (bf16[256,512]{1,0:T(8,128)(2,1)S(1)}, bf16[256,512]{1,0:T(8,128)(2,1)S(1)}, u32[]{:S(2)}, u32[]{:S(2)}) collective-permute-start(bf16[256,512]{1,0:T(8,128)(2,1)S(1)} %get-tuple-element.105), channel_id=1, source_target_pairs={{0,12},{4,0},{8,4},{12,8},{1,13},{5,1},{9,5},{13,9},{2,14},{6,2},{... | collective-permute-start | bytes 786440 | tf_op jit(solution)/shard_map/ppermute | solution.py:418
  124.1 17.2 %collective-permute-start.22 = (bf16[256,512]{1,0:T(8,128)(2,1)S(1)}, bf16[256,512]{1,0:T(8,128)(2,1)S(1)}, u32[]{:S(2)}, u32[]{:S(2)}) collective-permute-start(bf16[256,512]{1,0:T(8,128)(2,1)S(1)} %get-tuple-element.125), channel_id=1, source_target_pairs={{0,8},{4,12},{8,0},{12,4},{1,9},{5,13},{9,1},{13,5},{2,10},{6,14},... | collective-permute-start | bytes 786440 | tf_op jit(solution)/shard_map/ppermute | solution.py:418
  124.5 15.4 %collective-permute-start.20 = (f16[136,768]{1,0:T(8,128)(2,1)S(1)}, f16[136,768]{1,0:T(8,128)(2,1)S(1)}, u32[]{:S(2)}, u32[]{:S(2)}) collective-permute-start(f16[136,768]{1,0:T(8,128)(2,1)S(1)} %pad_maximum_fusion.2), channel_id=1, source_target_pairs={{8,12},{9,13},{10,14},{11,15},{24,28},{25,29},{26,30},{27,31}} | collective-permute-start | bytes 626696 | tf_op jit(solution)/shard_map/ppermute | solution.py:595
  125.8 18.8 %collective-permute-start.21 = (bf16[256,512]{1,0:T(8,128)(2,1)S(1)}, bf16[256,512]{1,0:T(8,128)(2,1)S(1)}, u32[]{:S(2)}, u32[]{:S(2)}) collective-permute-start(bf16[256,512]{1,0:T(8,128)(2,1)S(1)} %get-tuple-element.123), channel_id=1, source_target_pairs={{0,4},{4,8},{8,12},{12,0},{1,5},{5,9},{9,13},{13,1},{2,6},{6,10},{... | collective-permute-start | bytes 786440 | tf_op jit(solution)/shard_map/ppermute | solution.py:418
  145.8 3.8 %copy-start.8 = (f32[1280]{0:T(1024)S(1)}, f32[1280]{0:T(1024)}, u32[]{:S(2)}) copy-start(f32[1280]{0:T(1024)} %param.23) | copy-start | bytes 15364
  147.1 3.1 %collective-permute-start.23 = (f32[1,1024]{1,0:T(1,128)S(1)}, f32[1,1024]{1,0:T(1,128)S(1)}, u32[]{:S(2)}, u32[]{:S(2)}) collective-permute-start(f32[1,1024]{1,0:T(1,128)S(1)} %get-tuple-element.127.refs_0_), channel_id=1, source_target_pairs={{0,1},{1,2},{2,3},{3,0},{4,5},{5,6},{6,7},{7,4},{8,9},{9,10},{10,1... | collective-permute-start | bytes 12296 | tf_op jit(solution)/shard_map/ppermute | solution.py:418
  147.2 3.7 %collective-permute-start.24 = (f32[1,1024]{1,0:T(1,128)S(1)}, f32[1,1024]{1,0:T(1,128)S(1)}, u32[]{:S(2)}, u32[]{:S(2)}) collective-permute-start(f32[1,1024]{1,0:T(1,128)S(1)} %get-tuple-element.127.refs_0_), channel_id=1, source_target_pairs={{0,2},{1,3},{2,0},{3,1},{4,6},{5,7},{6,4},{7,5},{8,10},{9,11},{10,... | collective-permute-start | bytes 12296 | tf_op jit(solution)/shard_map/ppermute | solution.py:418
  148.2 2.7 %collective-permute-start.25 = (f32[1,1024]{1,0:T(1,128)S(1)}, f32[1,1024]{1,0:T(1,128)S(1)}, u32[]{:S(2)}, u32[]{:S(2)}) collective-permute-start(f32[1,1024]{1,0:T(1,128)S(1)} %get-tuple-element.127.refs_0_), channel_id=1, source_target_pairs={{0,3},{1,0},{2,1},{3,2},{4,7},{5,4},{6,5},{7,6},{8,11},{9,8},{10,9... | collective-permute-start | bytes 12296 | tf_op jit(solution)/shard_map/ppermute | solution.py:418

commit v6 on v5

--- a/solution.py
+++ b/solution.py
@@ -12,6 +12,7 @@
 TILE = 256
 LANES = 128
 RIM = 16
+EDGE = 4
 SHARES = (0.4,)
 GATE_SHARES = (0.6,)
 WINDOW = 2
@@ -135,19 +136,19 @@
             small_refs[k][:per] = (dot(pick, thick) + dot_nt(pick, thin)).astype(bf16)
             small_refs[k][per:] = (dot(rim, thick) + dot_nt(rim, thin)).astype(bf16)
 
-    gather_rows(shards, True, pick_ref, x_ref, *x_refs)
-
-
-def gather_rows(shards, with_rim, pick_ref, x_ref, *out_refs):
+    gather_rows(shards, pick_ref, x_ref, *x_refs)
+
+
+def gather_rows(shards, pick_ref, x_ref, *out_refs):
     rows = x_ref.shape[0]
     per = rows // shards
     values = x_ref[...]
     for k in range(shards):
-        out_refs[k][:per] = dot(pick_ref[k * per : (k + 1) * per], values).astype(bf16)
-    if with_rim:
-        rims = dot(pick_ref[rows:], values).astype(bf16)
-        for k in range(shards):
-            out_refs[k][per:] = rims[k * RIM : (k + 1) * RIM]
+        out_refs[k][...] = dot(pick_ref[k * per : (k + 1) * per], values).astype(bf16)
+
+
+def gather_rims(pick_ref, x_ref, out_ref):
+    out_ref[...] = dot(pick_ref[...], x_ref[...]).astype(bf16)
 
 
 def gather_parts(shards, parts, pick_ref, x_ref, *out_refs):
@@ -212,7 +213,9 @@
     slots = dot_nt(weights, own_main)[0:1].astype(jnp.int32) - 1
     rim_slots = dot_nt(weights, rim(first_ref))[0:1].astype(jnp.int32) - 1 - rows + HALO
     rim_pick = ones_where(iota((RIM, shards * RIM), 0) == rim_slots)
-    rims_ref[...] = rim_pick
+    source, wanted = iota((shards * RIM, shards * EDGE), 0), iota((shards * RIM, shards * EDGE), 1)
+    kept = ones_where((source // RIM == wanted // EDGE) & (source % RIM == wanted % EDGE))
+    rims_ref[...] = dot(rim_pick, kept).astype(bf16)
     me = lax.axis_index("head")
     bc_main, bc_rim = 0.0, 0.0
     for flip, ref in zip(flips, sources):
@@ -317,15 +320,14 @@
     lengths, pick_ref, rims_ref, gap_ref, score_high_ref, score_low_ref, kept_query_ref, keys_ref,
     inside_ref, outside_ref, expand_ref, factor_ref, rest_ref, taps_ref, *refs,
 ):
-    blocks = refs[:shards]
-    out_ref, state_ref, size_ref, arrived, packed = refs[shards:]
+    blocks, edge_ref = refs[:shards], refs[shards]
+    out_ref, state_ref, size_ref, arrived, packed = refs[shards + 1 :]
     rows = pick_ref.shape[0]
     per = rows // shards
     base = lax.axis_index("seq") * rows
     for k in range(shards):
-        arrived[k * per : (k + 1) * per] = blocks[k][:per]
-    rim = jnp.concatenate([blocks[k][per:] for k in range(shards)], 0)
-    packed[0:HALO] = dot(rims_ref[...], rim)[0:HALO]
+        arrived[k * per : (k + 1) * per] = blocks[k][...]
+    packed[0:HALO] = dot(rims_ref[...], edge_ref[...])[0:HALO]
     expand = expand_ref[...]
     state_ref[...] = jnp.zeros_like(state_ref)
     for b in range(rows // ROWS):
@@ -463,10 +465,12 @@
     first, last = parts[0]
     sent = call(
         functools.partial(send_order, shards, width, quarter),
-        [shape(full, rows)] + [shape(group, LANES)] * shards + [shape(group, (last - first) * TILE)] * shards,
+        [pltpu.VMEM((full, rows), bf16)]
+        + [pltpu.VMEM((group, LANES), bf16)] * shards
+        + [pltpu.VMEM((per, (last - first) * TILE), bf16)] * shards,
         (place, bc_in, thin, xs),
         [whole(place), whole(bc_in), whole(thin), columns(rows)],
-        [whole(shape(full, rows))] + [whole(shape(group, LANES))] * shards + [columns(group)] * shards,
+        [whole(shape(full, rows))] + [whole(shape(group, LANES))] * shards + [columns(per)] * shards,
         grid=(last - first,),
         micros=7,
         limit=56,
@@ -486,6 +490,20 @@
 
     arrived = [queued(x_send[0])]
 
+    rims = shards * RIM
+    edges = call(
+        gather_rims,
+        shape(rims, inner),
+        (picks, xs),
+        [pl.BlockSpec((rims, rows), lambda j: (rows // rims, 0)), columns(rows)],
+        columns(rims),
+        grid=(tiles,),
+        micros=2,
+    )
+    edges = [edges[k * RIM : k * RIM + EDGE] for k in range(shards)]
+    for k in range(1, shards):
+        edges[k] = moved(after(edges[k], arrived[0][distances[0]]), "seq", k)
+    edges = jnp.concatenate(edges, 0)
     small = [jnp.concatenate(small, 0)]
     mask = groups // 2
     while mask:
@@ -495,11 +513,11 @@
     for first, last in parts[1:]:
         x_send.append(
             call(
-                functools.partial(gather_rows, shards, True),
-                [shape(group, (last - first) * TILE)] * shards,
+                functools.partial(gather_rows, shards),
+                [shape(per, (last - first) * TILE)] * shards,
                 (picks, xs),
-                [whole(picks), columns(rows, start=first)],
-                [columns(group)] * shards,
+                [whole(shape(rows, rows)), columns(rows, start=first)],
+                [columns(per)] * shards,
                 grid=(last - first,),
                 micros=2 * (last - first),
             )
@@ -520,7 +538,7 @@
 
     kept = [
         shape(rows, rows),
-        shape(RIM, shards * RIM),
+        shape(RIM, shards * EDGE),
         shape(rows, LANES, dtype=jnp.int32),
         shape(rows, ROWS),
         shape(rows, ROWS),
@@ -566,12 +584,13 @@
             [shape(rows, size, dtype=f32), shape(state, size, dtype=f32), shape(8, size, dtype=f32)],
             (
                 lengths, pick, rims, gap, score_high, score_low, kept_query, keys, inside, outside,
-                expand, factor, rest, conv_x, *blocks,
+                expand, factor, rest, conv_x, *blocks, edges,
             ),
             [smem()]
             + [whole(a) for a in (pick, rims, gap, score_high, score_low, kept_query, keys, inside, outside)]
             + [columns(n, start=first) for n in (LANES, chunks, 8, width)]
-            + [columns(group)] * shards,
+            + [columns(per)] * shards
+            + [columns(shards * EDGE, start=first)],
             [columns(rows), columns(state), columns(8)],
             grid=(last - first,),
             scratch=[pltpu.VMEM((rows, TILE), bf16), pltpu.VMEM((rows + HALO, TILE), f32)],

time: 155 us -> 151 us (0.974)
  waiting for transfers between devices: 67.2 us -> 32.7 us
  starting transfers between devices: 32.9 us -> 65.9 us
  local copies, waits for them, and re-layouts: 2.76 us -> 0.25 us
    ppermute x18 -> x21, starting transfers between devices: 26.8 us -> 59.7 us  [moved(): lax.ppermute(block, axis, [(i, (i + steps) % count) for i in range(count)])]
    ppermute x18 -> x21, waiting for transfers between devices: 42 us -> 21.2 us  [moved(): lax.ppermute(block, axis, [(i, (i + steps) % count) for i in range(count)])]
    ppermute x6, waiting for transfers between devices: 25.2 us -> 9.15 us  [body(): lax.ppermute(packed_state(leaving, bound), 'seq', [(step - 1, step)])]
    unnamed x28 -> x22, local copies, waits for them, and re-layouts: 2.66 us -> 0.14 us
    ppermute x2, waiting for transfers between devices: 0.01 us -> 2.37 us  [body(): lax.ppermute(held, 'head', [(i, i ^ mask) for i in range(groups)])]
    pallas_call x12 -> x13, Pallas kernels: 48.4 us -> 48.7 us  [call(): pl.pallas_call(kernel, grid=grid, in_specs=in_specs, out_specs=out_specs,...]
  transfers between devices with their start and end apart: 26 -> 29, of which waited for: 10 -> 11; matrix products, arithmetic and copies ran while one was open for 2% -> 1% of each run, Pallas kernels for 24% -> 26%
where the time goes in v6:
time: 151 us; the launch traced here: 150 us
  starting transfers between devices  65.9 us (44%)
  Pallas kernels  48.7 us (32%)
  waiting for transfers between devices  32.7 us (22%)
    ppermute x21, starting transfers between devices, moved(): lax.ppermute(block, axis, [(i, (i + steps) % count) for i in range(count)])  59.7 us
    pallas_call x13, Pallas kernels, call(): pl.pallas_call(kernel, grid=grid, in_specs=in_specs, out_specs=out_specs,...  48.7 us
    ppermute x21, waiting for transfers between devices, moved(): lax.ppermute(block, axis, [(i, (i + steps) % count) for i in range(count)])  21.2 us
    ppermute x6, waiting for transfers between devices, body(): lax.ppermute(packed_state(leaving, bound), 'seq', [(step - 1, step)])  9.15 us
    ppermute x6, starting transfers between devices, body(): lax.ppermute(packed_state(leaving, bound), 'seq', [(step - 1, step)])  5.49 us
  transfers between devices with their start and end apart: 29, of which 11 were waited for; matrix products, arithmetic and copies ran while one was open for 1% of the time, Pallas kernels for 26%

profile of v6, /device:TPU:26, one launch (start us, length us, event | category | flops | bytes accessed | tf_op | source)
XLA Modules:
  0.0 149.6 jit_solution(10157204463399321276)
XLA Ops:
  0.0 5.1 %shard_map.118 = (bf16[1088,1024]{1,0:T(8,128)(2,1)S(1)}, bf16[272,128]{1,0:T(8,128)(2,1)S(1)}, bf16[272,128]{1,0:T(8,128)(2,1)S(1)}, bf16[272,128]{1,0:T(8,128)...) custom-call(s32[1,1024]{1,0:T(1,128)} %bitcast.24, ...), custom_call_target="tpu_custom_call" | custom-call | flops 8049999872 | tf_op jit(solution)/shard_map/pallas_call | solution.py:64
  5.1 0.3 collective-permute-start
  5.4 1.7 %collective-permute-start.1 = (bf16[272,128]{1,0:T(8,128)(2,1)S(1)}, bf16[272,128]{1,0:T(8,128)(2,1)S(1)}, u32[]{:S(2)}, u32[]{:S(2)}) collective-permute-start(bf16[272,128]{1,0:T(8,128)(2,1)S(1)} %get-tuple-element.74), channel_id=1, source_target_pairs={{0,8},{4,12},{8,0},{12,4},{1,9},{5,13},{9,1},{13,5},{2,10},{6,14},... | collective-permute-start | bytes 208904 | tf_op jit(solution)/shard_map/ppermute | solution.py:420
  7.1 0.4 collective-permute-start.2
  7.5 3.4 %collective-permute-start.5 = (bf16[256,512]{1,0:T(8,128)(2,1)S(1)}, bf16[256,512]{1,0:T(8,128)(2,1)S(1)}, u32[]{:S(2)}, u32[]{:S(2)}) collective-permute-start(bf16[256,512]{1,0:T(8,128)(2,1)S(1)} %get-tuple-element.91), channel_id=1, source_target_pairs={{0,4},{4,8},{8,12},{12,0},{1,5},{5,9},{9,13},{13,1},{2,6},{6,10},{... | collective-permute-start | bytes 786440 | tf_op jit(solution)/shard_map/ppermute | solution.py:420
  10.9 4.5 %shard_map.123 = (bf16[256,768]{1,0:T(8,128)(2,1)S(1)}, bf16[256,768]{1,0:T(8,128)(2,1)S(1)}, bf16[256,768]{1,0:T(8,128)(2,1)S(1)}, bf16[256,768]{1,0:T(8,128)(2...) custom-call(bf16[1088,1024]{1,0:T(8,128)(2,1)S(1)} %get-tuple-elemen, ...), custom_call_target="tpu_custom_call" | custom-call | flops 11500000256 | tf_op jit(solution)/shard_map/pallas_call | solution.py:64
  15.4 1.3 collective-permute-start.7
  16.8 0.6 collective-permute-start.3
  17.4 2.4 %shard_map.122 = (bf16[256,768]{1,0:T(8,128)(2,1)S(1)}, bf16[256,768]{1,0:T(8,128)(2,1)S(1)}, bf16[256,768]{1,0:T(8,128)(2,1)S(1)}, bf16[256,768]{1,0:T(8,128)(2,1)S(1)}) custom-call(bf16[1088,1024]{1,0:T(8,128)(2,1)S(1)} %get-tuple-element.94.pick_ref, bf16[1024,1280]{1,0:T(8,128)(2,1)S(1)} %copy-done.1), custom_call_target="tpu_custom_call" | custom-call | flops 6899999744 | tf_op jit(solution)/shard_map/pallas_call | solution.py:64
  19.8 0.0 copy-start.6
  19.9 0.0 copy-start.3
  19.9 0.0 copy-start.4
  19.9 1.3 shard_map.120
  21.2 2.4 %collective-permute-done.3.refs_0_ = bf16[1088,128]{1,0:T(8,128)(2,1)S(1)} collective-permute-done((bf16[1088,128]{1,0:T(8,128)(2,1)S(1)}, bf16[1088,128]{1,0:T(8,128)(2,1)S(1)}, u32[]{:S(2)}, u32[]{:S(2)}) %collective-permute-start.3) | collective-permute-done | bytes 278560 | tf_op jit(solution)/shard_map/ppermute | solution.py:511
  23.6 0.1 collective-permute-start.4
  23.7 6.2 %collective-permute-done.7.refs_3_ = bf16[256,512]{1,0:T(8,128)(2,1)S(1)} collective-permute-done((bf16[256,512]{1,0:T(8,128)(2,1)S(1)}, bf16[256,512]{1,0:T(8,128)(2,1)S(1)}, u32[]{:S(2)}, u32[]{:S(2)}) %collective-permute-start.7) | collective-permute-done | bytes 262176 | tf_op jit(solution)/shard_map/ppermute | solution.py:420
  29.9 5.4 %collective-permute-start.10 = (bf16[4,1280]{1,0:T(4,128)(2,1)S(1)}, bf16[4,1280]{1,0:T(4,128)(2,1)S(1)}, u32[]{:S(2)}, u32[]{:S(2)}) collective-permute-start(bf16[4,1280]{1,0:T(4,128)(2,1)S(1)} %get-tuple-element.97), channel_id=1, source_target_pairs={{0,12},{4,0},{8,4},{12,8},{1,13},{5,1},{9,5},{13,9},{2,14},{6,2},{... | collective-permute-start | bytes 30728 | tf_op jit(solution)/shard_map/ppermute | solution.py:420
  35.3 1.9 %collective-permute-start.9 = (bf16[4,1280]{1,0:T(4,128)(2,1)S(1)}, bf16[4,1280]{1,0:T(4,128)(2,1)S(1)}, u32[]{:S(2)}, u32[]{:S(2)}) collective-permute-start(bf16[4,1280]{1,0:T(4,128)(2,1)S(1)} %get-tuple-element.96), channel_id=1, source_target_pairs={{0,8},{4,12},{8,0},{12,4},{1,9},{5,13},{9,1},{13,5},{2,10},{6,14},... | collective-permute-start | bytes 30728 | tf_op jit(solution)/shard_map/ppermute | solution.py:420
  37.2 2.9 %collective-permute-start.8 = (bf16[4,1280]{1,0:T(4,128)(2,1)S(1)}, bf16[4,1280]{1,0:T(4,128)(2,1)S(1)}, u32[]{:S(2)}, u32[]{:S(2)}) collective-permute-start(bf16[4,1280]{1,0:T(4,128)(2,1)S(1)} %get-tuple-element.95), channel_id=1, source_target_pairs={{0,4},{4,8},{8,12},{12,0},{1,5},{5,9},{9,13},{13,1},{2,6},{6,10},{... | collective-permute-start | bytes 30728 | tf_op jit(solution)/shard_map/ppermute | solution.py:420
  40.2 0.1 fusion.16.lines_ref
  40.2 0.2 collective-permute-start.11
  40.5 0.6 collective-permute-start.18
  41.1 0.5 collective-permute-done.8
  41.6 6.4 %shard_map.119 = (bf16[1024,1024]{1,0:T(8,128)(2,1)S(1)}, bf16[16,16]{1,0:T(8,128)(2,1)S(1)}, s32[1024,128]{1,0:T(8,128)S(1)}, bf16[1024,256]{1,0:T(8,128)(2,1)S...) custom-call(s32[3]{0:T(128)S(1)} %copy-done.4, ...), custom_call_target="tpu_custom_call" | custom-call | flops 9200000000 | tf_op jit(solution)/shard_map/pallas_call | solution.py:64
  48.1 8.2 %shard_map.121 = (f32[1024,512]{1,0:T(8,128)S(1)}, f32[128,512]{1,0:T(8,128)S(1)}, f32[8,512]{1,0:T(8,128)S(1)}) custom-call(s32[3]{0:T(128)S(1)} %copy-done.4, bf16[1024,1024]{1,0:T(8,128)(2,1)S(1)} %get-tuple-element.76.pick_ref, bf16[16,16]{1,0:T(8,128)(2,1)S(1)} %get-tuple-element.80.rims_ref, s32[1024,128]{1,0:T(8,128)S(1)} %get-tuple-element.81.gap_ref, ...), custom_call_target="tpu_custom_call" | custom-call | flops 11500000256 | tf_op jit(solution)/shard_map/pallas_call | solution.py:64
  56.5 0.7 collective-permute-start.12
  57.1 4.9 %collective-permute-start.15 = (bf16[256,768]{1,0:T(8,128)(2,1)S(1)}, bf16[256,768]{1,0:T(8,128)(2,1)S(1)}, u32[]{:S(2)}, u32[]{:S(2)}) collective-permute-start(bf16[256,768]{1,0:T(8,128)(2,1)S(1)} %get-tuple-element.109), channel_id=1, source_target_pairs={{0,4},{4,8},{8,12},{12,0},{1,5},{5,9},{9,13},{13,1},{2,6},{6,10},{... | collective-permute-start | bytes 1179656 | tf_op jit(solution)/shard_map/ppermute | solution.py:420
  62.1 7.2 %collective-permute-done.18.refs_2_ = bf16[256,768]{1,0:T(8,128)(2,1)S(1)} collective-permute-done((bf16[256,768]{1,0:T(8,128)(2,1)S(1)}, bf16[256,768]{1,0:T(8,128)(2,1)S(1)}, u32[]{:S(2)}, u32[]{:S(2)}) %collective-permute-start.18) | collective-permute-done | bytes 393248 | tf_op jit(solution)/shard_map/ppermute | solution.py:420
  69.3 5.2 %collective-permute-start.19 = (bf16[256,768]{1,0:T(8,128)(2,1)S(1)}, bf16[256,768]{1,0:T(8,128)(2,1)S(1)}, u32[]{:S(2)}, u32[]{:S(2)}) collective-permute-start(bf16[256,768]{1,0:T(8,128)(2,1)S(1)} %get-tuple-element.117), channel_id=1, source_target_pairs={{0,12},{4,0},{8,4},{12,8},{1,13},{5,1},{9,5},{13,9},{2,14},{6,2},{... | collective-permute-start | bytes 1179656 | tf_op jit(solution)/shard_map/ppermute | solution.py:420
  74.6 0.1 fusion.15
  74.7 0.9 collective-permute-start.13
  75.6 0.1 collective-permute-done.15.refs_1_
  75.7 14.1 %collective-permute-start.16 = (bf16[256,768]{1,0:T(8,128)(2,1)S(1)}, bf16[256,768]{1,0:T(8,128)(2,1)S(1)}, u32[]{:S(2)}, u32[]{:S(2)}) collective-permute-start(bf16[256,768]{1,0:T(8,128)(2,1)S(1)} %get-tuple-element.110), channel_id=1, source_target_pairs={{0,8},{4,12},{8,0},{12,4},{1,9},{5,13},{9,1},{13,5},{2,10},{6,14},... | collective-permute-start | bytes 1179656 | tf_op jit(solution)/shard_map/ppermute | solution.py:420
  89.8 12.0 %shard_map.126 = (f32[1024,768]{1,0:T(8,128)S(1)}, f32[128,768]{1,0:T(8,128)S(1)}, f32[8,768]{1,0:T(8,128)S(1)}) custom-call(s32[3]{0:T(128)S(1)} %copy-done.4, bf16[1024,1024]{1,0:T(8,128)(2,1)S(1)} %get-tuple-element.76.pick_ref, bf16[16,16]{1,0:T(8,128)(2,1)S(1)} %get-tuple-element.80.rims_ref, s32[1024,128]{1,0:T(8,128)S(1)} %get-tuple-element.81.gap_ref, ...), custom_call_target="tpu_custom_call" | custom-call | flops 17250000896 | tf_op jit(solution)/shard_map/pallas_call | solution.py:64
  102.0 0.1 fusion.11
  102.2 1.3 collective-permute-start.14
  103.5 2.8 %collective-permute-start.20 = (bf16[256,768]{1,0:T(8,128)(2,1)S(1)}, bf16[256,768]{1,0:T(8,128)(2,1)S(1)}, u32[]{:S(2)}, u32[]{:S(2)}) collective-permute-start(bf16[256,768]{1,0:T(8,128)(2,1)S(1)} %get-tuple-element.118), channel_id=1, source_target_pairs={{0,4},{4,8},{8,12},{12,0},{1,5},{5,9},{9,13},{13,1},{2,6},{6,10},{... | collective-permute-start | bytes 1179656 | tf_op jit(solution)/shard_map/ppermute | solution.py:420
  106.3 0.1 pad_maximum_fusion
  106.4 0.7 collective-permute-start.21
  107.1 2.5 %collective-permute-done.14 = f16[136,512]{1,0:T(8,128)(2,1)S(1)} collective-permute-done((f16[136,512]{1,0:T(8,128)(2,1)S(1)}, f16[136,512]{1,0:T(8,128)(2,1)S(1)}, u32[]{:S(2)}, u32[]{:S(2)}) %collective-permute-start.14) | collective-permute-done | bytes 139296 | tf_op jit(solution)/shard_map/ppermute | solution.py:614
  109.7 0.1 collective-permute-start.17
  109.9 0.1 fusion.7
  110.0 0.1 pad_maximum_fusion.1
  110.1 0.7 collective-permute-start.22
  110.7 5.4 %collective-permute-done.20.refs_1_ = bf16[256,768]{1,0:T(8,128)(2,1)S(1)} collective-permute-done((bf16[256,768]{1,0:T(8,128)(2,1)S(1)}, bf16[256,768]{1,0:T(8,128)(2,1)S(1)}, u32[]{:S(2)}, u32[]{:S(2)}) %collective-permute-start.20) | collective-permute-done | bytes 393248 | tf_op jit(solution)/shard_map/ppermute | solution.py:420
  116.1 9.0 %collective-permute-start.25 = (bf16[256,512]{1,0:T(8,128)(2,1)S(1)}, bf16[256,512]{1,0:T(8,128)(2,1)S(1)}, u32[]{:S(2)}, u32[]{:S(2)}) collective-permute-start(bf16[256,512]{1,0:T(8,128)(2,1)S(1)} %get-tuple-element.131), channel_id=1, source_target_pairs={{0,8},{4,12},{8,0},{12,4},{1,9},{5,13},{9,1},{13,5},{2,10},{6,14},... | collective-permute-start | bytes 786440 | tf_op jit(solution)/shard_map/ppermute | solution.py:420
  125.1 0.4 collective-permute-done.17.refs_3_
  125.5 3.2 %collective-permute-start.24 = (bf16[256,512]{1,0:T(8,128)(2,1)S(1)}, bf16[256,512]{1,0:T(8,128)(2,1)S(1)}, u32[]{:S(2)}, u32[]{:S(2)}) collective-permute-start(bf16[256,512]{1,0:T(8,128)(2,1)S(1)} %get-tuple-element.129), channel_id=1, source_target_pairs={{0,4},{4,8},{8,12},{12,0},{1,5},{5,9},{9,13},{13,1},{2,6},{6,10},{... | collective-permute-start | bytes 786440 | tf_op jit(solution)/shard_map/ppermute | solution.py:420
  128.7 1.3 shard_map.124
  130.0 0.1 fusion.27
  130.1 0.1 fusion.3
  130.3 0.1 pad_maximum_fusion.2
  130.3 1.3 collective-permute-start.23
  131.6 1.3 shard_map.125
  132.9 6.6 %collective-permute-done.23 = f16[136,768]{1,0:T(8,128)(2,1)S(1)} collective-permute-done((f16[136,768]{1,0:T(8,128)(2,1)S(1)}, f16[136,768]{1,0:T(8,128)(2,1)S(1)}, u32[]{:S(2)}, u32[]{:S(2)}) %collective-permute-start.23) | collective-permute-done | bytes 208928 | tf_op jit(solution)/shard_map/ppermute | solution.py:614
  139.6 1.3 shard_map.127
  140.9 1.3 shard_map.128
  142.2 1.3 shard_map.129
  143.4 0.1 collective-permute-start.26
  143.5 0.9 collective-permute-start.27
  144.4 1.4 collective-permute-start.28
  145.8 0.8 collective-permute-done.26.refs_1_
  146.5 0.7 collective-permute-done.27.refs_2_
  147.2 2.4 %shard_map.130 = bf16[1024,1280]{1,0:T(8,128)(2,1)} custom-call(f32[1,1024]{1,0:T(1,128)S(1)} %get-tuple-element.133.refs_0_, f32[1,1024]{1,0:T(1,128)S(1)} %collective-permute-done.26.refs_1_, f32[1,1024]{1,0:T(1,128)S(1)} %collective-permute-done.27.refs_2_, f32[1,1024]{1,0:T(1,128)S(1)} %collective-permute-done.28.refs_3_, f32[1,1280]{1,0:T(1,128)S(1)} %reshape.7.refs_4_, ...), custom_call_target="tpu_custom_call" | custom-call | flops 5750000128 | tf_op jit(solution)/shard_map/pallas_call | solution.py:64
  (75 shorter events, 1.1 us)
Async XLA Ops:
  0.0 10.9 %copy-start = (bf16[1024,1280]{1,0:T(8,128)(2,1)S(1)}, bf16[1024,1280]{1,0:T(8,128)(2,1)}, u32[]{:S(2)}) copy-start(bf16[1024,1280]{1,0:T(8,128)(2,1)} %x_ref.7) | copy-start | bytes 7864324
  5.1 10.3 %collective-permute-start = (bf16[272,128]{1,0:T(8,128)(2,1)S(1)}, bf16[272,128]{1,0:T(8,128)(2,1)S(1)}, u32[]{:S(2)}, u32[]{:S(2)}) collective-permute-start(bf16[272,128]{1,0:T(8,128)(2,1)S(1)} %get-tuple-element.73), channel_id=1, source_target_pairs={{0,4},{4,8},{8,12},{12,0},{1,5},{5,9},{9,13},{13,1},{2,6},{6,10},{... | collective-permute-start | bytes 208904 | tf_op jit(solution)/shard_map/ppermute | solution.py:420
  5.4 11.4 %collective-permute-start.1 = (bf16[272,128]{1,0:T(8,128)(2,1)S(1)}, bf16[272,128]{1,0:T(8,128)(2,1)S(1)}, u32[]{:S(2)}, u32[]{:S(2)}) collective-permute-start(bf16[272,128]{1,0:T(8,128)(2,1)S(1)} %get-tuple-element.74), channel_id=1, source_target_pairs={{0,8},{4,12},{8,0},{12,4},{1,9},{5,13},{9,1},{13,5},{2,10},{6,14},... | collective-permute-start | bytes 208904 | tf_op jit(solution)/shard_map/ppermute | solution.py:420
  7.1 9.7 %collective-permute-start.2 = (bf16[272,128]{1,0:T(8,128)(2,1)S(1)}, bf16[272,128]{1,0:T(8,128)(2,1)S(1)}, u32[]{:S(2)}, u32[]{:S(2)}) collective-permute-start(bf16[272,128]{1,0:T(8,128)(2,1)S(1)} %get-tuple-element.75), channel_id=1, source_target_pairs={{0,12},{4,0},{8,4},{12,8},{1,13},{5,1},{9,5},{13,9},{2,14},{6,2},{... | collective-permute-start | bytes 208904 | tf_op jit(solution)/shard_map/ppermute | solution.py:420
  7.5 32.7 %collective-permute-start.5 = (bf16[256,512]{1,0:T(8,128)(2,1)S(1)}, bf16[256,512]{1,0:T(8,128)(2,1)S(1)}, u32[]{:S(2)}, u32[]{:S(2)}) collective-permute-start(bf16[256,512]{1,0:T(8,128)(2,1)S(1)} %get-tuple-element.91), channel_id=1, source_target_pairs={{0,4},{4,8},{8,12},{12,0},{1,5},{5,9},{9,13},{13,1},{2,6},{6,10},{... | collective-permute-start | bytes 786440 | tf_op jit(solution)/shard_map/ppermute | solution.py:420
  10.9 26.3 %collective-permute-start.6 = (bf16[256,512]{1,0:T(8,128)(2,1)S(1)}, bf16[256,512]{1,0:T(8,128)(2,1)S(1)}, u32[]{:S(2)}, u32[]{:S(2)}) collective-permute-start(bf16[256,512]{1,0:T(8,128)(2,1)S(1)} %get-tuple-element.92), channel_id=1, source_target_pairs={{0,8},{4,12},{8,0},{12,4},{1,9},{5,13},{9,1},{13,5},{2,10},{6,14},... | collective-permute-start | bytes 786440 | tf_op jit(solution)/shard_map/ppermute | solution.py:420
  10.9 6.5 %copy-start.1 = (bf16[1024,1280]{1,0:T(8,128)(2,1)S(1)}, bf16[1024,1280]{1,0:T(8,128)(2,1)}, u32[]{:S(2)}) copy-start(bf16[1024,1280]{1,0:T(8,128)(2,1)} %x_ref.6) | copy-start | bytes 7864324
  15.4 14.5 %collective-permute-start.7 = (bf16[256,512]{1,0:T(8,128)(2,1)S(1)}, bf16[256,512]{1,0:T(8,128)(2,1)S(1)}, u32[]{:S(2)}, u32[]{:S(2)}) collective-permute-start(bf16[256,512]{1,0:T(8,128)(2,1)S(1)} %get-tuple-element.93), channel_id=1, source_target_pairs={{0,12},{4,0},{8,4},{12,8},{1,13},{5,1},{9,5},{13,9},{2,14},{6,2},{... | collective-permute-start | bytes 786440 | tf_op jit(solution)/shard_map/ppermute | solution.py:420
  16.8 6.8 %collective-permute-start.3 = (bf16[1088,128]{1,0:T(8,128)(2,1)S(1)}, bf16[1088,128]{1,0:T(8,128)(2,1)S(1)}, u32[]{:S(2)}, u32[]{:S(2)}) collective-permute-start(bf16[1088,128]{1,0:T(8,128)(2,1)S(1)} %get-tuple-element.162.first_ref), channel_id=1, source_target_pairs={{0,2},{1,3},{2,0},{3,1},{4,6},{5,7},{6,4},{7,5},{8,10},{9,11},{10,... | collective-permute-start | bytes 835592 | tf_op jit(solution)/shard_map/ppermute | solution.py:511
  19.8 20.3 %copy-start.6 = (f32[16]{0:T(128)S(1)}, f32[16]{0:T(128)}, u32[]{:S(2)}) copy-start(f32[16]{0:T(128)} %param.22) | copy-start | bytes 196
  19.8 20.3 %copy-start.7 = (f32[16]{0:T(128)S(1)}, f32[16]{0:T(128)}, u32[]{:S(2)}) copy-start(f32[16]{0:T(128)} %param.20) | copy-start | bytes 196
  19.8 20.3 %copy-start.8 = (f32[16]{0:T(128)S(1)}, f32[16]{0:T(128)}, u32[]{:S(2)}) copy-start(f32[16]{0:T(128)} %param.21) | copy-start | bytes 196
  19.9 21.7 %copy-start.3 = (f32[4,256]{1,0:T(4,128)S(1)}, f32[4,256]{1,0:T(4,128)}, u32[]{:S(2)}) copy-start(f32[4,256]{1,0:T(4,128)} %taps_ref.3) | copy-start | bytes 12292
  19.9 21.7 %copy-start.4 = (s32[3]{0:T(128)S(1)}, s32[3]{0:T(128)}, u32[]{:S(2)}) copy-start(s32[3]{0:T(128)} %lengths.5) | copy-start | bytes 40
  23.6 17.9 %collective-permute-start.4 = (bf16[2176,128]{1,0:T(8,128)(2,1)S(1)}, bf16[2176,128]{1,0:T(8,128)(2,1)S(1)}, u32[]{:S(2)}, u32[]{:S(2)}) collective-permute-start(bf16[2176,128]{1,0:T(8,128)(2,1)S(1)} %constant_dynamic-update-slice_fusion.4), channel_id=1, source_target_pairs={{0,1},{1,0},{2,3},{3,2},{4,5},{5,4},{6,7},{7,6},{8,9},{9,8},{10,11... | collective-permute-start | bytes 1671176 | tf_op jit(solution)/shard_map/ppermute | solution.py:511
  29.9 10.6 %collective-permute-start.10 = (bf16[4,1280]{1,0:T(4,128)(2,1)S(1)}, bf16[4,1280]{1,0:T(4,128)(2,1)S(1)}, u32[]{:S(2)}, u32[]{:S(2)}) collective-permute-start(bf16[4,1280]{1,0:T(4,128)(2,1)S(1)} %get-tuple-element.97), channel_id=1, source_target_pairs={{0,12},{4,0},{8,4},{12,8},{1,13},{5,1},{9,5},{13,9},{2,14},{6,2},{... | collective-permute-start | bytes 30728 | tf_op jit(solution)/shard_map/ppermute | solution.py:420
  35.3 5.8 %collective-permute-start.9 = (bf16[4,1280]{1,0:T(4,128)(2,1)S(1)}, bf16[4,1280]{1,0:T(4,128)(2,1)S(1)}, u32[]{:S(2)}, u32[]{:S(2)}) collective-permute-start(bf16[4,1280]{1,0:T(4,128)(2,1)S(1)} %get-tuple-element.96), channel_id=1, source_target_pairs={{0,8},{4,12},{8,0},{12,4},{1,9},{5,13},{9,1},{13,5},{2,10},{6,14},... | collective-permute-start | bytes 30728 | tf_op jit(solution)/shard_map/ppermute | solution.py:420
  37.2 4.3 %collective-permute-start.8 = (bf16[4,1280]{1,0:T(4,128)(2,1)S(1)}, bf16[4,1280]{1,0:T(4,128)(2,1)S(1)}, u32[]{:S(2)}, u32[]{:S(2)}) collective-permute-start(bf16[4,1280]{1,0:T(4,128)(2,1)S(1)} %get-tuple-element.95), channel_id=1, source_target_pairs={{0,4},{4,8},{8,12},{12,0},{1,5},{5,9},{9,13},{13,1},{2,6},{6,10},{... | collective-permute-start | bytes 30728 | tf_op jit(solution)/shard_map/ppermute | solution.py:420
  40.2 16.1 %collective-permute-start.11 = (bf16[256,768]{1,0:T(8,128)(2,1)S(1)}, bf16[256,768]{1,0:T(8,128)(2,1)S(1)}, u32[]{:S(2)}, u32[]{:S(2)}) collective-permute-start(bf16[256,768]{1,0:T(8,128)(2,1)S(1)} %get-tuple-element.103), channel_id=1, source_target_pairs={{0,12},{4,0},{8,4},{12,8},{1,13},{5,1},{9,5},{13,9},{2,14},{6,2},{... | collective-permute-start | bytes 1179656 | tf_op jit(solution)/shard_map/ppermute | solution.py:420
  40.5 28.8 %collective-permute-start.18 = (bf16[256,768]{1,0:T(8,128)(2,1)S(1)}, bf16[256,768]{1,0:T(8,128)(2,1)S(1)}, u32[]{:S(2)}, u32[]{:S(2)}) collective-permute-start(bf16[256,768]{1,0:T(8,128)(2,1)S(1)} %get-tuple-element.116), channel_id=1, source_target_pairs={{0,8},{4,12},{8,0},{12,4},{1,9},{5,13},{9,1},{13,5},{2,10},{6,14},... | collective-permute-start | bytes 1179656 | tf_op jit(solution)/shard_map/ppermute | solution.py:420
  41.6 6.5 %copy-start.2 = (f32[4,1280]{1,0:T(4,128)S(1)}, f32[4,1280]{1,0:T(4,128)}, u32[]{:S(2)}) copy-start(f32[4,1280]{1,0:T(4,128)} %taps_ref.5) | copy-start | bytes 61444
  56.5 18.1 %collective-permute-start.12 = (f16[136,512]{1,0:T(8,128)(2,1)S(1)}, f16[136,512]{1,0:T(8,128)(2,1)S(1)}, u32[]{:S(2)}, u32[]{:S(2)}) collective-permute-start(f16[136,512]{1,0:T(8,128)(2,1)S(1)} %pad_maximum_fusion.3), channel_id=1, source_target_pairs={{0,4},{1,5},{2,6},{3,7},{16,20},{17,21},{18,22},{19,23}} | collective-permute-start | bytes 417800 | tf_op jit(solution)/shard_map/ppermute | solution.py:614
  57.1 18.6 %collective-permute-start.15 = (bf16[256,768]{1,0:T(8,128)(2,1)S(1)}, bf16[256,768]{1,0:T(8,128)(2,1)S(1)}, u32[]{:S(2)}, u32[]{:S(2)}) collective-permute-start(bf16[256,768]{1,0:T(8,128)(2,1)S(1)} %get-tuple-element.109), channel_id=1, source_target_pairs={{0,4},{4,8},{8,12},{12,0},{1,5},{5,9},{9,13},{13,1},{2,6},{6,10},{... | collective-permute-start | bytes 1179656 | tf_op jit(solution)/shard_map/ppermute | solution.py:420
  69.3 34.2 %collective-permute-start.19 = (bf16[256,768]{1,0:T(8,128)(2,1)S(1)}, bf16[256,768]{1,0:T(8,128)(2,1)S(1)}, u32[]{:S(2)}, u32[]{:S(2)}) collective-permute-start(bf16[256,768]{1,0:T(8,128)(2,1)S(1)} %get-tuple-element.117), channel_id=1, source_target_pairs={{0,12},{4,0},{8,4},{12,8},{1,13},{5,1},{9,5},{13,9},{2,14},{6,2},{... | collective-permute-start | bytes 1179656 | tf_op jit(solution)/shard_map/ppermute | solution.py:420
  74.7 27.2 %collective-permute-start.13 = (f16[136,512]{1,0:T(8,128)(2,1)S(1)}, f16[136,512]{1,0:T(8,128)(2,1)S(1)}, u32[]{:S(2)}, u32[]{:S(2)}) collective-permute-start(f16[136,512]{1,0:T(8,128)(2,1)S(1)} %pad_maximum_fusion.4), channel_id=1, source_target_pairs={{4,8},{5,9},{6,10},{7,11},{20,24},{21,25},{22,26},{23,27}} | collective-permute-start | bytes 417800 | tf_op jit(solution)/shard_map/ppermute | solution.py:614
  75.7 34.0 %collective-permute-start.16 = (bf16[256,768]{1,0:T(8,128)(2,1)S(1)}, bf16[256,768]{1,0:T(8,128)(2,1)S(1)}, u32[]{:S(2)}, u32[]{:S(2)}) collective-permute-start(bf16[256,768]{1,0:T(8,128)(2,1)S(1)} %get-tuple-element.110), channel_id=1, source_target_pairs={{0,8},{4,12},{8,0},{12,4},{1,9},{5,13},{9,1},{13,5},{2,10},{6,14},... | collective-permute-start | bytes 1179656 | tf_op jit(solution)/shard_map/ppermute | solution.py:420
  102.2 7.4 %collective-permute-start.14 = (f16[136,512]{1,0:T(8,128)(2,1)S(1)}, f16[136,512]{1,0:T(8,128)(2,1)S(1)}, u32[]{:S(2)}, u32[]{:S(2)}) collective-permute-start(f16[136,512]{1,0:T(8,128)(2,1)S(1)} %pad_maximum_fusion.5), channel_id=1, source_target_pairs={{8,12},{9,13},{10,14},{11,15},{24,28},{25,29},{26,30},{27,31}} | collective-permute-start | bytes 417800 | tf_op jit(solution)/shard_map/ppermute | solution.py:614
  103.5 12.7 %collective-permute-start.20 = (bf16[256,768]{1,0:T(8,128)(2,1)S(1)}, bf16[256,768]{1,0:T(8,128)(2,1)S(1)}, u32[]{:S(2)}, u32[]{:S(2)}) collective-permute-start(bf16[256,768]{1,0:T(8,128)(2,1)S(1)} %get-tuple-element.118), channel_id=1, source_target_pairs={{0,4},{4,8},{8,12},{12,0},{1,5},{5,9},{9,13},{13,1},{2,6},{6,10},{... | collective-permute-start | bytes 1179656 | tf_op jit(solution)/shard_map/ppermute | solution.py:420
  106.4 3.4 %collective-permute-start.21 = (f16[136,768]{1,0:T(8,128)(2,1)S(1)}, f16[136,768]{1,0:T(8,128)(2,1)S(1)}, u32[]{:S(2)}, u32[]{:S(2)}) collective-permute-start(f16[136,768]{1,0:T(8,128)(2,1)S(1)} %pad_maximum_fusion), channel_id=1, source_target_pairs={{0,4},{1,5},{2,6},{3,7},{16,20},{17,21},{18,22},{19,23}} | collective-permute-start | bytes 626696 | tf_op jit(solution)/shard_map/ppermute | solution.py:614
  109.7 15.8 %collective-permute-start.17 = (bf16[256,512]{1,0:T(8,128)(2,1)S(1)}, bf16[256,512]{1,0:T(8,128)(2,1)S(1)}, u32[]{:S(2)}, u32[]{:S(2)}) collective-permute-start(bf16[256,512]{1,0:T(8,128)(2,1)S(1)} %get-tuple-element.111), channel_id=1, source_target_pairs={{0,12},{4,0},{8,4},{12,8},{1,13},{5,1},{9,5},{13,9},{2,14},{6,2},{... | collective-permute-start | bytes 786440 | tf_op jit(solution)/shard_map/ppermute | solution.py:420
  110.1 19.9 %collective-permute-start.22 = (f16[136,768]{1,0:T(8,128)(2,1)S(1)}, f16[136,768]{1,0:T(8,128)(2,1)S(1)}, u32[]{:S(2)}, u32[]{:S(2)}) collective-permute-start(f16[136,768]{1,0:T(8,128)(2,1)S(1)} %pad_maximum_fusion.1), channel_id=1, source_target_pairs={{4,8},{5,9},{6,10},{7,11},{20,24},{21,25},{22,26},{23,27}} | collective-permute-start | bytes 626696 | tf_op jit(solution)/shard_map/ppermute | solution.py:614
  116.1 24.7 %collective-permute-start.25 = (bf16[256,512]{1,0:T(8,128)(2,1)S(1)}, bf16[256,512]{1,0:T(8,128)(2,1)S(1)}, u32[]{:S(2)}, u32[]{:S(2)}) collective-permute-start(bf16[256,512]{1,0:T(8,128)(2,1)S(1)} %get-tuple-element.131), channel_id=1, source_target_pairs={{0,8},{4,12},{8,0},{12,4},{1,9},{5,13},{9,1},{13,5},{2,10},{6,14},... | collective-permute-start | bytes 786440 | tf_op jit(solution)/shard_map/ppermute | solution.py:420
  125.5 15.3 %collective-permute-start.24 = (bf16[256,512]{1,0:T(8,128)(2,1)S(1)}, bf16[256,512]{1,0:T(8,128)(2,1)S(1)}, u32[]{:S(2)}, u32[]{:S(2)}) collective-permute-start(bf16[256,512]{1,0:T(8,128)(2,1)S(1)} %get-tuple-element.129), channel_id=1, source_target_pairs={{0,4},{4,8},{8,12},{12,0},{1,5},{5,9},{9,13},{13,1},{2,6},{6,10},{... | collective-permute-start | bytes 786440 | tf_op jit(solution)/shard_map/ppermute | solution.py:420
  130.3 9.2 %collective-permute-start.23 = (f16[136,768]{1,0:T(8,128)(2,1)S(1)}, f16[136,768]{1,0:T(8,128)(2,1)S(1)}, u32[]{:S(2)}, u32[]{:S(2)}) collective-permute-start(f16[136,768]{1,0:T(8,128)(2,1)S(1)} %pad_maximum_fusion.2), channel_id=1, source_target_pairs={{8,12},{9,13},{10,14},{11,15},{24,28},{25,29},{26,30},{27,31}} | collective-permute-start | bytes 626696 | tf_op jit(solution)/shard_map/ppermute | solution.py:614
  142.1 3.6 %copy-start.5 = (f32[1280]{0:T(1024)S(1)}, f32[1280]{0:T(1024)}, u32[]{:S(2)}) copy-start(f32[1280]{0:T(1024)} %param.23) | copy-start | bytes 15364
  143.4 3.1 %collective-permute-start.26 = (f32[1,1024]{1,0:T(1,128)S(1)}, f32[1,1024]{1,0:T(1,128)S(1)}, u32[]{:S(2)}, u32[]{:S(2)}) collective-permute-start(f32[1,1024]{1,0:T(1,128)S(1)} %get-tuple-element.133.refs_0_), channel_id=1, source_target_pairs={{0,1},{1,2},{2,3},{3,0},{4,5},{5,6},{6,7},{7,4},{8,9},{9,10},{10,1... | collective-permute-start | bytes 12296 | tf_op jit(solution)/shard_map/ppermute | solution.py:420
  143.5 3.7 %collective-permute-start.27 = (f32[1,1024]{1,0:T(1,128)S(1)}, f32[1,1024]{1,0:T(1,128)S(1)}, u32[]{:S(2)}, u32[]{:S(2)}) collective-permute-start(f32[1,1024]{1,0:T(1,128)S(1)} %get-tuple-element.133.refs_0_), channel_id=1, source_target_pairs={{0,2},{1,3},{2,0},{3,1},{4,6},{5,7},{6,4},{7,5},{8,10},{9,11},{10,... | collective-permute-start | bytes 12296 | tf_op jit(solution)/shard_map/ppermute | solution.py:420
  144.4 2.8 %collective-permute-start.28 = (f32[1,1024]{1,0:T(1,128)S(1)}, f32[1,1024]{1,0:T(1,128)S(1)}, u32[]{:S(2)}, u32[]{:S(2)}) collective-permute-start(f32[1,1024]{1,0:T(1,128)S(1)} %get-tuple-element.133.refs_0_), channel_id=1, source_target_pairs={{0,3},{1,0},{2,1},{3,2},{4,7},{5,4},{6,5},{7,6},{8,11},{9,8},{10,9... | collective-permute-start | bytes 12296 | tf_op jit(solution)/shard_map/ppermute | solution.py:420

commit v7 on v6

--- a/solution.py
+++ b/solution.py
@@ -616,22 +616,24 @@
         states.append(unpacked(packet)[0])
 
     outs, totals = [], [jnp.zeros((1, rows), f32)]
-    for tile in range(tiles):
-        part = sum(tile >= last for _, last in parts)
-        gate_part = sum(tile >= last for _, last in gate_parts)
+    bounds = sorted({bound for pair in parts + gate_parts for bound in pair})
+    for first, last in zip(bounds, bounds[1:]):
+        part = sum(first >= end for _, end in parts)
+        gate_part = sum(first >= end for _, end in gate_parts)
         blocks = gates[gate_part]
         if gate_part + 1 < len(gates):
             blocks = [after(blocks[0], gates[gate_part + 1][distances[0]])] + blocks[1:]
         gated, total = call(
             functools.partial(gate_columns, shards),
-            [shape(rows, TILE, dtype=f32), shape(1, rows, dtype=f32)],
+            [shape(rows, (last - first) * TILE, dtype=f32), shape(1, rows, dtype=f32)],
             (totals[-1], pick, query, carried, expand, scans[part], states[part], *blocks),
-            [whole(totals[-1]), whole(pick), whole(query), whole(carried), columns(LANES, start=tile)]
-            + [columns(n, start=tile - parts[part][0]) for n in (rows, state)]
-            + [columns(per, start=tile - gate_parts[gate_part][0])] * shards,
+            [whole(totals[-1]), whole(pick), whole(query), whole(carried), columns(LANES, start=first)]
+            + [columns(n, start=first - parts[part][0]) for n in (rows, state)]
+            + [columns(per, start=first - gate_parts[gate_part][0])] * shards,
             [columns(rows), whole(shape(1, rows))],
+            grid=(last - first,),
             scratch=[pltpu.VMEM((rows, TILE), bf16), pltpu.VMEM((rows, LANES), f32)],
-            micros=3,
+            micros=3 * (last - first),
         )
         outs.append(gated)
         totals.append(total)

time: 151 us -> 152 us (level)
    pallas_call x13 -> x11, Pallas kernels: 48.7 us -> 50 us  [call(): pl.pallas_call(kernel, grid=grid, in_specs=in_specs, out_specs=out_specs,...]
where the time goes in v7:
time: 152 us; the launch traced here: 150 us
  starting transfers between devices  65.8 us (43%)
  Pallas kernels  50 us (33%)
  waiting for transfers between devices  31.5 us (21%)
    ppermute x21, starting transfers between devices, moved(): lax.ppermute(block, axis, [(i, (i + steps) % count) for i in range(count)])  59.6 us
    pallas_call x11, Pallas kernels, call(): pl.pallas_call(kernel, grid=grid, in_specs=in_specs, out_specs=out_specs,...  50 us
    ppermute x21, waiting for transfers between devices, moved(): lax.ppermute(block, axis, [(i, (i + steps) % count) for i in range(count)])  21.2 us
    ppermute x6, waiting for transfers between devices, body(): lax.ppermute(packed_state(leaving, bound), 'seq', [(step - 1, step)])  7.9 us
    ppermute x6, starting transfers between devices, body(): lax.ppermute(packed_state(leaving, bound), 'seq', [(step - 1, step)])  5.49 us
  transfers between devices with their start and end apart: 29, of which 11 were waited for; matrix products, arithmetic and copies ran while one was open for 1% of the time, Pallas kernels for 26%

profile of v7, /device:TPU:26, one launch (start us, length us, event | category | flops | bytes accessed | tf_op | source)
XLA Modules:
  0.0 149.6 jit_solution(10029093472418552389)
XLA Ops:
  0.0 5.1 %shard_map.118 = (bf16[1088,1024]{1,0:T(8,128)(2,1)S(1)}, bf16[272,128]{1,0:T(8,128)(2,1)S(1)}, bf16[272,128]{1,0:T(8,128)(2,1)S(1)}, bf16[272,128]{1,0:T(8,128)...) custom-call(s32[1,1024]{1,0:T(1,128)} %bitcast.24, ...), custom_call_target="tpu_custom_call" | custom-call | flops 8049999872 | tf_op jit(solution)/shard_map/pallas_call | solution.py:64
  5.1 0.3 collective-permute-start
  5.4 1.7 %collective-permute-start.1 = (bf16[272,128]{1,0:T(8,128)(2,1)S(1)}, bf16[272,128]{1,0:T(8,128)(2,1)S(1)}, u32[]{:S(2)}, u32[]{:S(2)}) collective-permute-start(bf16[272,128]{1,0:T(8,128)(2,1)S(1)} %get-tuple-element.70), channel_id=1, source_target_pairs={{0,8},{4,12},{8,0},{12,4},{1,9},{5,13},{9,1},{13,5},{2,10},{6,14},... | collective-permute-start | bytes 208904 | tf_op jit(solution)/shard_map/ppermute | solution.py:420
  7.1 0.4 collective-permute-start.2
  7.5 3.4 %collective-permute-start.5 = (bf16[256,512]{1,0:T(8,128)(2,1)S(1)}, bf16[256,512]{1,0:T(8,128)(2,1)S(1)}, u32[]{:S(2)}, u32[]{:S(2)}) collective-permute-start(bf16[256,512]{1,0:T(8,128)(2,1)S(1)} %get-tuple-element.87), channel_id=1, source_target_pairs={{0,4},{4,8},{8,12},{12,0},{1,5},{5,9},{9,13},{13,1},{2,6},{6,10},{... | collective-permute-start | bytes 786440 | tf_op jit(solution)/shard_map/ppermute | solution.py:420
  10.9 4.5 %shard_map.123 = (bf16[256,768]{1,0:T(8,128)(2,1)S(1)}, bf16[256,768]{1,0:T(8,128)(2,1)S(1)}, bf16[256,768]{1,0:T(8,128)(2,1)S(1)}, bf16[256,768]{1,0:T(8,128)(2...) custom-call(bf16[1088,1024]{1,0:T(8,128)(2,1)S(1)} %get-tuple-elemen, ...), custom_call_target="tpu_custom_call" | custom-call | flops 11500000256 | tf_op jit(solution)/shard_map/pallas_call | solution.py:64
  15.4 1.3 collective-permute-start.7
  16.8 0.6 collective-permute-start.3
  17.4 2.4 %shard_map.122 = (bf16[256,768]{1,0:T(8,128)(2,1)S(1)}, bf16[256,768]{1,0:T(8,128)(2,1)S(1)}, bf16[256,768]{1,0:T(8,128)(2,1)S(1)}, bf16[256,768]{1,0:T(8,128)(2,1)S(1)}) custom-call(bf16[1088,1024]{1,0:T(8,128)(2,1)S(1)} %get-tuple-element.90.pick_ref, bf16[1024,1280]{1,0:T(8,128)(2,1)S(1)} %copy-done.1), custom_call_target="tpu_custom_call" | custom-call | flops 6899999744 | tf_op jit(solution)/shard_map/pallas_call | solution.py:64
  19.8 0.0 copy-start.6
  19.8 0.0 copy-start.7
  19.8 0.0 copy-start.8
  19.9 0.0 copy-start.3
  19.9 0.0 copy-start.4
  19.9 1.3 shard_map.120
  21.2 2.4 %collective-permute-done.3.refs_0_ = bf16[1088,128]{1,0:T(8,128)(2,1)S(1)} collective-permute-done((bf16[1088,128]{1,0:T(8,128)(2,1)S(1)}, bf16[1088,128]{1,0:T(8,128)(2,1)S(1)}, u32[]{:S(2)}, u32[]{:S(2)}) %collective-permute-start.3) | collective-permute-done | bytes 278560 | tf_op jit(solution)/shard_map/ppermute | solution.py:511
  23.6 0.1 collective-permute-start.4
  23.7 6.2 %collective-permute-done.7.refs_3_ = bf16[256,512]{1,0:T(8,128)(2,1)S(1)} collective-permute-done((bf16[256,512]{1,0:T(8,128)(2,1)S(1)}, bf16[256,512]{1,0:T(8,128)(2,1)S(1)}, u32[]{:S(2)}, u32[]{:S(2)}) %collective-permute-start.7) | collective-permute-done | bytes 262176 | tf_op jit(solution)/shard_map/ppermute | solution.py:420
  29.9 5.4 %collective-permute-start.10 = (bf16[4,1280]{1,0:T(4,128)(2,1)S(1)}, bf16[4,1280]{1,0:T(4,128)(2,1)S(1)}, u32[]{:S(2)}, u32[]{:S(2)}) collective-permute-start(bf16[4,1280]{1,0:T(4,128)(2,1)S(1)} %get-tuple-element.93), channel_id=1, source_target_pairs={{0,12},{4,0},{8,4},{12,8},{1,13},{5,1},{9,5},{13,9},{2,14},{6,2},{... | collective-permute-start | bytes 30728 | tf_op jit(solution)/shard_map/ppermute | solution.py:420
  35.3 1.9 %collective-permute-start.9 = (bf16[4,1280]{1,0:T(4,128)(2,1)S(1)}, bf16[4,1280]{1,0:T(4,128)(2,1)S(1)}, u32[]{:S(2)}, u32[]{:S(2)}) collective-permute-start(bf16[4,1280]{1,0:T(4,128)(2,1)S(1)} %get-tuple-element.92), channel_id=1, source_target_pairs={{0,8},{4,12},{8,0},{12,4},{1,9},{5,13},{9,1},{13,5},{2,10},{6,14},... | collective-permute-start | bytes 30728 | tf_op jit(solution)/shard_map/ppermute | solution.py:420
  37.2 2.9 %collective-permute-start.8 = (bf16[4,1280]{1,0:T(4,128)(2,1)S(1)}, bf16[4,1280]{1,0:T(4,128)(2,1)S(1)}, u32[]{:S(2)}, u32[]{:S(2)}) collective-permute-start(bf16[4,1280]{1,0:T(4,128)(2,1)S(1)} %get-tuple-element.91), channel_id=1, source_target_pairs={{0,4},{4,8},{8,12},{12,0},{1,5},{5,9},{9,13},{13,1},{2,6},{6,10},{... | collective-permute-start | bytes 30728 | tf_op jit(solution)/shard_map/ppermute | solution.py:420
  40.2 0.1 fusion.16.lines_ref
  40.2 0.2 collective-permute-start.11
  40.5 0.6 collective-permute-start.18
  41.1 0.5 collective-permute-done.8
  41.6 6.4 %shard_map.119 = (bf16[1024,1024]{1,0:T(8,128)(2,1)S(1)}, bf16[16,16]{1,0:T(8,128)(2,1)S(1)}, s32[1024,128]{1,0:T(8,128)S(1)}, bf16[1024,256]{1,0:T(8,128)(2,1)S...) custom-call(s32[3]{0:T(128)S(1)} %copy-done.4, ...), custom_call_target="tpu_custom_call" | custom-call | flops 9200000000 | tf_op jit(solution)/shard_map/pallas_call | solution.py:64
  48.1 8.2 %shard_map.121 = (f32[1024,512]{1,0:T(8,128)S(1)}, f32[128,512]{1,0:T(8,128)S(1)}, f32[8,512]{1,0:T(8,128)S(1)}) custom-call(s32[3]{0:T(128)S(1)} %copy-done.4, bf16[1024,1024]{1,0:T(8,128)(2,1)S(1)} %get-tuple-element.72.pick_ref, bf16[16,16]{1,0:T(8,128)(2,1)S(1)} %get-tuple-element.76.rims_ref, s32[1024,128]{1,0:T(8,128)S(1)} %get-tuple-element.77.gap_ref, ...), custom_call_target="tpu_custom_call" | custom-call | flops 11500000256 | tf_op jit(solution)/shard_map/pallas_call | solution.py:64
  56.5 0.7 collective-permute-start.12
  57.2 4.9 %collective-permute-start.15 = (bf16[256,768]{1,0:T(8,128)(2,1)S(1)}, bf16[256,768]{1,0:T(8,128)(2,1)S(1)}, u32[]{:S(2)}, u32[]{:S(2)}) collective-permute-start(bf16[256,768]{1,0:T(8,128)(2,1)S(1)} %get-tuple-element.105), channel_id=1, source_target_pairs={{0,4},{4,8},{8,12},{12,0},{1,5},{5,9},{9,13},{13,1},{2,6},{6,10},{... | collective-permute-start | bytes 1179656 | tf_op jit(solution)/shard_map/ppermute | solution.py:420
  62.1 7.2 %collective-permute-done.18.refs_2_ = bf16[256,768]{1,0:T(8,128)(2,1)S(1)} collective-permute-done((bf16[256,768]{1,0:T(8,128)(2,1)S(1)}, bf16[256,768]{1,0:T(8,128)(2,1)S(1)}, u32[]{:S(2)}, u32[]{:S(2)}) %collective-permute-start.18) | collective-permute-done | bytes 393248 | tf_op jit(solution)/shard_map/ppermute | solution.py:420
  69.3 5.2 %collective-permute-start.19 = (bf16[256,768]{1,0:T(8,128)(2,1)S(1)}, bf16[256,768]{1,0:T(8,128)(2,1)S(1)}, u32[]{:S(2)}, u32[]{:S(2)}) collective-permute-start(bf16[256,768]{1,0:T(8,128)(2,1)S(1)} %get-tuple-element.113), channel_id=1, source_target_pairs={{0,12},{4,0},{8,4},{12,8},{1,13},{5,1},{9,5},{13,9},{2,14},{6,2},{... | collective-permute-start | bytes 1179656 | tf_op jit(solution)/shard_map/ppermute | solution.py:420
  74.6 0.1 fusion.15
  74.8 0.9 collective-permute-start.13
  75.6 0.1 collective-permute-done.15.refs_1_
  75.7 14.1 %collective-permute-start.16 = (bf16[256,768]{1,0:T(8,128)(2,1)S(1)}, bf16[256,768]{1,0:T(8,128)(2,1)S(1)}, u32[]{:S(2)}, u32[]{:S(2)}) collective-permute-start(bf16[256,768]{1,0:T(8,128)(2,1)S(1)} %get-tuple-element.106), channel_id=1, source_target_pairs={{0,8},{4,12},{8,0},{12,4},{1,9},{5,13},{9,1},{13,5},{2,10},{6,14},... | collective-permute-start | bytes 1179656 | tf_op jit(solution)/shard_map/ppermute | solution.py:420
  89.8 12.0 %shard_map.125 = (f32[1024,768]{1,0:T(8,128)S(1)}, f32[128,768]{1,0:T(8,128)S(1)}, f32[8,768]{1,0:T(8,128)S(1)}) custom-call(s32[3]{0:T(128)S(1)} %copy-done.4, bf16[1024,1024]{1,0:T(8,128)(2,1)S(1)} %get-tuple-element.72.pick_ref, bf16[16,16]{1,0:T(8,128)(2,1)S(1)} %get-tuple-element.76.rims_ref, s32[1024,128]{1,0:T(8,128)S(1)} %get-tuple-element.77.gap_ref, ...), custom_call_target="tpu_custom_call" | custom-call | flops 17250000896 | tf_op jit(solution)/shard_map/pallas_call | solution.py:64
  102.1 0.1 fusion.11
  102.2 1.3 collective-permute-start.14
  103.5 2.8 %collective-permute-start.20 = (bf16[256,768]{1,0:T(8,128)(2,1)S(1)}, bf16[256,768]{1,0:T(8,128)(2,1)S(1)}, u32[]{:S(2)}, u32[]{:S(2)}) collective-permute-start(bf16[256,768]{1,0:T(8,128)(2,1)S(1)} %get-tuple-element.114), channel_id=1, source_target_pairs={{0,4},{4,8},{8,12},{12,0},{1,5},{5,9},{9,13},{13,1},{2,6},{6,10},{... | collective-permute-start | bytes 1179656 | tf_op jit(solution)/shard_map/ppermute | solution.py:420
  106.4 0.1 pad_maximum_fusion
  106.4 0.7 collective-permute-start.21
  107.1 2.5 %collective-permute-done.14 = f16[136,512]{1,0:T(8,128)(2,1)S(1)} collective-permute-done((f16[136,512]{1,0:T(8,128)(2,1)S(1)}, f16[136,512]{1,0:T(8,128)(2,1)S(1)}, u32[]{:S(2)}, u32[]{:S(2)}) %collective-permute-start.14) | collective-permute-done | bytes 139296 | tf_op jit(solution)/shard_map/ppermute | solution.py:614
  109.7 0.1 collective-permute-start.17
  109.9 0.1 fusion.7
  110.0 0.1 pad_maximum_fusion.1
  110.1 0.7 collective-permute-start.22
  110.8 5.4 %collective-permute-done.20.refs_1_ = bf16[256,768]{1,0:T(8,128)(2,1)S(1)} collective-permute-done((bf16[256,768]{1,0:T(8,128)(2,1)S(1)}, bf16[256,768]{1,0:T(8,128)(2,1)S(1)}, u32[]{:S(2)}, u32[]{:S(2)}) %collective-permute-start.20) | collective-permute-done | bytes 393248 | tf_op jit(solution)/shard_map/ppermute | solution.py:420
  116.1 8.9 %collective-permute-start.25 = (bf16[256,512]{1,0:T(8,128)(2,1)S(1)}, bf16[256,512]{1,0:T(8,128)(2,1)S(1)}, u32[]{:S(2)}, u32[]{:S(2)}) collective-permute-start(bf16[256,512]{1,0:T(8,128)(2,1)S(1)} %get-tuple-element.126), channel_id=1, source_target_pairs={{0,8},{4,12},{8,0},{12,4},{1,9},{5,13},{9,1},{13,5},{2,10},{6,14},... | collective-permute-start | bytes 786440 | tf_op jit(solution)/shard_map/ppermute | solution.py:420
  125.1 0.5 collective-permute-done.17.refs_3_
  125.5 3.2 %collective-permute-start.24 = (bf16[256,512]{1,0:T(8,128)(2,1)S(1)}, bf16[256,512]{1,0:T(8,128)(2,1)S(1)}, u32[]{:S(2)}, u32[]{:S(2)}) collective-permute-start(bf16[256,512]{1,0:T(8,128)(2,1)S(1)} %get-tuple-element.124), channel_id=1, source_target_pairs={{0,4},{4,8},{8,12},{12,0},{1,5},{5,9},{9,13},{13,1},{2,6},{6,10},{... | collective-permute-start | bytes 786440 | tf_op jit(solution)/shard_map/ppermute | solution.py:420
  128.7 0.1 fusion.27
  128.9 0.1 fusion.3
  129.0 0.1 pad_maximum_fusion.2
  129.0 1.3 collective-permute-start.23
  130.4 3.1 %shard_map.124 = (f32[1024,512]{1,0:T(8,128)S(1)}, f32[1,1024]{1,0:T(1,128)S(1)}) custom-call(f32[1,1024]{1,0:T(1,128)S(1)} %broadcast_in_dim.45.sum_ref, bf16[1024,1024]{1,0:T(8,128)(2,1)S(1)} %get-tuple-element.72.pick_ref, bf16[1024,128]{1,0:T(8,128)(2,1)S(1)} %get-tuple-element.73.query_ref, bf16[1024,128]{1,0:T(8,128)(2,1)S(1)} %get-tuple-element.74.carried_ref, ...), custom_call_target="tpu_custom_call" | custom-call | flops 6899999744 | tf_op jit(solution)/shard_map/pallas_call | solution.py:64
  133.5 5.3 %collective-permute-done.23 = f16[136,768]{1,0:T(8,128)(2,1)S(1)} collective-permute-done((f16[136,768]{1,0:T(8,128)(2,1)S(1)}, f16[136,768]{1,0:T(8,128)(2,1)S(1)}, u32[]{:S(2)}, u32[]{:S(2)}) %collective-permute-start.23) | collective-permute-done | bytes 208928 | tf_op jit(solution)/shard_map/ppermute | solution.py:614
  139.0 1.3 shard_map.126
  140.3 3.2 %shard_map.127 = (f32[1024,512]{1,0:T(8,128)S(1)}, f32[1,1024]{1,0:T(1,128)S(1)}) custom-call(f32[1,1024]{1,0:T(1,128)S(1)} %get-tuple-element.121.sum_ref, bf16[1024,1024]{1,0:T(8,128)(2,1)S(1)} %get-tuple-element.72.pick_ref, bf16[1024,128]{1,0:T(8,128)(2,1)S(1)} %get-tuple-element.73.query_ref, bf16[1024,128]{1,0:T(8,128)(2,1)S(1)} %get-tuple-element.74.carried_ref, ...), custom_call_target="tpu_custom_call" | custom-call | flops 6899999744 | tf_op jit(solution)/shard_map/pallas_call | solution.py:64
  143.5 0.1 collective-permute-start.26
  143.5 0.9 collective-permute-start.27
  144.4 1.4 collective-permute-start.28
  145.8 0.7 collective-permute-done.26.refs_1_
  146.5 0.7 collective-permute-done.27.refs_2_
  147.2 2.4 %shard_map.128 = bf16[1024,1280]{1,0:T(8,128)(2,1)} custom-call(f32[1,1024]{1,0:T(1,128)S(1)} %get-tuple-element.127.refs_0_, f32[1,1024]{1,0:T(1,128)S(1)} %collective-permute-done.26.refs_1_, f32[1,1024]{1,0:T(1,128)S(1)} %collective-permute-done.27.refs_2_, f32[1,1024]{1,0:T(1,128)S(1)} %collective-permute-done.28.refs_3_, f32[1,1280]{1,0:T(1,128)S(1)} %reshape.7.refs_4_, ...), custom_call_target="tpu_custom_call" | custom-call | flops 5750000128 | tf_op jit(solution)/shard_map/pallas_call | solution.py:64
  (73 shorter events, 1.1 us)
Async XLA Ops:
  0.0 10.9 %copy-start = (bf16[1024,1280]{1,0:T(8,128)(2,1)S(1)}, bf16[1024,1280]{1,0:T(8,128)(2,1)}, u32[]{:S(2)}) copy-start(bf16[1024,1280]{1,0:T(8,128)(2,1)} %x_ref.7) | copy-start | bytes 7864324
  5.1 10.3 %collective-permute-start = (bf16[272,128]{1,0:T(8,128)(2,1)S(1)}, bf16[272,128]{1,0:T(8,128)(2,1)S(1)}, u32[]{:S(2)}, u32[]{:S(2)}) collective-permute-start(bf16[272,128]{1,0:T(8,128)(2,1)S(1)} %get-tuple-element.69), channel_id=1, source_target_pairs={{0,4},{4,8},{8,12},{12,0},{1,5},{5,9},{9,13},{13,1},{2,6},{6,10},{... | collective-permute-start | bytes 208904 | tf_op jit(solution)/shard_map/ppermute | solution.py:420
  5.4 11.4 %collective-permute-start.1 = (bf16[272,128]{1,0:T(8,128)(2,1)S(1)}, bf16[272,128]{1,0:T(8,128)(2,1)S(1)}, u32[]{:S(2)}, u32[]{:S(2)}) collective-permute-start(bf16[272,128]{1,0:T(8,128)(2,1)S(1)} %get-tuple-element.70), channel_id=1, source_target_pairs={{0,8},{4,12},{8,0},{12,4},{1,9},{5,13},{9,1},{13,5},{2,10},{6,14},... | collective-permute-start | bytes 208904 | tf_op jit(solution)/shard_map/ppermute | solution.py:420
  7.1 9.7 %collective-permute-start.2 = (bf16[272,128]{1,0:T(8,128)(2,1)S(1)}, bf16[272,128]{1,0:T(8,128)(2,1)S(1)}, u32[]{:S(2)}, u32[]{:S(2)}) collective-permute-start(bf16[272,128]{1,0:T(8,128)(2,1)S(1)} %get-tuple-element.71), channel_id=1, source_target_pairs={{0,12},{4,0},{8,4},{12,8},{1,13},{5,1},{9,5},{13,9},{2,14},{6,2},{... | collective-permute-start | bytes 208904 | tf_op jit(solution)/shard_map/ppermute | solution.py:420
  7.5 32.7 %collective-permute-start.5 = (bf16[256,512]{1,0:T(8,128)(2,1)S(1)}, bf16[256,512]{1,0:T(8,128)(2,1)S(1)}, u32[]{:S(2)}, u32[]{:S(2)}) collective-permute-start(bf16[256,512]{1,0:T(8,128)(2,1)S(1)} %get-tuple-element.87), channel_id=1, source_target_pairs={{0,4},{4,8},{8,12},{12,0},{1,5},{5,9},{9,13},{13,1},{2,6},{6,10},{... | collective-permute-start | bytes 786440 | tf_op jit(solution)/shard_map/ppermute | solution.py:420
  10.9 26.3 %collective-permute-start.6 = (bf16[256,512]{1,0:T(8,128)(2,1)S(1)}, bf16[256,512]{1,0:T(8,128)(2,1)S(1)}, u32[]{:S(2)}, u32[]{:S(2)}) collective-permute-start(bf16[256,512]{1,0:T(8,128)(2,1)S(1)} %get-tuple-element.88), channel_id=1, source_target_pairs={{0,8},{4,12},{8,0},{12,4},{1,9},{5,13},{9,1},{13,5},{2,10},{6,14},... | collective-permute-start | bytes 786440 | tf_op jit(solution)/shard_map/ppermute | solution.py:420
  10.9 6.5 %copy-start.1 = (bf16[1024,1280]{1,0:T(8,128)(2,1)S(1)}, bf16[1024,1280]{1,0:T(8,128)(2,1)}, u32[]{:S(2)}) copy-start(bf16[1024,1280]{1,0:T(8,128)(2,1)} %x_ref.6) | copy-start | bytes 7864324
  15.4 14.5 %collective-permute-start.7 = (bf16[256,512]{1,0:T(8,128)(2,1)S(1)}, bf16[256,512]{1,0:T(8,128)(2,1)S(1)}, u32[]{:S(2)}, u32[]{:S(2)}) collective-permute-start(bf16[256,512]{1,0:T(8,128)(2,1)S(1)} %get-tuple-element.89), channel_id=1, source_target_pairs={{0,12},{4,0},{8,4},{12,8},{1,13},{5,1},{9,5},{13,9},{2,14},{6,2},{... | collective-permute-start | bytes 786440 | tf_op jit(solution)/shard_map/ppermute | solution.py:420
  16.8 6.8 %collective-permute-start.3 = (bf16[1088,128]{1,0:T(8,128)(2,1)S(1)}, bf16[1088,128]{1,0:T(8,128)(2,1)S(1)}, u32[]{:S(2)}, u32[]{:S(2)}) collective-permute-start(bf16[1088,128]{1,0:T(8,128)(2,1)S(1)} %get-tuple-element.154.first_ref), channel_id=1, source_target_pairs={{0,2},{1,3},{2,0},{3,1},{4,6},{5,7},{6,4},{7,5},{8,10},{9,11},{10,... | collective-permute-start | bytes 835592 | tf_op jit(solution)/shard_map/ppermute | solution.py:511
  19.8 20.3 %copy-start.6 = (f32[16]{0:T(128)S(1)}, f32[16]{0:T(128)}, u32[]{:S(2)}) copy-start(f32[16]{0:T(128)} %param.22) | copy-start | bytes 196
  19.8 20.3 %copy-start.7 = (f32[16]{0:T(128)S(1)}, f32[16]{0:T(128)}, u32[]{:S(2)}) copy-start(f32[16]{0:T(128)} %param.20) | copy-start | bytes 196
  19.8 20.3 %copy-start.8 = (f32[16]{0:T(128)S(1)}, f32[16]{0:T(128)}, u32[]{:S(2)}) copy-start(f32[16]{0:T(128)} %param.21) | copy-start | bytes 196
  19.9 21.7 %copy-start.3 = (f32[4,256]{1,0:T(4,128)S(1)}, f32[4,256]{1,0:T(4,128)}, u32[]{:S(2)}) copy-start(f32[4,256]{1,0:T(4,128)} %taps_ref.3) | copy-start | bytes 12292
  19.9 21.7 %copy-start.4 = (s32[3]{0:T(128)S(1)}, s32[3]{0:T(128)}, u32[]{:S(2)}) copy-start(s32[3]{0:T(128)} %lengths.5) | copy-start | bytes 40
  23.6 17.9 %collective-permute-start.4 = (bf16[2176,128]{1,0:T(8,128)(2,1)S(1)}, bf16[2176,128]{1,0:T(8,128)(2,1)S(1)}, u32[]{:S(2)}, u32[]{:S(2)}) collective-permute-start(bf16[2176,128]{1,0:T(8,128)(2,1)S(1)} %constant_dynamic-update-slice_fusion.4), channel_id=1, source_target_pairs={{0,1},{1,0},{2,3},{3,2},{4,5},{5,4},{6,7},{7,6},{8,9},{9,8},{10,11... | collective-permute-start | bytes 1671176 | tf_op jit(solution)/shard_map/ppermute | solution.py:511
  29.9 10.6 %collective-permute-start.10 = (bf16[4,1280]{1,0:T(4,128)(2,1)S(1)}, bf16[4,1280]{1,0:T(4,128)(2,1)S(1)}, u32[]{:S(2)}, u32[]{:S(2)}) collective-permute-start(bf16[4,1280]{1,0:T(4,128)(2,1)S(1)} %get-tuple-element.93), channel_id=1, source_target_pairs={{0,12},{4,0},{8,4},{12,8},{1,13},{5,1},{9,5},{13,9},{2,14},{6,2},{... | collective-permute-start | bytes 30728 | tf_op jit(solution)/shard_map/ppermute | solution.py:420
  35.3 5.8 %collective-permute-start.9 = (bf16[4,1280]{1,0:T(4,128)(2,1)S(1)}, bf16[4,1280]{1,0:T(4,128)(2,1)S(1)}, u32[]{:S(2)}, u32[]{:S(2)}) collective-permute-start(bf16[4,1280]{1,0:T(4,128)(2,1)S(1)} %get-tuple-element.92), channel_id=1, source_target_pairs={{0,8},{4,12},{8,0},{12,4},{1,9},{5,13},{9,1},{13,5},{2,10},{6,14},... | collective-permute-start | bytes 30728 | tf_op jit(solution)/shard_map/ppermute | solution.py:420
  37.2 4.3 %collective-permute-start.8 = (bf16[4,1280]{1,0:T(4,128)(2,1)S(1)}, bf16[4,1280]{1,0:T(4,128)(2,1)S(1)}, u32[]{:S(2)}, u32[]{:S(2)}) collective-permute-start(bf16[4,1280]{1,0:T(4,128)(2,1)S(1)} %get-tuple-element.91), channel_id=1, source_target_pairs={{0,4},{4,8},{8,12},{12,0},{1,5},{5,9},{9,13},{13,1},{2,6},{6,10},{... | collective-permute-start | bytes 30728 | tf_op jit(solution)/shard_map/ppermute | solution.py:420
  40.2 16.1 %collective-permute-start.11 = (bf16[256,768]{1,0:T(8,128)(2,1)S(1)}, bf16[256,768]{1,0:T(8,128)(2,1)S(1)}, u32[]{:S(2)}, u32[]{:S(2)}) collective-permute-start(bf16[256,768]{1,0:T(8,128)(2,1)S(1)} %get-tuple-element.99), channel_id=1, source_target_pairs={{0,12},{4,0},{8,4},{12,8},{1,13},{5,1},{9,5},{13,9},{2,14},{6,2},{... | collective-permute-start | bytes 1179656 | tf_op jit(solution)/shard_map/ppermute | solution.py:420
  40.5 28.8 %collective-permute-start.18 = (bf16[256,768]{1,0:T(8,128)(2,1)S(1)}, bf16[256,768]{1,0:T(8,128)(2,1)S(1)}, u32[]{:S(2)}, u32[]{:S(2)}) collective-permute-start(bf16[256,768]{1,0:T(8,128)(2,1)S(1)} %get-tuple-element.112), channel_id=1, source_target_pairs={{0,8},{4,12},{8,0},{12,4},{1,9},{5,13},{9,1},{13,5},{2,10},{6,14},... | collective-permute-start | bytes 1179656 | tf_op jit(solution)/shard_map/ppermute | solution.py:420
  41.6 6.5 %copy-start.2 = (f32[4,1280]{1,0:T(4,128)S(1)}, f32[4,1280]{1,0:T(4,128)}, u32[]{:S(2)}) copy-start(f32[4,1280]{1,0:T(4,128)} %taps_ref.5) | copy-start | bytes 61444
  56.5 18.1 %collective-permute-start.12 = (f16[136,512]{1,0:T(8,128)(2,1)S(1)}, f16[136,512]{1,0:T(8,128)(2,1)S(1)}, u32[]{:S(2)}, u32[]{:S(2)}) collective-permute-start(f16[136,512]{1,0:T(8,128)(2,1)S(1)} %pad_maximum_fusion.3), channel_id=1, source_target_pairs={{0,4},{1,5},{2,6},{3,7},{16,20},{17,21},{18,22},{19,23}} | collective-permute-start | bytes 417800 | tf_op jit(solution)/shard_map/ppermute | solution.py:614
  57.2 18.6 %collective-permute-start.15 = (bf16[256,768]{1,0:T(8,128)(2,1)S(1)}, bf16[256,768]{1,0:T(8,128)(2,1)S(1)}, u32[]{:S(2)}, u32[]{:S(2)}) collective-permute-start(bf16[256,768]{1,0:T(8,128)(2,1)S(1)} %get-tuple-element.105), channel_id=1, source_target_pairs={{0,4},{4,8},{8,12},{12,0},{1,5},{5,9},{9,13},{13,1},{2,6},{6,10},{... | collective-permute-start | bytes 1179656 | tf_op jit(solution)/shard_map/ppermute | solution.py:420
  69.3 34.2 %collective-permute-start.19 = (bf16[256,768]{1,0:T(8,128)(2,1)S(1)}, bf16[256,768]{1,0:T(8,128)(2,1)S(1)}, u32[]{:S(2)}, u32[]{:S(2)}) collective-permute-start(bf16[256,768]{1,0:T(8,128)(2,1)S(1)} %get-tuple-element.113), channel_id=1, source_target_pairs={{0,12},{4,0},{8,4},{12,8},{1,13},{5,1},{9,5},{13,9},{2,14},{6,2},{... | collective-permute-start | bytes 1179656 | tf_op jit(solution)/shard_map/ppermute | solution.py:420
  74.8 27.2 %collective-permute-start.13 = (f16[136,512]{1,0:T(8,128)(2,1)S(1)}, f16[136,512]{1,0:T(8,128)(2,1)S(1)}, u32[]{:S(2)}, u32[]{:S(2)}) collective-permute-start(f16[136,512]{1,0:T(8,128)(2,1)S(1)} %pad_maximum_fusion.4), channel_id=1, source_target_pairs={{4,8},{5,9},{6,10},{7,11},{20,24},{21,25},{22,26},{23,27}} | collective-permute-start | bytes 417800 | tf_op jit(solution)/shard_map/ppermute | solution.py:614
  75.7 34.0 %collective-permute-start.16 = (bf16[256,768]{1,0:T(8,128)(2,1)S(1)}, bf16[256,768]{1,0:T(8,128)(2,1)S(1)}, u32[]{:S(2)}, u32[]{:S(2)}) collective-permute-start(bf16[256,768]{1,0:T(8,128)(2,1)S(1)} %get-tuple-element.106), channel_id=1, source_target_pairs={{0,8},{4,12},{8,0},{12,4},{1,9},{5,13},{9,1},{13,5},{2,10},{6,14},... | collective-permute-start | bytes 1179656 | tf_op jit(solution)/shard_map/ppermute | solution.py:420
  102.2 7.5 %collective-permute-start.14 = (f16[136,512]{1,0:T(8,128)(2,1)S(1)}, f16[136,512]{1,0:T(8,128)(2,1)S(1)}, u32[]{:S(2)}, u32[]{:S(2)}) collective-permute-start(f16[136,512]{1,0:T(8,128)(2,1)S(1)} %pad_maximum_fusion.5), channel_id=1, source_target_pairs={{8,12},{9,13},{10,14},{11,15},{24,28},{25,29},{26,30},{27,31}} | collective-permute-start | bytes 417800 | tf_op jit(solution)/shard_map/ppermute | solution.py:614
  103.5 12.7 %collective-permute-start.20 = (bf16[256,768]{1,0:T(8,128)(2,1)S(1)}, bf16[256,768]{1,0:T(8,128)(2,1)S(1)}, u32[]{:S(2)}, u32[]{:S(2)}) collective-permute-start(bf16[256,768]{1,0:T(8,128)(2,1)S(1)} %get-tuple-element.114), channel_id=1, source_target_pairs={{0,4},{4,8},{8,12},{12,0},{1,5},{5,9},{9,13},{13,1},{2,6},{6,10},{... | collective-permute-start | bytes 1179656 | tf_op jit(solution)/shard_map/ppermute | solution.py:420
  106.4 3.4 %collective-permute-start.21 = (f16[136,768]{1,0:T(8,128)(2,1)S(1)}, f16[136,768]{1,0:T(8,128)(2,1)S(1)}, u32[]{:S(2)}, u32[]{:S(2)}) collective-permute-start(f16[136,768]{1,0:T(8,128)(2,1)S(1)} %pad_maximum_fusion), channel_id=1, source_target_pairs={{0,4},{1,5},{2,6},{3,7},{16,20},{17,21},{18,22},{19,23}} | collective-permute-start | bytes 626696 | tf_op jit(solution)/shard_map/ppermute | solution.py:614
  109.7 15.8 %collective-permute-start.17 = (bf16[256,512]{1,0:T(8,128)(2,1)S(1)}, bf16[256,512]{1,0:T(8,128)(2,1)S(1)}, u32[]{:S(2)}, u32[]{:S(2)}) collective-permute-start(bf16[256,512]{1,0:T(8,128)(2,1)S(1)} %get-tuple-element.107), channel_id=1, source_target_pairs={{0,12},{4,0},{8,4},{12,8},{1,13},{5,1},{9,5},{13,9},{2,14},{6,2},{... | collective-permute-start | bytes 786440 | tf_op jit(solution)/shard_map/ppermute | solution.py:420
  110.1 18.7 %collective-permute-start.22 = (f16[136,768]{1,0:T(8,128)(2,1)S(1)}, f16[136,768]{1,0:T(8,128)(2,1)S(1)}, u32[]{:S(2)}, u32[]{:S(2)}) collective-permute-start(f16[136,768]{1,0:T(8,128)(2,1)S(1)} %pad_maximum_fusion.1), channel_id=1, source_target_pairs={{4,8},{5,9},{6,10},{7,11},{20,24},{21,25},{22,26},{23,27}} | collective-permute-start | bytes 626696 | tf_op jit(solution)/shard_map/ppermute | solution.py:614
  116.1 24.1 %collective-permute-start.25 = (bf16[256,512]{1,0:T(8,128)(2,1)S(1)}, bf16[256,512]{1,0:T(8,128)(2,1)S(1)}, u32[]{:S(2)}, u32[]{:S(2)}) collective-permute-start(bf16[256,512]{1,0:T(8,128)(2,1)S(1)} %get-tuple-element.126), channel_id=1, source_target_pairs={{0,8},{4,12},{8,0},{12,4},{1,9},{5,13},{9,1},{13,5},{2,10},{6,14},... | collective-permute-start | bytes 786440 | tf_op jit(solution)/shard_map/ppermute | solution.py:420
  125.5 14.7 %collective-permute-start.24 = (bf16[256,512]{1,0:T(8,128)(2,1)S(1)}, bf16[256,512]{1,0:T(8,128)(2,1)S(1)}, u32[]{:S(2)}, u32[]{:S(2)}) collective-permute-start(bf16[256,512]{1,0:T(8,128)(2,1)S(1)} %get-tuple-element.124), channel_id=1, source_target_pairs={{0,4},{4,8},{8,12},{12,0},{1,5},{5,9},{9,13},{13,1},{2,6},{6,10},{... | collective-permute-start | bytes 786440 | tf_op jit(solution)/shard_map/ppermute | solution.py:420
  129.0 9.8 %collective-permute-start.23 = (f16[136,768]{1,0:T(8,128)(2,1)S(1)}, f16[136,768]{1,0:T(8,128)(2,1)S(1)}, u32[]{:S(2)}, u32[]{:S(2)}) collective-permute-start(f16[136,768]{1,0:T(8,128)(2,1)S(1)} %pad_maximum_fusion.2), channel_id=1, source_target_pairs={{8,12},{9,13},{10,14},{11,15},{24,28},{25,29},{26,30},{27,31}} | collective-permute-start | bytes 626696 | tf_op jit(solution)/shard_map/ppermute | solution.py:614
  140.3 5.5 %copy-start.5 = (f32[1280]{0:T(1024)S(1)}, f32[1280]{0:T(1024)}, u32[]{:S(2)}) copy-start(f32[1280]{0:T(1024)} %param.23) | copy-start | bytes 15364
  143.5 3.1 %collective-permute-start.26 = (f32[1,1024]{1,0:T(1,128)S(1)}, f32[1,1024]{1,0:T(1,128)S(1)}, u32[]{:S(2)}, u32[]{:S(2)}) collective-permute-start(f32[1,1024]{1,0:T(1,128)S(1)} %get-tuple-element.127.refs_0_), channel_id=1, source_target_pairs={{0,1},{1,2},{2,3},{3,0},{4,5},{5,6},{6,7},{7,4},{8,9},{9,10},{10,1... | collective-permute-start | bytes 12296 | tf_op jit(solution)/shard_map/ppermute | solution.py:420
  143.5 3.7 %collective-permute-start.27 = (f32[1,1024]{1,0:T(1,128)S(1)}, f32[1,1024]{1,0:T(1,128)S(1)}, u32[]{:S(2)}, u32[]{:S(2)}) collective-permute-start(f32[1,1024]{1,0:T(1,128)S(1)} %get-tuple-element.127.refs_0_), channel_id=1, source_target_pairs={{0,2},{1,3},{2,0},{3,1},{4,6},{5,7},{6,4},{7,5},{8,10},{9,11},{10,... | collective-permute-start | bytes 12296 | tf_op jit(solution)/shard_map/ppermute | solution.py:420
  144.4 2.8 %collective-permute-start.28 = (f32[1,1024]{1,0:T(1,128)S(1)}, f32[1,1024]{1,0:T(1,128)S(1)}, u32[]{:S(2)}, u32[]{:S(2)}) collective-permute-start(f32[1,1024]{1,0:T(1,128)S(1)} %get-tuple-element.127.refs_0_), channel_id=1, source_target_pairs={{0,3},{1,0},{2,1},{3,2},{4,7},{5,4},{6,5},{7,6},{8,11},{9,8},{10,9... | collective-permute-start | bytes 12296 | tf_op jit(solution)/shard_map/ppermute | solution.py:420
